TPU v7x, 32 devices: a whole 2x2x4 slice. The times are simulated.
32 devices in a mesh: grp: 2 (over y), tx: 4 (over z), ty: 4 (over x, core).
Axes of the slice: x: 2, y: 2, z: 4, core: 2. Of those that a mesh axis runs over, the one named last changes fastest.
Arguments:
- cell_current: float32 [4096, 512], P(('grp', 'tx'), 'ty'), parts along dimension 0, may hold values from -48 to 48
- block_row: int32 [4096], P(('grp', 'tx')), parts along dimension 0, may hold values from 0 to 255
- block_count: int32 [8], P(('grp', 'tx')), parts along dimension 0, may hold values from 128 to 512, as said below
- cond_x: float32 [4, 512, 512], P(None, ('grp', 'tx'), 'ty'), parts along dimension 1, may hold values from 0.5 to 8
- cond_y: float32 [4, 512, 512], P(None, ('grp', 'tx'), 'ty'), parts along dimension 1, may hold values from 0.5 to 8
- cond_via: float32 [3, 512, 512], P(None, ('grp', 'tx'), 'ty'), parts along dimension 1, may hold values from 0.5 to 8
- ground: float32 [4, 512, 512], P(None, ('grp', 'tx'), 'ty'), parts along dimension 1, may hold values from 0.5 to 4
- drop_weight: float32 [4, 512, 512], P(None, ('grp', 'tx'), 'ty'), parts along dimension 1, may hold values from -48 to 48
Outputs:
- drop: float32 [4, 512, 512], P(None, ('grp', 'tx'), 'ty'), parts along dimension 1
- cell_sense: float32 [4096, 512], P(('grp', 'tx'), 'ty'), parts along dimension 0
There are 2 independent parts, one for each index of `grp`. A program takes and returns all parts, laid end to end along the dimension named above; each array names one. Nothing has to cross between parts.
Inputs may be any that keep to these rules, and one draw needn't show every extreme that they name: `block_count`: every live count is at least a quarter of 512; in every draw some index of tx has all 512 blocks live.
All inputs are finite; a program needn't handle non-finite values.
Results may differ from a plain program's by a relative error of at most 0.00013.
Values sent between devices are 32-bit elements; how exact they have to be, the bound alone decides.
No kernel may reach another device: no remote copies, remote signals or barrier semaphores. Data moves between devices by JAX's collectives and lax.ppermute only.
A program may use at most 64 MiB of HBM per device.

v0:
```python
import jax
import jax.numpy as jnp
from jax import lax
from jax.sharding import PartitionSpec as P

ITERS = 2


HIGH = lax.Precision.HIGHEST


def from_behind(value, axis, steps):
    count = lax.axis_size(axis)
    initial, last = (max(0, -steps), min(count, count - steps))
    return lax.ppermute(value, axis, [(source, source + steps) for source in range(initial, last)])


def with_halo(block, sides, width):
    for axis, dim in sides:
        count = lax.axis_size(axis)
        forward = [(i, i + 1) for i in range(count - 1)]
        backward = [(target, source) for source, target in forward]
        low = lax.ppermute(
            lax.slice_in_dim(block, block.shape[dim] - width, None, axis=dim), axis, forward
        )
        high = lax.ppermute(lax.slice_in_dim(block, 0, width, axis=dim), axis, backward)
        block = jnp.concatenate([low, block, high], axis=dim)
    return block


def body(cell_current, block_row, block_count, cond_x, cond_y, cond_via, ground, drop_weight):
    blocks_here, width = cell_current.shape
    depth, tile_rows, tile_cols = cond_x.shape
    live = lax.iota(jnp.int32, blocks_here) < block_count[0]
    targets = lax.iota(jnp.int32, lax.axis_size("tx") * tile_rows)
    picker = ((targets[:, None] == block_row[None, :]) & live[None, :]).astype(jnp.float32)
    source = lax.psum_scatter(
        jnp.dot(picker, cell_current, precision=HIGH, preferred_element_type=jnp.float32),
        "tx",
        scatter_dimension=0,
        tiled=True,
    )
    rhs = jnp.concatenate(
        [source[None], jnp.zeros((depth - 1, tile_rows, tile_cols), jnp.float32)], 0
    )
    prev_rowcond = from_behind(cond_x[:, -1:, :], "tx", 1)
    prev_colcond = from_behind(cond_y[:, :, -1:], "ty", 1)
    cond_x_low = jnp.concatenate([prev_rowcond, cond_x[:, :-1]], 1)
    cond_y_low = jnp.concatenate([prev_colcond, cond_y[:, :, :-1]], 2)
    layer_zero = jnp.zeros((1, tile_rows, tile_cols), jnp.float32)
    diagonal = (
        ground
        + cond_x
        + cond_x_low
        + cond_y
        + cond_y_low
        + jnp.concatenate([cond_via, layer_zero], 0)
        + jnp.concatenate([layer_zero, cond_via], 0)
    )
    inverse = 1.0 / diagonal

    def apply(field):
        padded = with_halo(field, (("tx", 2), ("ty", 3)), 1)
        inner = padded[:, :, 1:-1, 1:-1]
        flux_x = cond_x * (inner - padded[:, :, 2:, 1:-1])
        flux_x_low = cond_x_low * (padded[:, :, :-2, 1:-1] - inner)
        flux_y = cond_y * (inner - padded[:, :, 1:-1, 2:])
        flux_y_low = cond_y_low * (padded[:, :, 1:-1, :-2] - inner)
        flux_z = cond_via * (inner[:, :-1] - inner[:, 1:])
        slab_zero = jnp.zeros((field.shape[0], 1, tile_rows, tile_cols), jnp.float32)
        vertical = jnp.concatenate([flux_z, slab_zero], 1) - jnp.concatenate([slab_zero, flux_z], 1)
        return ground * inner + (flux_x - flux_x_low) + (flux_y - flux_y_low) + vertical

    def inner_sum(left, right):
        return lax.psum(jnp.sum(left * right, axis=(1, 2, 3)), ("tx", "ty"))

    def precondition(resid):
        guess = inverse * resid
        guess = guess + inverse * (resid - apply(guess))
        return guess

    def expand(values):
        return values[:, None, None, None]

    def solve(rhs_stack):
        solution = jnp.zeros_like(rhs_stack)
        resid = rhs_stack
        zvec = precondition(resid)
        direction = zvec
        rz_now = inner_sum(resid, zvec)
        for step in range(ITERS):
            image = apply(direction)
            alpha = rz_now / inner_sum(direction, image)
            solution = solution + expand(alpha) * direction
            resid = resid - expand(alpha) * image
            if step + 1 < ITERS:
                zvec = precondition(resid)
                rz_next = inner_sum(resid, zvec)
                direction = zvec + expand(rz_next / rz_now) * direction
                rz_now = rz_next
        return solution

    drop = solve(rhs[None])[0]
    adjoint = solve(drop_weight[None])[0]
    piece = lax.all_gather(adjoint[0], "tx", axis=0, tiled=True)
    count = piece.shape[0]
    picker = ((block_row[:, None] == lax.iota(jnp.int32, count)[None, :]) & live[:, None]).astype(
        jnp.float32
    )
    cell_sense = jnp.dot(picker, piece, precision=HIGH, preferred_element_type=jnp.float32)
    return (drop, cell_sense)


def solution(mesh):
    placed = (
        P(("grp", "tx"), "ty"),
        P(("grp", "tx")),
        P(("grp", "tx")),
        P(None, ("grp", "tx"), "ty"),
        P(None, ("grp", "tx"), "ty"),
        P(None, ("grp", "tx"), "ty"),
        P(None, ("grp", "tx"), "ty"),
        P(None, ("grp", "tx"), "ty"),
    )
    return jax.shard_map(
        body,
        mesh=mesh,
        in_specs=placed,
        out_specs=(P(None, ("grp", "tx"), "ty"), P(("grp", "tx"), "ty")),
        check_vma=False,
    )
```

profile of v0, /device:TPU:0, one launch (start us, length us, event | category | flops | bytes accessed | tf_op | source)
XLA Modules:
  0.0 257.8 jit_solution(14410577668966842581)
XLA Ops:
  8.0 5.0 %collective-permute-start = (f32[4,1,128]{2,1,0:T(1,128)S(1)}, f32[4,1,128]{2,1,0:T(1,128)S(1)}, u32[]{:S(2)}, u32[]{:S(2)}) collective-permute-start(f32[4,1,128]{2,1,0:T(1,128)S(1)} %slice.288), channel_id=1, source_target_pairs={{0,4},{4,8},{8,12},{1,5},{5,9},{9,13},{2,6},{6,10},{10,14},{3,7},{... | collective-permute-start | bytes 6152 | tf_op jit(solution)/shard_map/ppermute | solution.py:15
  14.0 1.5 collective-permute-start.1
  17.7 1.3 collective-permute-start.18
  19.0 4.5 %collective-permute-start.19 = (f32[1,4,1,128]{3,2,1,0:T(1,128)S(1)}, f32[1,4,1,128]{3,2,1,0:T(1,128)S(1)}, u32[]{:S(2)}, u32[]{:S(2)}) collective-permute-start(f32[1,4,1,128]{3,2,1,0:T(1,128)S(1)} %get-tuple-element.52), channel_id=1, source_target_pairs={{0,4},{4,8},{8,12},{1,5},{5,9},{9,13},{2,6},{6,10},{10,14},{3,7},{... | collective-permute-start | bytes 6152 | tf_op jit(solution)/shard_map/ppermute | solution.py:23
  25.0 1.3 collective-permute-start.20
  26.3 4.8 %collective-permute-start.21 = (f32[1,4,66,1]{3,2,1,0:T(8,128)S(1)}, f32[1,4,66,1]{3,2,1,0:T(8,128)S(1)}, u32[]{:S(2)}, u32[]{:S(2)}) collective-permute-start(f32[1,4,66,1]{3,2,1,0:T(8,128)S(1)} %get-tuple-element.36), channel_id=1, source_target_pairs={{0,1},{1,2},{2,3},{4,5},{5,6},{6,7},{8,9},{9,10},{10,11},{12,13},{... | collective-permute-start | bytes 3176 | tf_op jit(solution)/shard_map/ppermute | solution.py:23
  31.1 17.0 %reduce-scatter.2.cloned.1.call-done = f32[64,128]{1,0:T(8,128)} async-done(((f32[256,128]{1,0:T(8,128)}), f32[64,128]{1,0:T(8,128)}) %reduce-scatter.2.cloned.1.call-update) | async-done | bytes 32784 | tf_op jit(solution)/shard_map/reduce_scatter | solution.py:37
  49.1 1.4 collective-permute-start.2
  50.5 4.5 %collective-permute-start.3 = (f32[1,4,1,128]{3,2,1,0:T(1,128)S(1)}, f32[1,4,1,128]{3,2,1,0:T(1,128)S(1)}, u32[]{:S(2)}, u32[]{:S(2)}) collective-permute-start(f32[1,4,1,128]{3,2,1,0:T(1,128)S(1)} %get-tuple-element.56), channel_id=1, source_target_pairs={{0,4},{4,8},{8,12},{1,5},{5,9},{9,13},{2,6},{6,10},{10,14},{3,7},{... | collective-permute-start | bytes 6152 | tf_op jit(solution)/shard_map/ppermute | solution.py:23
  55.3 1.3 collective-permute-start.22
  56.6 4.5 %collective-permute-start.23 = (f32[1,4,1,128]{3,2,1,0:T(1,128)S(1)}, f32[1,4,1,128]{3,2,1,0:T(1,128)S(1)}, u32[]{:S(2)}, u32[]{:S(2)}) collective-permute-start(f32[1,4,1,128]{3,2,1,0:T(1,128)S(1)} %get-tuple-element.50), channel_id=1, source_target_pairs={{0,4},{4,8},{8,12},{1,5},{5,9},{9,13},{2,6},{6,10},{10,14},{3,7},{... | collective-permute-start | bytes 6152 | tf_op jit(solution)/shard_map/ppermute | solution.py:23
  61.3 1.3 collective-permute-start.4
  62.6 3.0 %collective-permute-start.5 = (f32[1,4,66,1]{3,2,1,0:T(8,128)S(1)}, f32[1,4,66,1]{3,2,1,0:T(8,128)S(1)}, u32[]{:S(2)}, u32[]{:S(2)}) collective-permute-start(f32[1,4,66,1]{3,2,1,0:T(8,128)S(1)} %get-tuple-element.40), channel_id=1, source_target_pairs={{0,1},{1,2},{2,3},{4,5},{5,6},{6,7},{8,9},{9,10},{10,11},{12,13},{... | collective-permute-start | bytes 3176 | tf_op jit(solution)/shard_map/ppermute | solution.py:23
  67.1 3.6 %collective-permute-start.25 = (f32[1,4,66,1]{3,2,1,0:T(8,128)S(1)}, f32[1,4,66,1]{3,2,1,0:T(8,128)S(1)}, u32[]{:S(2)}, u32[]{:S(2)}) collective-permute-start(f32[1,4,66,1]{3,2,1,0:T(8,128)S(1)} %get-tuple-element.34), channel_id=1, source_target_pairs={{0,1},{1,2},{2,3},{4,5},{5,6},{6,7},{8,9},{9,10},{10,11},{12,13},{... | collective-permute-start | bytes 3176 | tf_op jit(solution)/shard_map/ppermute | solution.py:23
  71.0 1.3 collective-permute-start.6
  72.3 4.5 %collective-permute-start.7 = (f32[1,4,1,128]{3,2,1,0:T(1,128)S(1)}, f32[1,4,1,128]{3,2,1,0:T(1,128)S(1)}, u32[]{:S(2)}, u32[]{:S(2)}) collective-permute-start(f32[1,4,1,128]{3,2,1,0:T(1,128)S(1)} %get-tuple-element.54), channel_id=1, source_target_pairs={{0,4},{4,8},{8,12},{1,5},{5,9},{9,13},{2,6},{6,10},{10,14},{3,7},{... | collective-permute-start | bytes 6152 | tf_op jit(solution)/shard_map/ppermute | solution.py:23
  79.5 3.1 %collective-permute-start.9 = (f32[1,4,66,1]{3,2,1,0:T(8,128)S(1)}, f32[1,4,66,1]{3,2,1,0:T(8,128)S(1)}, u32[]{:S(2)}, u32[]{:S(2)}) collective-permute-start(f32[1,4,66,1]{3,2,1,0:T(8,128)S(1)} %get-tuple-element.38), channel_id=1, source_target_pairs={{0,1},{1,2},{2,3},{4,5},{5,6},{6,7},{8,9},{9,10},{10,11},{12,13},{... | collective-permute-start | bytes 3176 | tf_op jit(solution)/shard_map/ppermute | solution.py:23
  84.5 33.4 %all-reduce.21 = (f32[1]{0:T(128)}, f32[1]{0:T(128)}, f32[1]{0:T(128)}, f32[1]{0:T(128)}) all-reduce(f32[1]{0:T(128)} %bitcast.11, f32[1]{0:T(128)} %bitcast.13, f32[1]{0:T(128)} %bitcast.23, f32[1]{0:T(128)} %bitcast.24), channel_id=1, replica_groups=mesh['grp'=2,'tx'=4,'ty'=4] {'tx','ty'}, use_global_device_ids=true, to_apply=%region_2.0 | all-reduce | flops 4 | bytes 32 | tf_op jit(solution)/shard_map/psum | solution.py:75
  121.8 4.5 %collective-permute-start.11 = (f32[1,4,1,128]{3,2,1,0:T(1,128)S(1)}, f32[1,4,1,128]{3,2,1,0:T(1,128)S(1)}, u32[]{:S(2)}, u32[]{:S(2)}) collective-permute-start(f32[1,4,1,128]{3,2,1,0:T(1,128)S(1)} %get-tuple-element.48), channel_id=1, source_target_pairs={{0,4},{4,8},{8,12},{1,5},{5,9},{9,13},{2,6},{6,10},{10,14},{3,7},{... | collective-permute-start | bytes 6152 | tf_op jit(solution)/shard_map/ppermute | solution.py:23
  127.7 4.5 %collective-permute-start.27 = (f32[1,4,1,128]{3,2,1,0:T(1,128)S(1)}, f32[1,4,1,128]{3,2,1,0:T(1,128)S(1)}, u32[]{:S(2)}, u32[]{:S(2)}) collective-permute-start(f32[1,4,1,128]{3,2,1,0:T(1,128)S(1)} %get-tuple-element.45), channel_id=1, source_target_pairs={{0,4},{4,8},{8,12},{1,5},{5,9},{9,13},{2,6},{6,10},{10,14},{3,7},{... | collective-permute-start | bytes 6152 | tf_op jit(solution)/shard_map/ppermute | solution.py:23
  133.7 3.0 %collective-permute-start.13 = (f32[1,4,66,1]{3,2,1,0:T(8,128)S(1)}, f32[1,4,66,1]{3,2,1,0:T(8,128)S(1)}, u32[]{:S(2)}, u32[]{:S(2)}) collective-permute-start(f32[1,4,66,1]{3,2,1,0:T(8,128)S(1)} %get-tuple-element.32), channel_id=1, source_target_pairs={{0,1},{1,2},{2,3},{4,5},{5,6},{6,7},{8,9},{9,10},{10,11},{12,13},{... | collective-permute-start | bytes 3176 | tf_op jit(solution)/shard_map/ppermute | solution.py:23
  138.2 3.0 %collective-permute-start.29 = (f32[1,4,66,1]{3,2,1,0:T(8,128)S(1)}, f32[1,4,66,1]{3,2,1,0:T(8,128)S(1)}, u32[]{:S(2)}, u32[]{:S(2)}) collective-permute-start(f32[1,4,66,1]{3,2,1,0:T(8,128)S(1)} %get-tuple-element.30), channel_id=1, source_target_pairs={{0,1},{1,2},{2,3},{4,5},{5,6},{6,7},{8,9},{9,10},{10,11},{12,13},{... | collective-permute-start | bytes 3176 | tf_op jit(solution)/shard_map/ppermute | solution.py:23
  143.0 32.5 %all-reduce.20 = (f32[1]{0:T(128)}, f32[1]{0:T(128)}) all-reduce(f32[1]{0:T(128)} %bitcast.15, f32[1]{0:T(128)} %bitcast.26), channel_id=1, replica_groups=mesh['grp'=2,'tx'=4,'ty'=4] {'tx','ty'}, use_global_device_ids=true, to_apply=%region_6.0 | all-reduce | flops 2 | bytes 16 | tf_op jit(solution)/shard_map/psum | solution.py:75
  178.1 1.3 collective-permute-start.30
  179.4 4.5 %collective-permute-start.31 = (f32[1,4,1,128]{3,2,1,0:T(1,128)S(1)}, f32[1,4,1,128]{3,2,1,0:T(1,128)S(1)}, u32[]{:S(2)}, u32[]{:S(2)}) collective-permute-start(f32[1,4,1,128]{3,2,1,0:T(1,128)S(1)} %get-tuple-element.41), channel_id=1, source_target_pairs={{0,4},{4,8},{8,12},{1,5},{5,9},{9,13},{2,6},{6,10},{10,14},{3,7},{... | collective-permute-start | bytes 6152 | tf_op jit(solution)/shard_map/ppermute | solution.py:23
  184.0 1.3 collective-permute-start.14
  185.3 4.5 %collective-permute-start.15 = (f32[1,4,1,128]{3,2,1,0:T(1,128)S(1)}, f32[1,4,1,128]{3,2,1,0:T(1,128)S(1)}, u32[]{:S(2)}, u32[]{:S(2)}) collective-permute-start(f32[1,4,1,128]{3,2,1,0:T(1,128)S(1)} %get-tuple-element.43), channel_id=1, source_target_pairs={{0,4},{4,8},{8,12},{1,5},{5,9},{9,13},{2,6},{6,10},{10,14},{3,7},{... | collective-permute-start | bytes 6152 | tf_op jit(solution)/shard_map/ppermute | solution.py:23
  191.3 3.0 %collective-permute-start.33 = (f32[1,4,66,1]{3,2,1,0:T(8,128)S(1)}, f32[1,4,66,1]{3,2,1,0:T(8,128)S(1)}, u32[]{:S(2)}, u32[]{:S(2)}) collective-permute-start(f32[1,4,66,1]{3,2,1,0:T(8,128)S(1)} %get-tuple-element.26), channel_id=1, source_target_pairs={{0,1},{1,2},{2,3},{4,5},{5,6},{6,7},{8,9},{9,10},{10,11},{12,13},{... | collective-permute-start | bytes 3176 | tf_op jit(solution)/shard_map/ppermute | solution.py:23
  194.5 1.3 collective-permute-start.16
  195.8 3.0 %collective-permute-start.17 = (f32[1,4,66,1]{3,2,1,0:T(8,128)S(1)}, f32[1,4,66,1]{3,2,1,0:T(8,128)S(1)}, u32[]{:S(2)}, u32[]{:S(2)}) collective-permute-start(f32[1,4,66,1]{3,2,1,0:T(8,128)S(1)} %get-tuple-element.28), channel_id=1, source_target_pairs={{0,1},{1,2},{2,3},{4,5},{5,6},{6,7},{8,9},{9,10},{10,11},{12,13},{... | collective-permute-start | bytes 3176 | tf_op jit(solution)/shard_map/ppermute | solution.py:23
  200.6 32.4 %all-reduce.19 = (f32[1]{0:T(128)}, f32[1]{0:T(128)}) all-reduce(f32[1]{0:T(128)} %bitcast.17, f32[1]{0:T(128)} %bitcast.28), channel_id=1, replica_groups=mesh['grp'=2,'tx'=4,'ty'=4] {'tx','ty'}, use_global_device_ids=true, to_apply=%region_8.0 | all-reduce | flops 2 | bytes 16 | tf_op jit(solution)/shard_map/psum | solution.py:75
  234.4 13.4 %all-gather = f32[1,1,256,128]{3,2,1,0:T(8,128)S(1)} all-gather(f32[1,1,64,128]{3,2,1,0:T(8,128)S(1)} %fusion.144), channel_id=2, replica_groups=mesh['grp'=2,'tx'=4,'ty'=4] {'tx'}, dimensions={2}, use_global_device_ids=true | all-gather | bytes 163840 | tf_op jit(solution)/shard_map/all_gather | solution.py:105
  (106 shorter events, 24.5 us)
Async XLA Ops:
  7.2 40.9 %reduce-scatter.2.cloned.1.call-start = ((), (), s32[]{:S(2)}) async-start(), calls=%async_computation.1 | async-start | bytes 163840 | tf_op jit(solution)/shard_map/reduce_scatter | solution.py:37
  8.0 8.5 %collective-permute-start = (f32[4,1,128]{2,1,0:T(1,128)S(1)}, f32[4,1,128]{2,1,0:T(1,128)S(1)}, u32[]{:S(2)}, u32[]{:S(2)}) collective-permute-start(f32[4,1,128]{2,1,0:T(1,128)S(1)} %slice.288), channel_id=1, source_target_pairs={{0,4},{4,8},{8,12},{1,5},{5,9},{9,13},{2,6},{6,10},{10,14},{3,7},{... | collective-permute-start | bytes 6152 | tf_op jit(solution)/shard_map/ppermute | solution.py:15
  17.7 7.0 %collective-permute-start.18 = (f32[1,4,1,128]{3,2,1,0:T(1,128)S(1)}, f32[1,4,1,128]{3,2,1,0:T(1,128)S(1)}, u32[]{:S(2)}, u32[]{:S(2)}) collective-permute-start(f32[1,4,1,128]{3,2,1,0:T(1,128)S(1)} %get-tuple-element.53), channel_id=1, source_target_pairs={{4,0},{8,4},{12,8},{5,1},{9,5},{13,9},{6,2},{10,6},{14,10},{7,3},{... | collective-permute-start | bytes 6152 | tf_op jit(solution)/shard_map/ppermute | solution.py:26
  19.0 5.8 %collective-permute-start.19 = (f32[1,4,1,128]{3,2,1,0:T(1,128)S(1)}, f32[1,4,1,128]{3,2,1,0:T(1,128)S(1)}, u32[]{:S(2)}, u32[]{:S(2)}) collective-permute-start(f32[1,4,1,128]{3,2,1,0:T(1,128)S(1)} %get-tuple-element.52), channel_id=1, source_target_pairs={{0,4},{4,8},{8,12},{1,5},{5,9},{9,13},{2,6},{6,10},{10,14},{3,7},{... | collective-permute-start | bytes 6152 | tf_op jit(solution)/shard_map/ppermute | solution.py:23
  25.0 30.1 %collective-permute-start.20 = (f32[1,4,66,1]{3,2,1,0:T(8,128)S(1)}, f32[1,4,66,1]{3,2,1,0:T(8,128)S(1)}, u32[]{:S(2)}, u32[]{:S(2)}) collective-permute-start(f32[1,4,66,1]{3,2,1,0:T(8,128)S(1)} %get-tuple-element.35), channel_id=1, source_target_pairs={{1,0},{2,1},{3,2},{5,4},{6,5},{7,6},{9,8},{10,9},{11,10},{13,12},{... | collective-permute-start | bytes 3176 | tf_op jit(solution)/shard_map/ppermute | solution.py:26
  26.3 28.8 %collective-permute-start.21 = (f32[1,4,66,1]{3,2,1,0:T(8,128)S(1)}, f32[1,4,66,1]{3,2,1,0:T(8,128)S(1)}, u32[]{:S(2)}, u32[]{:S(2)}) collective-permute-start(f32[1,4,66,1]{3,2,1,0:T(8,128)S(1)} %get-tuple-element.36), channel_id=1, source_target_pairs={{0,1},{1,2},{2,3},{4,5},{5,6},{6,7},{8,9},{9,10},{10,11},{12,13},{... | collective-permute-start | bytes 3176 | tf_op jit(solution)/shard_map/ppermute | solution.py:23
  49.1 12.1 %collective-permute-start.2 = (f32[1,4,1,128]{3,2,1,0:T(1,128)S(1)}, f32[1,4,1,128]{3,2,1,0:T(1,128)S(1)}, u32[]{:S(2)}, u32[]{:S(2)}) collective-permute-start(f32[1,4,1,128]{3,2,1,0:T(1,128)S(1)} %get-tuple-element.57), channel_id=1, source_target_pairs={{4,0},{8,4},{12,8},{5,1},{9,5},{13,9},{6,2},{10,6},{14,10},{7,3},{... | collective-permute-start | bytes 6152 | tf_op jit(solution)/shard_map/ppermute | solution.py:26
  50.5 10.7 %collective-permute-start.3 = (f32[1,4,1,128]{3,2,1,0:T(1,128)S(1)}, f32[1,4,1,128]{3,2,1,0:T(1,128)S(1)}, u32[]{:S(2)}, u32[]{:S(2)}) collective-permute-start(f32[1,4,1,128]{3,2,1,0:T(1,128)S(1)} %get-tuple-element.56), channel_id=1, source_target_pairs={{0,4},{4,8},{8,12},{1,5},{5,9},{9,13},{2,6},{6,10},{10,14},{3,7},{... | collective-permute-start | bytes 6152 | tf_op jit(solution)/shard_map/ppermute | solution.py:23
  55.3 10.4 %collective-permute-start.22 = (f32[1,4,1,128]{3,2,1,0:T(1,128)S(1)}, f32[1,4,1,128]{3,2,1,0:T(1,128)S(1)}, u32[]{:S(2)}, u32[]{:S(2)}) collective-permute-start(f32[1,4,1,128]{3,2,1,0:T(1,128)S(1)} %get-tuple-element.51), channel_id=1, source_target_pairs={{4,0},{8,4},{12,8},{5,1},{9,5},{13,9},{6,2},{10,6},{14,10},{7,3},{... | collective-permute-start | bytes 6152 | tf_op jit(solution)/shard_map/ppermute | solution.py:26
  56.6 9.1 %collective-permute-start.23 = (f32[1,4,1,128]{3,2,1,0:T(1,128)S(1)}, f32[1,4,1,128]{3,2,1,0:T(1,128)S(1)}, u32[]{:S(2)}, u32[]{:S(2)}) collective-permute-start(f32[1,4,1,128]{3,2,1,0:T(1,128)S(1)} %get-tuple-element.50), channel_id=1, source_target_pairs={{0,4},{4,8},{8,12},{1,5},{5,9},{9,13},{2,6},{6,10},{10,14},{3,7},{... | collective-permute-start | bytes 6152 | tf_op jit(solution)/shard_map/ppermute | solution.py:23
  61.3 9.4 %collective-permute-start.4 = (f32[1,4,66,1]{3,2,1,0:T(8,128)S(1)}, f32[1,4,66,1]{3,2,1,0:T(8,128)S(1)}, u32[]{:S(2)}, u32[]{:S(2)}) collective-permute-start(f32[1,4,66,1]{3,2,1,0:T(8,128)S(1)} %get-tuple-element.39), channel_id=1, source_target_pairs={{1,0},{2,1},{3,2},{5,4},{6,5},{7,6},{9,8},{10,9},{11,10},{13,12},{... | collective-permute-start | bytes 3176 | tf_op jit(solution)/shard_map/ppermute | solution.py:26
  62.6 8.1 %collective-permute-start.5 = (f32[1,4,66,1]{3,2,1,0:T(8,128)S(1)}, f32[1,4,66,1]{3,2,1,0:T(8,128)S(1)}, u32[]{:S(2)}, u32[]{:S(2)}) collective-permute-start(f32[1,4,66,1]{3,2,1,0:T(8,128)S(1)} %get-tuple-element.40), channel_id=1, source_target_pairs={{0,1},{1,2},{2,3},{4,5},{5,6},{6,7},{8,9},{9,10},{10,11},{12,13},{... | collective-permute-start | bytes 3176 | tf_op jit(solution)/shard_map/ppermute | solution.py:23
  65.8 16.9 %collective-permute-start.24 = (f32[1,4,66,1]{3,2,1,0:T(8,128)S(1)}, f32[1,4,66,1]{3,2,1,0:T(8,128)S(1)}, u32[]{:S(2)}, u32[]{:S(2)}) collective-permute-start(f32[1,4,66,1]{3,2,1,0:T(8,128)S(1)} %get-tuple-element.33), channel_id=1, source_target_pairs={{1,0},{2,1},{3,2},{5,4},{6,5},{7,6},{9,8},{10,9},{11,10},{13,12},{... | collective-permute-start | bytes 3176 | tf_op jit(solution)/shard_map/ppermute | solution.py:26
  67.1 15.6 %collective-permute-start.25 = (f32[1,4,66,1]{3,2,1,0:T(8,128)S(1)}, f32[1,4,66,1]{3,2,1,0:T(8,128)S(1)}, u32[]{:S(2)}, u32[]{:S(2)}) collective-permute-start(f32[1,4,66,1]{3,2,1,0:T(8,128)S(1)} %get-tuple-element.34), channel_id=1, source_target_pairs={{0,1},{1,2},{2,3},{4,5},{5,6},{6,7},{8,9},{9,10},{10,11},{12,13},{... | collective-permute-start | bytes 3176 | tf_op jit(solution)/shard_map/ppermute | solution.py:23
  71.0 5.9 %collective-permute-start.6 = (f32[1,4,1,128]{3,2,1,0:T(1,128)S(1)}, f32[1,4,1,128]{3,2,1,0:T(1,128)S(1)}, u32[]{:S(2)}, u32[]{:S(2)}) collective-permute-start(f32[1,4,1,128]{3,2,1,0:T(1,128)S(1)} %get-tuple-element.55), channel_id=1, source_target_pairs={{4,0},{8,4},{12,8},{5,1},{9,5},{13,9},{6,2},{10,6},{14,10},{7,3},{... | collective-permute-start | bytes 6152 | tf_op jit(solution)/shard_map/ppermute | solution.py:26
  72.3 5.8 %collective-permute-start.7 = (f32[1,4,1,128]{3,2,1,0:T(1,128)S(1)}, f32[1,4,1,128]{3,2,1,0:T(1,128)S(1)}, u32[]{:S(2)}, u32[]{:S(2)}) collective-permute-start(f32[1,4,1,128]{3,2,1,0:T(1,128)S(1)} %get-tuple-element.54), channel_id=1, source_target_pairs={{0,4},{4,8},{8,12},{1,5},{5,9},{9,13},{2,6},{6,10},{10,14},{3,7},{... | collective-permute-start | bytes 6152 | tf_op jit(solution)/shard_map/ppermute | solution.py:23
  78.2 5.3 %collective-permute-start.8 = (f32[1,4,66,1]{3,2,1,0:T(8,128)S(1)}, f32[1,4,66,1]{3,2,1,0:T(8,128)S(1)}, u32[]{:S(2)}, u32[]{:S(2)}) collective-permute-start(f32[1,4,66,1]{3,2,1,0:T(8,128)S(1)} %get-tuple-element.37), channel_id=1, source_target_pairs={{1,0},{2,1},{3,2},{5,4},{6,5},{7,6},{9,8},{10,9},{11,10},{13,12},{... | collective-permute-start | bytes 3176 | tf_op jit(solution)/shard_map/ppermute | solution.py:26
  79.5 4.1 %collective-permute-start.9 = (f32[1,4,66,1]{3,2,1,0:T(8,128)S(1)}, f32[1,4,66,1]{3,2,1,0:T(8,128)S(1)}, u32[]{:S(2)}, u32[]{:S(2)}) collective-permute-start(f32[1,4,66,1]{3,2,1,0:T(8,128)S(1)} %get-tuple-element.38), channel_id=1, source_target_pairs={{0,1},{1,2},{2,3},{4,5},{5,6},{6,7},{8,9},{9,10},{10,11},{12,13},{... | collective-permute-start | bytes 3176 | tf_op jit(solution)/shard_map/ppermute | solution.py:23
  120.5 11.7 %collective-permute-start.10 = (f32[1,4,1,128]{3,2,1,0:T(1,128)S(1)}, f32[1,4,1,128]{3,2,1,0:T(1,128)S(1)}, u32[]{:S(2)}, u32[]{:S(2)}) collective-permute-start(f32[1,4,1,128]{3,2,1,0:T(1,128)S(1)} %get-tuple-element.49), channel_id=1, source_target_pairs={{4,0},{8,4},{12,8},{5,1},{9,5},{13,9},{6,2},{10,6},{14,10},{7,3},{... | collective-permute-start | bytes 6152 | tf_op jit(solution)/shard_map/ppermute | solution.py:26
  121.8 10.4 %collective-permute-start.11 = (f32[1,4,1,128]{3,2,1,0:T(1,128)S(1)}, f32[1,4,1,128]{3,2,1,0:T(1,128)S(1)}, u32[]{:S(2)}, u32[]{:S(2)}) collective-permute-start(f32[1,4,1,128]{3,2,1,0:T(1,128)S(1)} %get-tuple-element.48), channel_id=1, source_target_pairs={{0,4},{4,8},{8,12},{1,5},{5,9},{9,13},{2,6},{6,10},{10,14},{3,7},{... | collective-permute-start | bytes 6152 | tf_op jit(solution)/shard_map/ppermute | solution.py:23
  126.4 10.4 %collective-permute-start.26 = (f32[1,4,1,128]{3,2,1,0:T(1,128)S(1)}, f32[1,4,1,128]{3,2,1,0:T(1,128)S(1)}, u32[]{:S(2)}, u32[]{:S(2)}) collective-permute-start(f32[1,4,1,128]{3,2,1,0:T(1,128)S(1)} %get-tuple-element.46), channel_id=1, source_target_pairs={{4,0},{8,4},{12,8},{5,1},{9,5},{13,9},{6,2},{10,6},{14,10},{7,3},{... | collective-permute-start | bytes 6152 | tf_op jit(solution)/shard_map/ppermute | solution.py:26
  127.7 9.1 %collective-permute-start.27 = (f32[1,4,1,128]{3,2,1,0:T(1,128)S(1)}, f32[1,4,1,128]{3,2,1,0:T(1,128)S(1)}, u32[]{:S(2)}, u32[]{:S(2)}) collective-permute-start(f32[1,4,1,128]{3,2,1,0:T(1,128)S(1)} %get-tuple-element.45), channel_id=1, source_target_pairs={{0,4},{4,8},{8,12},{1,5},{5,9},{9,13},{2,6},{6,10},{10,14},{3,7},{... | collective-permute-start | bytes 6152 | tf_op jit(solution)/shard_map/ppermute | solution.py:23
  132.4 8.8 %collective-permute-start.12 = (f32[1,4,66,1]{3,2,1,0:T(8,128)S(1)}, f32[1,4,66,1]{3,2,1,0:T(8,128)S(1)}, u32[]{:S(2)}, u32[]{:S(2)}) collective-permute-start(f32[1,4,66,1]{3,2,1,0:T(8,128)S(1)} %get-tuple-element.31), channel_id=1, source_target_pairs={{1,0},{2,1},{3,2},{5,4},{6,5},{7,6},{9,8},{10,9},{11,10},{13,12},{... | collective-permute-start | bytes 3176 | tf_op jit(solution)/shard_map/ppermute | solution.py:26
  133.7 7.6 %collective-permute-start.13 = (f32[1,4,66,1]{3,2,1,0:T(8,128)S(1)}, f32[1,4,66,1]{3,2,1,0:T(8,128)S(1)}, u32[]{:S(2)}, u32[]{:S(2)}) collective-permute-start(f32[1,4,66,1]{3,2,1,0:T(8,128)S(1)} %get-tuple-element.32), channel_id=1, source_target_pairs={{0,1},{1,2},{2,3},{4,5},{5,6},{6,7},{8,9},{9,10},{10,11},{12,13},{... | collective-permute-start | bytes 3176 | tf_op jit(solution)/shard_map/ppermute | solution.py:23
  136.9 5.2 %collective-permute-start.28 = (f32[1,4,66,1]{3,2,1,0:T(8,128)S(1)}, f32[1,4,66,1]{3,2,1,0:T(8,128)S(1)}, u32[]{:S(2)}, u32[]{:S(2)}) collective-permute-start(f32[1,4,66,1]{3,2,1,0:T(8,128)S(1)} %get-tuple-element.29), channel_id=1, source_target_pairs={{1,0},{2,1},{3,2},{5,4},{6,5},{7,6},{9,8},{10,9},{11,10},{13,12},{... | collective-permute-start | bytes 3176 | tf_op jit(solution)/shard_map/ppermute | solution.py:26
  178.1 11.8 %collective-permute-start.30 = (f32[1,4,1,128]{3,2,1,0:T(1,128)S(1)}, f32[1,4,1,128]{3,2,1,0:T(1,128)S(1)}, u32[]{:S(2)}, u32[]{:S(2)}) collective-permute-start(f32[1,4,1,128]{3,2,1,0:T(1,128)S(1)} %get-tuple-element.42), channel_id=1, source_target_pairs={{4,0},{8,4},{12,8},{5,1},{9,5},{13,9},{6,2},{10,6},{14,10},{7,3},{... | collective-permute-start | bytes 6152 | tf_op jit(solution)/shard_map/ppermute | solution.py:26
  179.4 10.5 %collective-permute-start.31 = (f32[1,4,1,128]{3,2,1,0:T(1,128)S(1)}, f32[1,4,1,128]{3,2,1,0:T(1,128)S(1)}, u32[]{:S(2)}, u32[]{:S(2)}) collective-permute-start(f32[1,4,1,128]{3,2,1,0:T(1,128)S(1)} %get-tuple-element.41), channel_id=1, source_target_pairs={{0,4},{4,8},{8,12},{1,5},{5,9},{9,13},{2,6},{6,10},{10,14},{3,7},{... | collective-permute-start | bytes 6152 | tf_op jit(solution)/shard_map/ppermute | solution.py:23
  184.0 10.4 %collective-permute-start.14 = (f32[1,4,1,128]{3,2,1,0:T(1,128)S(1)}, f32[1,4,1,128]{3,2,1,0:T(1,128)S(1)}, u32[]{:S(2)}, u32[]{:S(2)}) collective-permute-start(f32[1,4,1,128]{3,2,1,0:T(1,128)S(1)} %get-tuple-element.44), channel_id=1, source_target_pairs={{4,0},{8,4},{12,8},{5,1},{9,5},{13,9},{6,2},{10,6},{14,10},{7,3},{... | collective-permute-start | bytes 6152 | tf_op jit(solution)/shard_map/ppermute | solution.py:26
  185.3 9.1 %collective-permute-start.15 = (f32[1,4,1,128]{3,2,1,0:T(1,128)S(1)}, f32[1,4,1,128]{3,2,1,0:T(1,128)S(1)}, u32[]{:S(2)}, u32[]{:S(2)}) collective-permute-start(f32[1,4,1,128]{3,2,1,0:T(1,128)S(1)} %get-tuple-element.43), channel_id=1, source_target_pairs={{0,4},{4,8},{8,12},{1,5},{5,9},{9,13},{2,6},{6,10},{10,14},{3,7},{... | collective-permute-start | bytes 6152 | tf_op jit(solution)/shard_map/ppermute | solution.py:23
  190.0 8.8 %collective-permute-start.32 = (f32[1,4,66,1]{3,2,1,0:T(8,128)S(1)}, f32[1,4,66,1]{3,2,1,0:T(8,128)S(1)}, u32[]{:S(2)}, u32[]{:S(2)}) collective-permute-start(f32[1,4,66,1]{3,2,1,0:T(8,128)S(1)} %get-tuple-element.25), channel_id=1, source_target_pairs={{1,0},{2,1},{3,2},{5,4},{6,5},{7,6},{9,8},{10,9},{11,10},{13,12},{... | collective-permute-start | bytes 3176 | tf_op jit(solution)/shard_map/ppermute | solution.py:26
  191.3 7.6 %collective-permute-start.33 = (f32[1,4,66,1]{3,2,1,0:T(8,128)S(1)}, f32[1,4,66,1]{3,2,1,0:T(8,128)S(1)}, u32[]{:S(2)}, u32[]{:S(2)}) collective-permute-start(f32[1,4,66,1]{3,2,1,0:T(8,128)S(1)} %get-tuple-element.26), channel_id=1, source_target_pairs={{0,1},{1,2},{2,3},{4,5},{5,6},{6,7},{8,9},{9,10},{10,11},{12,13},{... | collective-permute-start | bytes 3176 | tf_op jit(solution)/shard_map/ppermute | solution.py:23
  194.5 5.2 %collective-permute-start.16 = (f32[1,4,66,1]{3,2,1,0:T(8,128)S(1)}, f32[1,4,66,1]{3,2,1,0:T(8,128)S(1)}, u32[]{:S(2)}, u32[]{:S(2)}) collective-permute-start(f32[1,4,66,1]{3,2,1,0:T(8,128)S(1)} %get-tuple-element.27), channel_id=1, source_target_pairs={{1,0},{2,1},{3,2},{5,4},{6,5},{7,6},{9,8},{10,9},{11,10},{13,12},{... | collective-permute-start | bytes 3176 | tf_op jit(solution)/shard_map/ppermute | solution.py:26
  (11 other events, 67.8 us)
Sparse Core Ops, SparseCore 0:
  24.8 23.2 reduce-scatter.1
where the time goes:
time: 259 us; the launch traced here: 258 us
  blocking collectives  112 us (43%)
  starting transfers between devices  90.5 us (35%)
  between operations  23.2 us (9%)
  waiting for transfers between devices  19.1 us (7%)
  other arithmetic  8.34 us (3%)
  local copies, waits for them, and re-layouts  2.7 us (1%)
    psum x3, blocking collectives, inner_sum(): return lax.psum(jnp.sum(left * right, axis=(1, 2, 3)), ('tx', 'ty'))  98.3 us
    ppermute x16, starting transfers between devices, with_halo(): lax.ppermute(lax.slice_in_dim(block, block.shape[dim] - width, None, axis...  63.1 us
    ppermute x16, starting transfers between devices, with_halo(): lax.ppermute(lax.slice_in_dim(block, 0, width, axis=dim), axis, backward)  20.8 us
    reduce_scatter x1, waiting for transfers between devices, body(): lax.psum_scatter(jnp.dot(picker, cell_current, precision=HIGH, preferred_...  17 us
    all_gather x1, blocking collectives, body(): piece = lax.all_gather(adjoint[0], 'tx', axis=0, tiled=True)  13.4 us
    ppermute x2, starting transfers between devices, from_behind(): lax.ppermute(value, axis, [(source, source + steps) for source in range(i...  6.51 us
  transfers between devices with their start and end apart: 35, of which 7 were waited for; matrix products, arithmetic and copies ran while one was open for 3% of the time, Pallas kernels for 0%

commit v1 on v0

v1 whole, which is shorter than its diff:
```python
import functools

import jax
import jax.numpy as jnp
from jax import lax
from jax.experimental import pallas as pl
from jax.experimental.pallas import tpu as pltpu
from jax.sharding import PartitionSpec as P

HALO = 4
SUB = 8
LANES = 128
SLOTS = LANES // HALO
PAIRS = LANES // (2 * HALO)
F32 = jnp.float32
BF16 = jnp.bfloat16


def lanes_of(shape):
    return lax.broadcasted_iota(jnp.int32, shape, len(shape) - 1)


def rows_of(shape):
    return lax.broadcasted_iota(jnp.int32, shape, len(shape) - 2)


def tiles_of(refs):
    found = []
    for ref in refs:
        rows = ref.shape[-2]
        for plane in range(ref.shape[0] if len(ref.shape) == 3 else 1):
            for at in range(0, rows, SUB):
                if len(ref.shape) == 3:
                    found.append((ref, (plane, slice(at, at + SUB), slice(None))))
                else:
                    found.append((ref, (slice(at, at + SUB), slice(None))))
    return found


def three_parts(value):
    high = value.astype(BF16)
    rest = value - high.astype(F32)
    middle = rest.astype(BF16)
    low = (rest - middle.astype(F32)).astype(BF16)
    return high, middle, low


def dot(left, right):
    return jnp.dot(left, right, preferred_element_type=F32)


def pack_columns(cx, cy, via, ground, weight, cell, to_right, to_left):
    slot = lanes_of((SUB, LANES)) // HALO
    tiles = tiles_of((cx, cy, via, ground, weight, cell))
    for first in range(0, len(tiles), SLOTS):
        left = jnp.zeros((SUB, LANES), F32)
        right = left
        for s, (ref, index) in enumerate(tiles[first : first + SLOTS]):
            turned = pltpu.roll(ref[index], HALO * s, 1) if s else ref[index]
            left = jnp.where(slot == s, turned, left)
            right = jnp.where(slot == (s - 1) % SLOTS, turned, right)
        at = first // SLOTS * SUB
        to_right[at : at + SUB, :] = right
        to_left[at : at + SUB, :] = left


def pick(count, rows, block_row, block_count, cell, picker, chooser, main):
    me = lax.axis_index("tx")
    blocks = block_row.shape[1]
    ring = rows + 2 * HALO
    at = block_row[...]
    live = lanes_of((1, blocks)) < block_count[0]
    at = jnp.where(live, at, -rows)
    line = rows_of((ring, blocks))
    line = jnp.where(line < rows + HALO, line, line - ring)
    for k in range(count):
        owner = lax.rem(me + k, count) * rows
        hot = (line == at - owner).astype(F32)
        picker[k * ring : (k + 1) * ring, :] = hot
        owner = lax.rem(me - k + count, count) * rows
        hot = (rows_of((rows, blocks)) == at - owner).astype(F32)
        chooser[:, k * rows : (k + 1) * rows] = hot.T.astype(BF16)
    high, middle, low = three_parts(cell[...])
    hot = picker[...].astype(BF16)
    main[...] = dot(hot, high) + dot(hot, middle) + dot(hot, low)


def assemble(count, shape, refs):
    cx, cy, via, ground, weight, from_left, from_right, picker, main = refs[:9]
    side, source = refs[9:11]
    sends = refs[11 : 11 + count - 1]
    cells = refs[-1]
    rows, ring = shape
    slot = lanes_of((SUB, LANES)) // HALO
    pair = lanes_of((SUB, LANES)) // (2 * HALO)
    lower = rows_of((SUB, LANES)) < HALO
    for j, (ref, index) in enumerate(tiles_of((side, cells))):
        q, s = divmod(j, SLOTS)
        both = jnp.where(
            slot == s, from_right[q * SUB : (q + 1) * SUB, :], from_left[q * SUB : (q + 1) * SUB, :]
        )
        ref[index] = pltpu.roll(both, LANES - HALO * s, 1) if s else both

    lane = lanes_of(cells.shape)
    edge = jnp.where((lane < HALO) | (lane >= LANES - HALO), cells[...], 0.0)
    high = edge.astype(BF16).astype(F32)
    rest = edge - high
    middle = rest.astype(BF16).astype(F32)
    low = rest - middle
    spread = high + pltpu.roll(middle, 2 * HALO, 1) + pltpu.roll(low, 4 * HALO, 1)
    sums = dot(picker[...].astype(BF16), spread.astype(BF16))
    sums = (
        sums
        + pltpu.roll(sums, LANES - 2 * HALO, 1)
        + pltpu.roll(sums, LANES - 4 * HALO, 1)
    )

    def narrow(parts):
        packed = jnp.zeros((SUB, LANES), F32)
        for s, part in enumerate(parts):
            packed = jnp.where(pair == s, pltpu.roll(part, HALO + 2 * HALO * s, 1), packed)
        return packed

    source[0] = main[0:ring, :]
    source[1] = sums[0:ring]
    for k in range(1, count):
        send = sends[k - 1]
        send[0:ring, :] = main[k * ring : (k + 1) * ring, :]
        part = sums[k * ring : (k + 1) * ring]
        send[ring : ring + SUB, :] = narrow([part[i : i + SUB] for i in range(0, ring, SUB)])

    def halves(ref_planes, take, keep):
        packed = []
        for i in range(0, len(ref_planes), 2):
            tile = ref_planes[i][take]
            if i + 1 < len(ref_planes):
                other = pltpu.roll(ref_planes[i + 1][take], HALO, 0)
                tile = jnp.where(keep, tile, other)
            packed.append(tile)
        return packed

    whole = [ref.at[p] for ref in (cx, cy, via, ground, weight) for p in range(ref.shape[0])]
    sides = [side.at[p] for p in range(side.shape[0])]
    for k, take, keep in (
        (1, (slice(rows - SUB, rows), slice(None)), ~lower),
        (count - 1, (slice(0, SUB), slice(None)), lower),
    ):
        send = sends[k - 1]
        at = ring + SUB
        for tile in halves(whole, take, keep):
            send[at : at + SUB, :] = tile
            at += SUB
        send[at : at + SUB, :] = narrow(halves(sides, take, keep))


def solve(count, layers, shape, refs):
    cx_in, cy_in, via_in, ground_in, weight_in, side, source = refs[:7]
    got = refs[7 : 7 + count - 1]
    zed, you, message = refs[7 + count - 1 : 10 + count - 1]
    ext, base, zs, qs, ts, us = refs[10 + count - 1 :]
    rows, ring = shape
    width = 2 * LANES
    pair = lanes_of((SUB, LANES)) // (2 * HALO)
    lower = rows_of((SUB, LANES)) < HALO

    def widen(packed, s):
        return pltpu.roll(packed, LANES - HALO - 2 * HALO * s, 1)

    for i in range(0, ring, SUB):
        total = source[0, i : i + SUB, :]
        for ref in got:
            total = total + ref[i : i + SUB, :]
        base[i : i + SUB, 0:LANES] = total
        s = i // SUB
        total = got[0][ring : ring + SUB, :]
        for ref in got[1:]:
            total = total + ref[ring : ring + SUB, :]
        base[i : i + SUB, LANES:] = source[1, i : i + SUB, :] + widen(total, s)

    before, after = got[0], got[count - 2]
    inputs = [ref.at[p] for ref in (cx_in, cy_in, via_in, ground_in, weight_in) for p in range(ref.shape[0])]
    planes = len(inputs)
    at_side = ring + SUB + (planes + 1) // 2 * SUB

    def halo(p, prev_tile, next_tile):
        if p % 2 == 0:
            return jnp.where(lower, next_tile, prev_tile)
        return pltpu.roll(jnp.where(lower, prev_tile, next_tile), HALO, 0)

    for p, ref in enumerate(inputs):
        ext[p, 0:rows, 0:LANES] = ref[...]
        ext[p, 0:rows, LANES:] = side[p]
        at = ring + SUB + p // 2 * SUB
        ext[p, rows:ring, 0:LANES] = halo(p, before[at : at + SUB, :], after[at : at + SUB, :])
        ext[p, rows:ring, LANES:] = halo(
            p,
            widen(before[at_side : at_side + SUB, :], p // 2),
            widen(after[at_side : at_side + SUB, :], p // 2),
        )

    def below(v):
        return pltpu.roll(v, ring - 1, 0)

    def above(v):
        return pltpu.roll(v, 1, 0)

    def right(v):
        return pltpu.roll(v, width - 1, 1)

    def left(v):
        return pltpu.roll(v, 1, 1)

    cx = [ext[p] for p in range(layers)]
    cy = [ext[layers + p] for p in range(layers)]
    via = [ext[2 * layers + p] for p in range(layers - 1)]
    ground = [ext[3 * layers - 1 + p] for p in range(layers)]
    weight = [ext[4 * layers - 1 + p] for p in range(layers)]
    row, lane = rows_of((ring, width)), lanes_of((ring, width))
    tx, ty = lax.axis_index("tx"), lax.axis_index("ty")
    inside = (
        ((row < rows) | (row >= rows + HALO) | (tx < lax.axis_size("tx") - 1))
        & ((row < rows + HALO) | (tx > 0))
        & ((lane < LANES) | (lane >= width - HALO) | ((lane < LANES + HALO) & (ty < lax.axis_size("ty") - 1)))
        & ((lane < width - HALO) | (ty > 0))
    )
    cx_low = [jnp.where((row == 0) & (tx == 0), 0.0, above(v)) for v in cx]
    cy_low = [jnp.where((lane == 0) & (ty == 0), 0.0, left(v)) for v in cy]
    diagonal, inverse = [], []
    for p in range(layers):
        total = ground[p] + cx[p] + cx_low[p] + cy[p] + cy_low[p]
        if p + 1 < layers:
            total = total + via[p]
        if p > 0:
            total = total + via[p - 1]
        diagonal.append(total)
        inverse.append(jnp.where(inside, 1.0 / total, 0.0))

    def couple(v, p):
        total = None
        if v[p] is not None:
            total = (
                cx[p] * below(v[p])
                + cx_low[p] * above(v[p])
                + cy[p] * right(v[p])
                + cy_low[p] * left(v[p])
            )
        if p + 1 < layers and v[p + 1] is not None:
            term = via[p] * v[p + 1]
            total = term if total is None else total + term
        if p > 0 and v[p - 1] is not None:
            term = via[p - 1] * v[p - 1]
            total = term if total is None else total + term
        return total

    def smooth(b):
        scaled = [None if b[p] is None else inverse[p] * b[p] for p in range(layers)]
        result = []
        for p in range(layers):
            total = couple(scaled, p)
            if total is None:
                result.append(None)
                continue
            if b[p] is not None:
                total = total + b[p]
            result.append(inverse[p] * total)
        return result

    def tile_sum(left_, right_):
        total = None
        for p in range(layers):
            if left_[p] is None or right_[p] is None:
                continue
            term = left_[p][0:rows, 0:LANES] * right_[p][0:rows, 0:LANES]
            total = term if total is None else total + term
        return jnp.sum(total, axis=0, keepdims=True)

    for which, b in enumerate(([base[...]] + [None] * (layers - 1), weight)):
        z = smooth(b)
        q = []
        for p in range(layers):
            term = couple(z, p)
            q.append(None if z[p] is None and term is None else (-term if z[p] is None else diagonal[p] * z[p] - term))
        u = smooth(q)
        flow = []
        for p in range(layers):
            term = cx[p] * below(u[p]) + cy[p] * right(u[p])
            if p + 1 < layers:
                term = term + via[p] * u[p + 1]
            flow.append(diagonal[p] * u[p] - 2.0 * term)
        at = 2 * rows + 4 * which
        message[at : at + 4, :] = jnp.concatenate(
            [tile_sum(b, z), tile_sum(z, q), tile_sum(q, u), tile_sum(u, flow)], axis=0
        )
        if which == 0:
            for p in range(layers):
                if z[p] is not None:
                    zed[p] = z[p][0:rows, 0:LANES]
                you[p] = u[p][0:rows, 0:LANES]
        else:
            message[0:rows, :] = z[0][0:rows, 0:LANES]
            message[rows : 2 * rows, :] = u[0][0:rows, 0:LANES]


def choose(count, rows, refs):
    chooser = refs[0]
    messages = refs[1 : 1 + count]
    chosen = refs[1 + count]
    hot = chooser[...]
    for half in range(2):
        field = jnp.concatenate([ref[half * rows : (half + 1) * rows, :] for ref in messages], axis=0)
        high, middle, low = three_parts(field)
        chosen[:, half * LANES : (half + 1) * LANES] = dot(hot, high) + dot(hot, middle) + dot(hot, low)


def finish(ways, refs):
    sums = refs[:ways]
    zed, you, chosen, drop, sense = refs[ways:]
    total = sums[0][...]
    for ref in sums[1:]:
        total = total + ref[...]
    total = jnp.broadcast_to(jnp.sum(total, axis=1, keepdims=True), (SUB, LANES))
    for which in range(2):
        bz, zq, qu, uw = (total[4 * which + i : 4 * which + i + 1] for i in range(4))
        ratio = qu / zq
        step = bz / zq
        second = (zq - ratio * bz) / (uw - ratio * qu)
        first = step - second * ratio
        if which == 0:
            for p in range(you.shape[0]):
                part = second * you[p]
                drop[p] = first * zed[p] + part if p < zed.shape[0] else part
        else:
            sense[...] = first * chosen[:, 0:LANES] + second * chosen[:, LANES:]


def vmem():
    return pl.BlockSpec(memory_space=pltpu.VMEM)


def call(kernel, outs, args, scratch=(), specs=None, flops=0):
    size = sum(a.size * a.dtype.itemsize for a in list(args) + list(outs))
    return pl.pallas_call(
        kernel,
        out_shape=tuple(outs),
        in_specs=specs or [vmem() for _ in args],
        out_specs=tuple(vmem() for _ in outs),
        scratch_shapes=scratch,
        cost_estimate=pl.CostEstimate(flops=flops, bytes_accessed=size, transcendentals=0),
        compiler_params=pltpu.CompilerParams(vmem_limit_bytes=48 * 1024 * 1024),
    )(*args)


def shift(value, axis, steps):
    count = lax.axis_size(axis)
    return lax.ppermute(value, axis, [(i, (i + steps) % count) for i in range(count)])


def body(cell_current, block_row, block_count, cond_x, cond_y, cond_via, ground, drop_weight):
    blocks, width = cell_current.shape
    layers, rows, _ = cond_x.shape
    count, ways = lax.axis_size("tx"), lax.axis_size("ty")
    ring = rows + 2 * HALO
    fields = (cond_x, cond_y, cond_via, ground, drop_weight)
    planes = sum(f.shape[0] for f in fields)

    def array(*dims, dtype=F32):
        return jax.ShapeDtypeStruct(dims, dtype)

    tiles = planes * rows // SUB + blocks // SUB
    packed = array(pl.cdiv(tiles, SLOTS) * SUB, LANES)
    to_right, to_left = call(pack_columns, (packed, packed), fields + (cell_current,))
    from_left = shift(to_right, "ty", 1)
    from_right = shift(to_left, "ty", -1)

    picker, chooser, main = call(
        functools.partial(pick, count, rows),
        (array(count * ring, blocks), array(blocks, count * rows, dtype=BF16), array(count * ring, width)),
        (block_row.reshape(1, blocks), block_count, cell_current),
        specs=[vmem(), pl.BlockSpec(memory_space=pltpu.SMEM), vmem()],
    )

    edges = (planes + 1) // 2 * SUB + SUB
    lengths = [ring + SUB + (edges if k in (1, count - 1) else 0) for k in range(1, count)]
    side, source, *sends = call(
        lambda *refs: assemble(count, (rows, ring), refs),
        [array(planes, rows, LANES), array(2, ring, LANES)] + [array(n, LANES) for n in lengths],
        fields + (from_left, from_right, picker, main),
        scratch=[pltpu.VMEM((blocks, LANES), F32)],
    )
    got = [shift(send, "tx", k + 1) for k, send in enumerate(sends)]

    field = pltpu.VMEM((layers, ring, 2 * LANES), F32)
    zed, you, message = call(
        lambda *refs: solve(count, layers, (rows, ring), refs),
        (array(min(2, layers), rows, LANES), array(layers, rows, LANES), array(2 * rows + SUB, LANES)),
        fields + (side, source, *got),
        scratch=[pltpu.VMEM((planes, ring, 2 * LANES), F32), pltpu.VMEM((ring, 2 * LANES), F32)] + [field] * 4,
    )
    messages = [message] + [shift(message, "tx", k) for k in range(1, count)]
    total = functools.reduce(jnp.add, [m[2 * rows :] for m in messages])
    totals = [total] + [shift(total, "ty", k) for k in range(1, ways)]
    (chosen,) = call(
        lambda *refs: choose(count, rows, refs),
        (array(blocks, 2 * LANES),),
        (chooser, *messages),
    )
    return call(
        lambda *refs: finish(ways, refs),
        (array(layers, rows, LANES), array(blocks, width)),
        (*totals, zed, you, chosen),
    )


def solution(mesh):
    placed = (
        P(("grp", "tx"), "ty"),
        P(("grp", "tx")),
        P(("grp", "tx")),
        P(None, ("grp", "tx"), "ty"),
        P(None, ("grp", "tx"), "ty"),
        P(None, ("grp", "tx"), "ty"),
        P(None, ("grp", "tx"), "ty"),
        P(None, ("grp", "tx"), "ty"),
    )
    return jax.shard_map(
        body,
        mesh=mesh,
        in_specs=placed,
        out_specs=(P(None, ("grp", "tx"), "ty"), P(("grp", "tx"), "ty")),
        check_vma=False,
    )
```

time: 259 us -> 39.2 us (0.15)
  blocking collectives: 112 us -> 0 us
  starting transfers between devices: 90.5 us -> 12.4 us
  between operations: 23.2 us -> 1.39 us
  other arithmetic: 8.34 us -> 0.01 us
  Pallas kernels: 0 us -> 4.42 us
  waiting for transfers between devices: 19.1 us -> 15.2 us
  local copies, waits for them, and re-layouts: 2.7 us -> 5.51 us
    psum x3 -> x0, blocking collectives: 98.3 us -> none  [inner_sum(): return lax.psum(jnp.sum(left * right, axis=(1, 2, 3)), ('tx', 'ty'))]
    ppermute x34 -> x11, starting transfers between devices: 90.4 us -> 12.4 us  [shift(): lax.ppermute(value, axis, [(i, (i + steps) % count) for i in range(count)])]
    reduce_scatter x1 -> x0, waiting for transfers between devices: 17 us -> none  [body(): lax.psum_scatter(jnp.dot(picker, cell_current, precision=HIGH, preferred_...]
    all_gather x1 -> x0, blocking collectives: 13.4 us -> none  [body(): piece = lax.all_gather(adjoint[0], 'tx', axis=0, tiled=True)]
    ppermute x34 -> x11, waiting for transfers between devices: 2.14 us -> 15.2 us  [shift(): lax.ppermute(value, axis, [(i, (i + steps) % count) for i in range(count)])]
    unnamed x16 -> x26, local copies, waits for them, and re-layouts: 0.14 us -> 5.51 us
    reduce_sum x6 -> x0, other arithmetic: 4.92 us -> none  [inner_sum(): return lax.psum(jnp.sum(left * right, axis=(1, 2, 3)), ('tx', 'ty'))]
    pallas_call x0 -> x6, Pallas kernels: none -> 4.42 us  [call(): pl.pallas_call(kernel, out_shape=tuple(outs), in_specs=specs or [vmem() f...]
  transfers between devices with their start and end apart: 35 -> 11, of which waited for: 7 -> 7; matrix products, arithmetic and copies ran while one was open for 3% -> 0% of each run, Pallas kernels for 0% -> 3%
where the time goes in v1:
time: 39.2 us; the launch traced here: 38.9 us
  waiting for transfers between devices  15.2 us (39%)
  starting transfers between devices  12.4 us (32%)
  local copies, waits for them, and re-layouts  5.51 us (14%)
  Pallas kernels  4.42 us (11%)
  between operations  1.39 us (4%)
    ppermute x11, waiting for transfers between devices, shift(): lax.ppermute(value, axis, [(i, (i + steps) % count) for i in range(count)])  15.2 us
    ppermute x11, starting transfers between devices, shift(): lax.ppermute(value, axis, [(i, (i + steps) % count) for i in range(count)])  12.4 us
    unnamed x26, local copies, waits for them, and re-layouts  5.51 us
    pallas_call x6, Pallas kernels, call(): pl.pallas_call(kernel, out_shape=tuple(outs), in_specs=specs or [vmem() f...  4.42 us
  transfers between devices with their start and end apart: 11, of which 7 were waited for; matrix products, arithmetic and copies ran while one was open for 0% of the time, Pallas kernels for 3%

profile of v1, /device:TPU:0, one launch (start us, length us, event | category | flops | bytes accessed | tf_op | source)
XLA Modules:
  0.0 38.9 jit_solution(12229889654507605047)
XLA Ops:
  0.6 0.0 copy-start
  0.6 0.9 %copy-done = f32[4,64,128]{2,1,0:T(8,128)S(1)} copy-done((f32[4,64,128]{2,1,0:T(8,128)S(1)}, f32[4,64,128]{2,1,0:T(8,128)}, u32[]{:S(2)}) %copy-start) | copy-done | bytes 131096
  1.5 0.9 %copy-done.2 = f32[4,64,128]{2,1,0:T(8,128)S(1)} copy-done((f32[4,64,128]{2,1,0:T(8,128)S(1)}, f32[4,64,128]{2,1,0:T(8,128)}, u32[]{:S(2)}) %copy-start.2) | copy-done | bytes 131096
  2.4 0.9 %copy-done.4 = f32[4,64,128]{2,1,0:T(8,128)S(1)} copy-done((f32[4,64,128]{2,1,0:T(8,128)S(1)}, f32[4,64,128]{2,1,0:T(8,128)}, u32[]{:S(2)}) %copy-start.4) | copy-done | bytes 131096
  3.3 0.9 %copy-done.6 = f32[4,64,128]{2,1,0:T(8,128)S(1)} copy-done((f32[4,64,128]{2,1,0:T(8,128)S(1)}, f32[4,64,128]{2,1,0:T(8,128)}, u32[]{:S(2)}) %copy-start.6) | copy-done | bytes 131096
  4.3 0.9 %copy-done.8 = f32[512,128]{1,0:T(8,128)S(1)} copy-done((f32[512,128]{1,0:T(8,128)S(1)}, f32[512,128]{1,0:T(8,128)}, u32[]{:S(2)}) %copy-start.8) | copy-done | bytes 262168
  5.2 0.9 %copy-done.10 = f32[3,64,128]{2,1,0:T(8,128)S(1)} copy-done((f32[3,64,128]{2,1,0:T(8,128)S(1)}, f32[3,64,128]{2,1,0:T(8,128)}, u32[]{:S(2)}) %copy-start.10) | copy-done | bytes 98328
  6.1 0.3 shard_map.95
  6.4 0.5 %collective-permute-start = (f32[56,128]{1,0:T(8,128)S(1)}, f32[56,128]{1,0:T(8,128)S(1)}, u32[]{:S(2)}, u32[]{:S(2)}) collective-permute-start(f32[56,128]{1,0:T(8,128)S(1)} %get-tuple-element.15), channel_id=1, source_target_pairs={{0,1},{1,2},{2,3},{3,0},{4,5},{5,6},{6,7},{7,4},{8,9},{9,10},{10,1... | collective-permute-start | bytes 86024 | tf_op jit(solution)/shard_map/ppermute | solution.py:355
  6.9 2.0 %collective-permute-start.1 = (f32[56,128]{1,0:T(8,128)S(1)}, f32[56,128]{1,0:T(8,128)S(1)}, u32[]{:S(2)}, u32[]{:S(2)}) collective-permute-start(f32[56,128]{1,0:T(8,128)S(1)} %get-tuple-element.16), channel_id=1, source_target_pairs={{0,3},{1,0},{2,1},{3,2},{4,7},{5,4},{6,5},{7,6},{8,11},{9,8},{10,9... | collective-permute-start | bytes 86024 | tf_op jit(solution)/shard_map/ppermute | solution.py:355
  9.6 0.0 copy-start.1
  9.6 0.5 %shard_map.96 = (f32[288,512]{1,0:T(8,128)S(1)}, bf16[512,256]{1,0:T(8,128)(2,1)S(1)}, f32[288,128]{1,0:T(8,128)S(1)}) custom-call(s32[1,512]{1,0:T(1,128)S(1)} %bitcast.1, s32[1]{0:T(128)S(6)} %copy.10.block_count, f32[512,128]{1,0:T(8,128)S(1)} %copy-done.9), custom_call_target="tpu_custom_call" | custom-call | bytes 1263620 | tf_op jit(solution)/shard_map/pallas_call | solution.py:342
  10.1 0.3 collective-permute-done.refs_5_
  10.4 0.1 collective-permute-done.1.refs_6_
  10.5 0.0 copy-done.3
  10.6 0.8 %shard_map.97 = (f32[19,64,128]{2,1,0:T(8,128)S(1)}, f32[2,72,128]{2,1,0:T(8,128)S(1)}, f32[168,128]{1,0:T(8,128)S(1)}, f32[80,128]{1,0:T(8,128)S(1)}, f32[168,128]{1,0:T(8,128)S(1)}) custom-call(f32[4,64,128]{2,1,0:T(8,128)S(1)} %copy-done.1, f32[4,64,128]{2,1,0:T(8,128)S(1)} %copy-done.3, f32[3,64,128]{2,1,0:T(8,128)S(1)} %copy-done.11, ...), custom_call_target="tpu_custom_call" | custom-call | bytes 2326528 | tf_op jit(solution)/shard_map/pallas_call | solution.py:342
  11.3 2.4 %collective-permute-start.2 = (f32[168,128]{1,0:T(8,128)S(1)}, f32[168,128]{1,0:T(8,128)S(1)}, u32[]{:S(2)}, u32[]{:S(2)}) collective-permute-start(f32[168,128]{1,0:T(8,128)S(1)} %get-tuple-element.21), channel_id=1, source_target_pairs={{0,4},{4,8},{8,12},{12,0},{1,5},{5,9},{9,13},{13,1},{2,6},{6,10},{... | collective-permute-start | bytes 258056 | tf_op jit(solution)/shard_map/ppermute | solution.py:355
  13.7 2.1 %collective-permute-start.4 = (f32[168,128]{1,0:T(8,128)S(1)}, f32[168,128]{1,0:T(8,128)S(1)}, u32[]{:S(2)}, u32[]{:S(2)}) collective-permute-start(f32[168,128]{1,0:T(8,128)S(1)} %get-tuple-element.23), channel_id=1, source_target_pairs={{0,12},{4,0},{8,4},{12,8},{1,13},{5,1},{9,5},{13,9},{2,14},{6,2},{... | collective-permute-start | bytes 258056 | tf_op jit(solution)/shard_map/ppermute | solution.py:355
  15.8 0.9 %collective-permute-start.3 = (f32[80,128]{1,0:T(8,128)S(1)}, f32[80,128]{1,0:T(8,128)S(1)}, u32[]{:S(2)}, u32[]{:S(2)}) collective-permute-start(f32[80,128]{1,0:T(8,128)S(1)} %get-tuple-element.22), channel_id=1, source_target_pairs={{0,8},{4,12},{8,0},{12,4},{1,9},{5,13},{9,1},{13,5},{2,10},{6,14},... | collective-permute-start | bytes 122888 | tf_op jit(solution)/shard_map/ppermute | solution.py:355
  16.7 5.9 %collective-permute-done.3.refs_8_ = f32[80,128]{1,0:T(8,128)S(1)} collective-permute-done((f32[80,128]{1,0:T(8,128)S(1)}, f32[80,128]{1,0:T(8,128)S(1)}, u32[]{:S(2)}, u32[]{:S(2)}) %collective-permute-start.3) | collective-permute-done | bytes 40992 | tf_op jit(solution)/shard_map/ppermute | solution.py:355
  22.7 1.5 %shard_map.98 = (f32[2,64,128]{2,1,0:T(8,128)S(1)}, f32[4,64,128]{2,1,0:T(8,128)S(1)}, f32[136,128]{1,0:T(8,128)S(1)}) custom-call(f32[4,64,128]{2,1,0:T(8,128)S(1)} %copy-done.1, f32[4,64,128]{2,1,0:T(8,128)S(1)} %copy-done.3, f32[3,64,128]{2,1,0:T(8,128)S(1)} %copy-done.11, f32[4,64,128]{2,1,0:T(8,128)S(1)} %copy-done.5, f32[4,64,128]{2,1,0:T(8,128)S(1)} %copy-done.7, ...), custom_call_target="tpu_custom_call" | custom-call | bytes 1798144 | tf_op jit(solution)/shard_map/pallas_call | solution.py:342
  24.1 2.2 %collective-permute-start.7 = (f32[136,128]{1,0:T(8,128)S(1)}, f32[136,128]{1,0:T(8,128)S(1)}, u32[]{:S(2)}, u32[]{:S(2)}) collective-permute-start(f32[136,128]{1,0:T(8,128)S(1)} %get-tuple-element.24.refs_1_), channel_id=1, source_target_pairs={{0,12},{4,0},{8,4},{12,8},{1,13},{5,1},{9,5},{13,9},{2,14},{6,2},{... | collective-permute-start | bytes 208904 | tf_op jit(solution)/shard_map/ppermute | solution.py:355
  26.3 0.6 %collective-permute-start.5 = (f32[136,128]{1,0:T(8,128)S(1)}, f32[136,128]{1,0:T(8,128)S(1)}, u32[]{:S(2)}, u32[]{:S(2)}) collective-permute-start(f32[136,128]{1,0:T(8,128)S(1)} %get-tuple-element.24.refs_1_), channel_id=1, source_target_pairs={{0,4},{4,8},{8,12},{12,0},{1,5},{5,9},{9,13},{13,1},{2,6},{6,10},{... | collective-permute-start | bytes 208904 | tf_op jit(solution)/shard_map/ppermute | solution.py:355
  26.9 1.9 %collective-permute-done.7.refs_4_ = f32[136,128]{1,0:T(8,128)S(1)} collective-permute-done((f32[136,128]{1,0:T(8,128)S(1)}, f32[136,128]{1,0:T(8,128)S(1)}, u32[]{:S(2)}, u32[]{:S(2)}) %collective-permute-start.7) | collective-permute-done | bytes 69664 | tf_op jit(solution)/shard_map/ppermute | solution.py:355
  28.9 4.6 %collective-permute-done.6.refs_3_ = f32[136,128]{1,0:T(8,128)S(1)} collective-permute-done((f32[136,128]{1,0:T(8,128)S(1)}, f32[136,128]{1,0:T(8,128)S(1)}, u32[]{:S(2)}, u32[]{:S(2)}) %collective-permute-start.6) | collective-permute-done | bytes 69664 | tf_op jit(solution)/shard_map/ppermute | solution.py:355
  33.5 0.7 %collective-permute-start.10 = (f32[8,128]{1,0:T(8,128)S(1)}, f32[8,128]{1,0:T(8,128)S(1)}, u32[]{:S(2)}, u32[]{:S(2)}) collective-permute-start(f32[8,128]{1,0:T(8,128)S(1)} %slice_add_fusion.refs_0_), channel_id=1, source_target_pairs={{0,3},{1,0},{2,1},{3,2},{4,7},{5,4},{6,5},{7,6},{8,11},{9,8},{10,9... | collective-permute-start | bytes 12296 | tf_op jit(solution)/shard_map/ppermute | solution.py:355
  34.2 0.8 %collective-permute-start.9 = (f32[8,128]{1,0:T(8,128)S(1)}, f32[8,128]{1,0:T(8,128)S(1)}, u32[]{:S(2)}, u32[]{:S(2)}) collective-permute-start(f32[8,128]{1,0:T(8,128)S(1)} %slice_add_fusion.refs_0_), channel_id=1, source_target_pairs={{0,2},{1,3},{2,0},{3,1},{4,6},{5,7},{6,4},{7,5},{8,10},{9,11},{10,... | collective-permute-start | bytes 12296 | tf_op jit(solution)/shard_map/ppermute | solution.py:355
  35.0 0.2 collective-permute-start.8
  35.2 0.6 %shard_map.99.refs_6_ = f32[512,256]{1,0:T(8,128)S(1)} custom-call(bf16[512,256]{1,0:T(8,128)(2,1)S(1)} %get-tuple-element.27.refs_0_, f32[136,128]{1,0:T(8,128)S(1)} %get-tuple-element.24.refs_1_, f32[136,128]{1,0:T(8,128)S(1)} %collective-permute-done.5.refs_2_, f32[136,128]{1,0:T(8,128)S(1)} %collective-permute-done.6.refs_3_, ...), custom_call_target="tpu_custom_call" | custom-call | bytes 1064960 | tf_op jit(solution)/shard_map/pallas_call | solution.py:342
  35.7 2.0 %collective-permute-done.9.refs_2_ = f32[8,128]{1,0:T(8,128)S(1)} collective-permute-done((f32[8,128]{1,0:T(8,128)S(1)}, f32[8,128]{1,0:T(8,128)S(1)}, u32[]{:S(2)}, u32[]{:S(2)}) %collective-permute-start.9) | collective-permute-done | bytes 4128 | tf_op jit(solution)/shard_map/ppermute | solution.py:355
  37.8 0.2 collective-permute-done.8.refs_1_
  38.0 0.9 %shard_map.100 = (f32[4,64,128]{2,1,0:T(8,128)}, f32[512,128]{1,0:T(8,128)}) custom-call(f32[8,128]{1,0:T(8,128)S(1)} %slice_add_fusion.refs_0_, f32[8,128]{1,0:T(8,128)S(1)} %collective-permute-done.8.refs_1_, f32[8,128]{1,0:T(8,128)S(1)} %collective-permute-done.9.refs_2_, f32[8,128]{1,0:T(8,128)S(1)} %collective-permute-done.10.refs_3_, ...), custom_call_target="tpu_custom_call" | custom-call | bytes 1130496 | tf_op jit(solution)/shard_map/pallas_call | solution.py:342
  (23 shorter events, 0.1 us)
Async XLA Ops:
  0.6 0.9 %copy-start = (f32[4,64,128]{2,1,0:T(8,128)S(1)}, f32[4,64,128]{2,1,0:T(8,128)}, u32[]{:S(2)}) copy-start(f32[4,64,128]{2,1,0:T(8,128)} %refs_0_.3) | copy-start | bytes 393220
  1.5 0.9 %copy-start.2 = (f32[4,64,128]{2,1,0:T(8,128)S(1)}, f32[4,64,128]{2,1,0:T(8,128)}, u32[]{:S(2)}) copy-start(f32[4,64,128]{2,1,0:T(8,128)} %refs_1_.3) | copy-start | bytes 393220
  2.4 0.9 %copy-start.4 = (f32[4,64,128]{2,1,0:T(8,128)S(1)}, f32[4,64,128]{2,1,0:T(8,128)}, u32[]{:S(2)}) copy-start(f32[4,64,128]{2,1,0:T(8,128)} %refs_3_.3) | copy-start | bytes 393220
  3.3 0.9 %copy-start.6 = (f32[4,64,128]{2,1,0:T(8,128)S(1)}, f32[4,64,128]{2,1,0:T(8,128)}, u32[]{:S(2)}) copy-start(f32[4,64,128]{2,1,0:T(8,128)} %refs_4_.3) | copy-start | bytes 393220
  4.3 0.9 %copy-start.8 = (f32[512,128]{1,0:T(8,128)S(1)}, f32[512,128]{1,0:T(8,128)}, u32[]{:S(2)}) copy-start(f32[512,128]{1,0:T(8,128)} %cell.3) | copy-start | bytes 786436
  5.2 0.9 %copy-start.10 = (f32[3,64,128]{2,1,0:T(8,128)S(1)}, f32[3,64,128]{2,1,0:T(8,128)}, u32[]{:S(2)}) copy-start(f32[3,64,128]{2,1,0:T(8,128)} %refs_2_.3) | copy-start | bytes 294916
  6.1 3.5 %copy-start.9 = (f32[512,128]{1,0:T(8,128)S(1)}, f32[512,128]{1,0:T(8,128)}, u32[]{:S(2)}) copy-start(f32[512,128]{1,0:T(8,128)} %cell.3) | copy-start | bytes 786436
  6.1 4.4 %copy-start.5 = (f32[4,64,128]{2,1,0:T(8,128)S(1)}, f32[4,64,128]{2,1,0:T(8,128)}, u32[]{:S(2)}) copy-start(f32[4,64,128]{2,1,0:T(8,128)} %refs_3_.3) | copy-start | bytes 393220
  6.1 4.4 %copy-start.7 = (f32[4,64,128]{2,1,0:T(8,128)S(1)}, f32[4,64,128]{2,1,0:T(8,128)}, u32[]{:S(2)}) copy-start(f32[4,64,128]{2,1,0:T(8,128)} %refs_4_.3) | copy-start | bytes 393220
  6.1 4.4 %copy-start.11 = (f32[3,64,128]{2,1,0:T(8,128)S(1)}, f32[3,64,128]{2,1,0:T(8,128)}, u32[]{:S(2)}) copy-start(f32[3,64,128]{2,1,0:T(8,128)} %refs_2_.3) | copy-start | bytes 294916
  6.4 4.0 %collective-permute-start = (f32[56,128]{1,0:T(8,128)S(1)}, f32[56,128]{1,0:T(8,128)S(1)}, u32[]{:S(2)}, u32[]{:S(2)}) collective-permute-start(f32[56,128]{1,0:T(8,128)S(1)} %get-tuple-element.15), channel_id=1, source_target_pairs={{0,1},{1,2},{2,3},{3,0},{4,5},{5,6},{6,7},{7,4},{8,9},{9,10},{10,1... | collective-permute-start | bytes 86024 | tf_op jit(solution)/shard_map/ppermute | solution.py:355
  6.9 2.7 %copy-start.12 = (s32[512]{0:T(512)S(1)}, s32[512]{0:T(512)}, u32[]{:S(2)}) copy-start(s32[512]{0:T(512)} %param.9) | copy-start | bytes 6148
  6.9 3.6 %collective-permute-start.1 = (f32[56,128]{1,0:T(8,128)S(1)}, f32[56,128]{1,0:T(8,128)S(1)}, u32[]{:S(2)}, u32[]{:S(2)}) collective-permute-start(f32[56,128]{1,0:T(8,128)S(1)} %get-tuple-element.16), channel_id=1, source_target_pairs={{0,3},{1,0},{2,1},{3,2},{4,7},{5,4},{6,5},{7,6},{8,11},{9,8},{10,9... | collective-permute-start | bytes 86024 | tf_op jit(solution)/shard_map/ppermute | solution.py:355
  9.6 0.9 %copy-start.1 = (f32[4,64,128]{2,1,0:T(8,128)S(1)}, f32[4,64,128]{2,1,0:T(8,128)}, u32[]{:S(2)}) copy-start(f32[4,64,128]{2,1,0:T(8,128)} %refs_0_.3) | copy-start | bytes 393220
  9.6 1.0 %copy-start.3 = (f32[4,64,128]{2,1,0:T(8,128)S(1)}, f32[4,64,128]{2,1,0:T(8,128)}, u32[]{:S(2)}) copy-start(f32[4,64,128]{2,1,0:T(8,128)} %refs_1_.3) | copy-start | bytes 393220
  11.3 11.3 %collective-permute-start.2 = (f32[168,128]{1,0:T(8,128)S(1)}, f32[168,128]{1,0:T(8,128)S(1)}, u32[]{:S(2)}, u32[]{:S(2)}) collective-permute-start(f32[168,128]{1,0:T(8,128)S(1)} %get-tuple-element.21), channel_id=1, source_target_pairs={{0,4},{4,8},{8,12},{12,0},{1,5},{5,9},{9,13},{13,1},{2,6},{6,10},{... | collective-permute-start | bytes 258056 | tf_op jit(solution)/shard_map/ppermute | solution.py:355
  13.7 9.0 %collective-permute-start.4 = (f32[168,128]{1,0:T(8,128)S(1)}, f32[168,128]{1,0:T(8,128)S(1)}, u32[]{:S(2)}, u32[]{:S(2)}) collective-permute-start(f32[168,128]{1,0:T(8,128)S(1)} %get-tuple-element.23), channel_id=1, source_target_pairs={{0,12},{4,0},{8,4},{12,8},{1,13},{5,1},{9,5},{13,9},{2,14},{6,2},{... | collective-permute-start | bytes 258056 | tf_op jit(solution)/shard_map/ppermute | solution.py:355
  15.8 6.9 %collective-permute-start.3 = (f32[80,128]{1,0:T(8,128)S(1)}, f32[80,128]{1,0:T(8,128)S(1)}, u32[]{:S(2)}, u32[]{:S(2)}) collective-permute-start(f32[80,128]{1,0:T(8,128)S(1)} %get-tuple-element.22), channel_id=1, source_target_pairs={{0,8},{4,12},{8,0},{12,4},{1,9},{5,13},{9,1},{13,5},{2,10},{6,14},... | collective-permute-start | bytes 122888 | tf_op jit(solution)/shard_map/ppermute | solution.py:355
  24.1 4.7 %collective-permute-start.7 = (f32[136,128]{1,0:T(8,128)S(1)}, f32[136,128]{1,0:T(8,128)S(1)}, u32[]{:S(2)}, u32[]{:S(2)}) collective-permute-start(f32[136,128]{1,0:T(8,128)S(1)} %get-tuple-element.24.refs_1_), channel_id=1, source_target_pairs={{0,12},{4,0},{8,4},{12,8},{1,13},{5,1},{9,5},{13,9},{2,14},{6,2},{... | collective-permute-start | bytes 208904 | tf_op jit(solution)/shard_map/ppermute | solution.py:355
  26.3 7.2 %collective-permute-start.6 = (f32[136,128]{1,0:T(8,128)S(1)}, f32[136,128]{1,0:T(8,128)S(1)}, u32[]{:S(2)}, u32[]{:S(2)}) collective-permute-start(f32[136,128]{1,0:T(8,128)S(1)} %get-tuple-element.24.refs_1_), channel_id=1, source_target_pairs={{0,8},{4,12},{8,0},{12,4},{1,9},{5,13},{9,1},{13,5},{2,10},{6,14},... | collective-permute-start | bytes 208904 | tf_op jit(solution)/shard_map/ppermute | solution.py:355
  26.3 7.2 %collective-permute-start.5 = (f32[136,128]{1,0:T(8,128)S(1)}, f32[136,128]{1,0:T(8,128)S(1)}, u32[]{:S(2)}, u32[]{:S(2)}) collective-permute-start(f32[136,128]{1,0:T(8,128)S(1)} %get-tuple-element.24.refs_1_), channel_id=1, source_target_pairs={{0,4},{4,8},{8,12},{12,0},{1,5},{5,9},{9,13},{13,1},{2,6},{6,10},{... | collective-permute-start | bytes 208904 | tf_op jit(solution)/shard_map/ppermute | solution.py:355
  33.5 2.3 %collective-permute-start.10 = (f32[8,128]{1,0:T(8,128)S(1)}, f32[8,128]{1,0:T(8,128)S(1)}, u32[]{:S(2)}, u32[]{:S(2)}) collective-permute-start(f32[8,128]{1,0:T(8,128)S(1)} %slice_add_fusion.refs_0_), channel_id=1, source_target_pairs={{0,3},{1,0},{2,1},{3,2},{4,7},{5,4},{6,5},{7,6},{8,11},{9,8},{10,9... | collective-permute-start | bytes 12296 | tf_op jit(solution)/shard_map/ppermute | solution.py:355
  34.2 3.6 %collective-permute-start.9 = (f32[8,128]{1,0:T(8,128)S(1)}, f32[8,128]{1,0:T(8,128)S(1)}, u32[]{:S(2)}, u32[]{:S(2)}) collective-permute-start(f32[8,128]{1,0:T(8,128)S(1)} %slice_add_fusion.refs_0_), channel_id=1, source_target_pairs={{0,2},{1,3},{2,0},{3,1},{4,6},{5,7},{6,4},{7,5},{8,10},{9,11},{10,... | collective-permute-start | bytes 12296 | tf_op jit(solution)/shard_map/ppermute | solution.py:355
  35.0 3.0 %collective-permute-start.8 = (f32[8,128]{1,0:T(8,128)S(1)}, f32[8,128]{1,0:T(8,128)S(1)}, u32[]{:S(2)}, u32[]{:S(2)}) collective-permute-start(f32[8,128]{1,0:T(8,128)S(1)} %slice_add_fusion.refs_0_), channel_id=1, source_target_pairs={{0,1},{1,2},{2,3},{3,0},{4,5},{5,6},{6,7},{7,4},{8,9},{9,10},{10,1... | collective-permute-start | bytes 12296 | tf_op jit(solution)/shard_map/ppermute | solution.py:355

commit v2 on v1

v2 whole, which is shorter than its diff:
```python
import functools

import jax
import jax.numpy as jnp
from jax import lax
from jax.experimental import pallas as pl
from jax.experimental.pallas import tpu as pltpu
from jax.sharding import PartitionSpec as P

HALO = 4
SUB = 8
LANES = 128
SLOTS = LANES // HALO
F32 = jnp.float32
BF16 = jnp.bfloat16


def lanes_of(shape):
    return lax.broadcasted_iota(jnp.int32, shape, len(shape) - 1)


def rows_of(shape):
    return lax.broadcasted_iota(jnp.int32, shape, len(shape) - 2)


def tiles_of(refs):
    found = []
    for ref in refs:
        rows = ref.shape[-2]
        for plane in range(ref.shape[0] if len(ref.shape) == 3 else 1):
            for at in range(0, rows, SUB):
                if len(ref.shape) == 3:
                    found.append((ref, (plane, slice(at, at + SUB), slice(None))))
                else:
                    found.append((ref, (slice(at, at + SUB), slice(None))))
    return found


def three_parts(value):
    high = value.astype(BF16)
    rest = value - high.astype(F32)
    middle = rest.astype(BF16)
    low = (rest - middle.astype(F32)).astype(BF16)
    return high, middle, low


def dot(left, right):
    return jnp.dot(left, right, preferred_element_type=F32)


def rounds(index, count):
    even = [(i + 1) % count if i % 2 == 0 else (i - 1) % count for i in range(count)]
    odd = [(i - 1) % count if i % 2 == 0 else (i + 1) % count for i in range(count)]
    is_even = lax.rem(index, 2) == 0
    up, down = lax.rem(index + 1, count), lax.rem(index + count - 1, count)
    plan = [
        (even, jnp.where(is_even, up, down), jnp.where(is_even, up, down)),
        (odd, jnp.where(is_even, down, up), jnp.where(is_even, down, up)),
    ]
    for k in range(2, count - 1):
        target = [(i + k) % count for i in range(count)]
        plan.append((target, lax.rem(index + k, count), lax.rem(index - k + count, count)))
    return plan


def begin(count, shape, refs):
    fields, cell_in, block_row, block_count = refs[:5], refs[5], refs[6], refs[7]
    planes, own = refs[8:10]
    sends = refs[10 : 10 + count - 1]
    cell, picker, sems = refs[10 + count - 1 :]
    rows, ring = shape
    fetch_cell = pltpu.make_async_copy(cell_in, cell, sems.at[0])
    fetch_cell.start()
    fetches, at = [], 0
    for i, ref in enumerate(fields):
        part = planes.at[at : at + ref.shape[0]]
        fetches.append(pltpu.make_async_copy(ref, part, sems.at[i + 1]))
        fetches[-1].start()
        at += ref.shape[0]

    me = lax.axis_index("tx")
    even = lax.rem(me, 2) == 0
    blocks = block_row.shape[1]
    live = lanes_of((1, blocks)) < block_count[0]
    home = jnp.where(live, block_row[...], -rows)
    line = rows_of((ring, blocks))
    line = jnp.where(line < rows + HALO, line, line - ring)
    targets = [me] + [target for _, target, _ in rounds(me, count)]
    for k, target in enumerate(targets):
        picker[k * ring : (k + 1) * ring, :] = (line == home - target * rows).astype(F32)
    hot = picker[...].astype(BF16)
    fetch_cell.wait()
    high, middle, low = three_parts(cell[...])
    sums = dot(hot, high) + dot(hot, middle) + dot(hot, low)
    own[...] = sums[0:ring]
    for k, send in enumerate(sends):
        send[0:ring, :] = sums[(k + 1) * ring : (k + 2) * ring]

    for fetch in fetches:
        fetch.wait()
    lower = rows_of((SUB, LANES)) < HALO
    for p in range(0, planes.shape[0], 2):
        first = planes[p, 0:SUB, :]
        last = planes[p, rows - SUB : rows, :]
        if p + 1 < planes.shape[0]:
            first = jnp.where(lower, first, pltpu.roll(planes[p + 1, 0:SUB, :], HALO, 0))
            last = jnp.where(lower, pltpu.roll(planes[p + 1, rows - SUB : rows, :], HALO, 0), last)
        at = ring + p // 2 * SUB
        sends[0][at : at + SUB, :] = jnp.where(even, last, first)
        sends[1][at : at + SUB, :] = jnp.where(even, first, last)


def order(count, rows, block_row, block_count, own, chooser):
    me = lax.axis_index("tx")
    blocks = block_row.shape[1]
    live = lanes_of((1, blocks)) < block_count[0]
    home = jnp.where(live, block_row[...], -rows)
    line = rows_of((rows, blocks))
    for k, source in enumerate([me] + [source for _, _, source in rounds(me, count)]):
        hot = (line == home - source * rows).astype(F32)
        chooser[:, k * rows : (k + 1) * rows] = hot.T.astype(BF16)


def columns(count, shape, refs):
    planes, own = refs[:2]
    got = refs[2 : 2 + count - 1]
    base, rims, send_even, send_odd = refs[2 + count - 1 :]
    rows, ring = shape
    tx_even = lax.rem(lax.axis_index("tx"), 2) == 0
    ty_even = lax.rem(lax.axis_index("ty"), 2) == 0
    lower = rows_of((SUB, LANES)) < HALO
    for i in range(0, ring, SUB):
        total = own[i : i + SUB, :]
        for ref in got:
            total = total + ref[i : i + SUB, :]
        base[i : i + SUB, :] = total
    for p in range(0, planes.shape[0], 2):
        at = ring + p // 2 * SUB
        one, two = got[0][at : at + SUB, :], got[1][at : at + SUB, :]
        after = jnp.where(tx_even, one, two)
        before = jnp.where(tx_even, two, one)
        rims[p] = jnp.where(lower, after, before)
        if p + 1 < planes.shape[0]:
            rims[p + 1] = pltpu.roll(jnp.where(lower, before, after), HALO, 0)

    slot = lanes_of((SUB, LANES)) // HALO
    tiles = tiles_of((planes, rims, base))
    for first in range(0, len(tiles), SLOTS):
        left = jnp.zeros((SUB, LANES), F32)
        right = left
        for s, (ref, index) in enumerate(tiles[first : first + SLOTS]):
            turned = pltpu.roll(ref[index], HALO * s, 1) if s else ref[index]
            left = jnp.where(slot == s, turned, left)
            right = jnp.where(slot == (s - 1) % SLOTS, turned, right)
        at = first // SLOTS * SUB
        send_even[at : at + SUB, :] = jnp.where(ty_even, right, left)
        send_odd[at : at + SUB, :] = jnp.where(ty_even, left, right)


def solve(layers, shape, refs):
    planes, rims, middle, even, odd, zed, you, message, ext, base = refs
    rows, ring = shape
    width = 2 * LANES
    tx, ty = lax.axis_index("tx"), lax.axis_index("ty")
    ty_even = lax.rem(ty, 2) == 0

    slot = lanes_of((SUB, LANES)) // HALO
    for j, (ref, index) in enumerate(tiles_of((planes, rims, middle))):
        q, s = divmod(j, SLOTS)
        one, two = even[q * SUB : (q + 1) * SUB, :], odd[q * SUB : (q + 1) * SUB, :]
        both = jnp.where(
            slot == s, jnp.where(ty_even, one, two), jnp.where(ty_even, two, one)
        )
        both = pltpu.roll(both, LANES - HALO * s, 1) if s else both
        if ref is middle:
            base[index[0], 0:LANES] = ref[index]
            base[index[0], LANES:] = both
        else:
            at = slice(rows, ring) if ref is rims else index[1]
            ext[index[0], at, 0:LANES] = ref[index]
            ext[index[0], at, LANES:] = both

    def below(v):
        return pltpu.roll(v, ring - 1, 0)

    def above(v):
        return pltpu.roll(v, 1, 0)

    def right(v):
        return pltpu.roll(v, width - 1, 1)

    def left(v):
        return pltpu.roll(v, 1, 1)

    cx = [ext[p] for p in range(layers)]
    cy = [ext[layers + p] for p in range(layers)]
    via = [ext[2 * layers + p] for p in range(layers - 1)]
    ground = [ext[3 * layers - 1 + p] for p in range(layers)]
    weight = [ext[4 * layers - 1 + p] for p in range(layers)]
    row, lane = rows_of((ring, width)), lanes_of((ring, width))
    inside = (
        ((row < rows) | (row >= rows + HALO) | (tx < lax.axis_size("tx") - 1))
        & ((row < rows + HALO) | (tx > 0))
        & ((lane < LANES) | (lane >= width - HALO) | ((lane < LANES + HALO) & (ty < lax.axis_size("ty") - 1)))
        & ((lane < width - HALO) | (ty > 0))
    )
    cx_low = [jnp.where((row == 0) & (tx == 0), 0.0, above(v)) for v in cx]
    cy_low = [jnp.where((lane == 0) & (ty == 0), 0.0, left(v)) for v in cy]
    diagonal, inverse = [], []
    for p in range(layers):
        total = ground[p] + cx[p] + cx_low[p] + cy[p] + cy_low[p]
        if p + 1 < layers:
            total = total + via[p]
        if p > 0:
            total = total + via[p - 1]
        diagonal.append(total)
        inverse.append(jnp.where(inside, 1.0 / total, 0.0))

    def couple(v, p):
        total = None
        if v[p] is not None:
            total = (
                cx[p] * below(v[p])
                + cx_low[p] * above(v[p])
                + cy[p] * right(v[p])
                + cy_low[p] * left(v[p])
            )
        if p + 1 < layers and v[p + 1] is not None:
            term = via[p] * v[p + 1]
            total = term if total is None else total + term
        if p > 0 and v[p - 1] is not None:
            term = via[p - 1] * v[p - 1]
            total = term if total is None else total + term
        return total

    def smooth(b):
        scaled = [None if b[p] is None else inverse[p] * b[p] for p in range(layers)]
        result = []
        for p in range(layers):
            total = couple(scaled, p)
            if total is None:
                result.append(None)
                continue
            if b[p] is not None:
                total = total + b[p]
            result.append(inverse[p] * total)
        return result

    def tile_sum(left_, right_):
        total = None
        for p in range(layers):
            if left_[p] is None or right_[p] is None:
                continue
            term = left_[p][0:rows, 0:LANES] * right_[p][0:rows, 0:LANES]
            total = term if total is None else total + term
        return jnp.sum(total, axis=0, keepdims=True)

    for which, b in enumerate(([base[...]] + [None] * (layers - 1), weight)):
        z = smooth(b)
        q = []
        for p in range(layers):
            term = couple(z, p)
            q.append(None if z[p] is None and term is None else (-term if z[p] is None else diagonal[p] * z[p] - term))
        u = smooth(q)
        flow = []
        for p in range(layers):
            term = cx[p] * below(u[p]) + cy[p] * right(u[p])
            if p + 1 < layers:
                term = term + via[p] * u[p + 1]
            flow.append(diagonal[p] * u[p] - 2.0 * term)
        at = 2 * rows + 4 * which
        message[at : at + 4, :] = jnp.concatenate(
            [tile_sum(b, z), tile_sum(z, q), tile_sum(q, u), tile_sum(u, flow)], axis=0
        )
        if which == 0:
            for p in range(layers):
                if z[p] is not None:
                    zed[p] = z[p][0:rows, 0:LANES]
                you[p] = u[p][0:rows, 0:LANES]
        else:
            message[0:rows, :] = z[0][0:rows, 0:LANES]
            message[rows : 2 * rows, :] = u[0][0:rows, 0:LANES]


def choose(count, rows, refs):
    chooser = refs[0]
    messages = refs[1 : 1 + count]
    chosen = refs[1 + count]
    hot = chooser[...]
    for half in range(2):
        field = jnp.concatenate([ref[half * rows : (half + 1) * rows, :] for ref in messages], axis=0)
        high, middle, low = three_parts(field)
        chosen[:, half * LANES : (half + 1) * LANES] = dot(hot, high) + dot(hot, middle) + dot(hot, low)


def finish(ways, refs):
    sums = refs[:ways]
    zed, you, chosen, drop, sense = refs[ways:]
    total = sums[0][...]
    for ref in sums[1:]:
        total = total + ref[...]
    total = jnp.broadcast_to(jnp.sum(total, axis=1, keepdims=True), (SUB, LANES))
    for which in range(2):
        bz, zq, qu, uw = (total[4 * which + i : 4 * which + i + 1] for i in range(4))
        ratio = qu / zq
        step = bz / zq
        second = (zq - ratio * bz) / (uw - ratio * qu)
        first = step - second * ratio
        if which == 0:
            for p in range(you.shape[0]):
                part = second * you[p]
                drop[p] = first * zed[p] + part if p < zed.shape[0] else part
        else:
            sense[...] = first * chosen[:, 0:LANES] + second * chosen[:, LANES:]


def vmem():
    return pl.BlockSpec(memory_space=pltpu.VMEM)


def call(kernel, outs, args, scratch=(), specs=None, flops=0, spare=16384):
    size = sum(a.size * a.dtype.itemsize for a in list(args) + list(outs))
    return pl.pallas_call(
        kernel,
        out_shape=tuple(outs),
        in_specs=specs or [vmem() for _ in args],
        out_specs=tuple(vmem() for _ in outs),
        scratch_shapes=scratch,
        cost_estimate=pl.CostEstimate(flops=flops, bytes_accessed=size, transcendentals=0),
        compiler_params=pltpu.CompilerParams(vmem_limit_bytes=(64 * 1024 - spare) * 1024),
    )(*args)


def exchange(values, axis):
    count = lax.axis_size(axis)
    plan = rounds(lax.axis_index(axis), count)
    return [
        lax.ppermute(value, axis, list(enumerate(target)))
        for value, (target, _, _) in zip(values, plan)
    ]


def body(cell_current, block_row, block_count, cond_x, cond_y, cond_via, ground, drop_weight):
    blocks, width = cell_current.shape
    layers, rows, _ = cond_x.shape
    count, ways = lax.axis_size("tx"), lax.axis_size("ty")
    ring = rows + 2 * HALO
    shape = (rows, ring)
    fields = (cond_x, cond_y, cond_via, ground, drop_weight)
    planes = sum(f.shape[0] for f in fields)
    block_row = block_row.reshape(1, blocks)
    smem, hbm = pl.BlockSpec(memory_space=pltpu.SMEM), pl.BlockSpec(memory_space=pltpu.HBM)

    def array(*dims, dtype=F32):
        return jax.ShapeDtypeStruct(dims, dtype)

    edges = (planes + 1) // 2 * SUB
    lengths = [ring + (edges if k < 2 else 0) for k in range(count - 1)]
    held, own, *sends = call(
        lambda *refs: begin(count, shape, refs),
        [array(planes, rows, LANES), array(ring, LANES)] + [array(n, LANES) for n in lengths],
        (
            *(pltpu.with_memory_space_constraint(f, pltpu.HBM) for f in (*fields, cell_current)),
            block_row,
            block_count,
        ),
        scratch=[
            pltpu.VMEM((blocks, LANES), F32),
            pltpu.VMEM((count * ring, blocks), F32),
            pltpu.SemaphoreType.DMA((len(fields) + 1,)),
        ],
        specs=[hbm] * 6 + [vmem(), smem],
    )
    got = exchange(sends, "tx")
    (chooser,) = call(
        functools.partial(order, count, rows),
        (array(blocks, count * rows, dtype=BF16),),
        (block_row, block_count, own),
        specs=[vmem(), smem, vmem()],
    )
    packed = array(pl.cdiv(planes * (rows // SUB + 1) + ring // SUB, SLOTS) * SUB, LANES)
    middle, rims, *sends = call(
        lambda *refs: columns(count, shape, refs),
        (array(ring, LANES), array(planes, SUB, LANES), packed, packed),
        (held, own, *got),
    )
    even, odd = exchange(sends, "ty")
    zed, you, message = call(
        lambda *refs: solve(layers, shape, refs),
        (array(min(2, layers), rows, LANES), array(layers, rows, LANES), array(2 * rows + SUB, LANES)),
        (held, rims, middle, even, odd),
        scratch=[pltpu.VMEM((planes, ring, 2 * LANES), F32), pltpu.VMEM((ring, 2 * LANES), F32)],
    )
    messages = [message] + exchange([message] * (count - 1), "tx")
    total = functools.reduce(jnp.add, [m[2 * rows :] for m in messages])
    totals = [total] + exchange([total] * (ways - 1), "ty")
    (chosen,) = call(
        lambda *refs: choose(count, rows, refs),
        (array(blocks, 2 * LANES),),
        (chooser, *messages),
    )
    return call(
        lambda *refs: finish(ways, refs),
        (array(layers, rows, LANES), array(blocks, width)),
        (*totals, zed, you, chosen),
    )


def solution(mesh):
    placed = (
        P(("grp", "tx"), "ty"),
        P(("grp", "tx")),
        P(("grp", "tx")),
        P(None, ("grp", "tx"), "ty"),
        P(None, ("grp", "tx"), "ty"),
        P(None, ("grp", "tx"), "ty"),
        P(None, ("grp", "tx"), "ty"),
        P(None, ("grp", "tx"), "ty"),
    )
    return jax.shard_map(
        body,
        mesh=mesh,
        in_specs=placed,
        out_specs=(P(None, ("grp", "tx"), "ty"), P(("grp", "tx"), "ty")),
        check_vma=False,
    )
```

time: 39.2 us -> 35.3 us (0.901)
  local copies, waits for them, and re-layouts: 5.51 us -> 0.02 us
  Pallas kernels: 4.42 us -> 5.26 us
  starting transfers between devices: 12.4 us -> 13.1 us
    unnamed x26 -> x2, local copies, waits for them, and re-layouts: 5.51 us -> 0.02 us
    pallas_call x6, Pallas kernels: 4.42 us -> 5.26 us  [call(): pl.pallas_call(kernel, out_shape=tuple(outs), in_specs=specs or [vmem() f...]
    ppermute x11, starting transfers between devices: 12.4 us -> 13.1 us  [exchange(): lax.ppermute(value, axis, list(enumerate(target)))]
where the time goes in v2:
time: 35.3 us; the launch traced here: 35 us
  waiting for transfers between devices  15.4 us (44%)
  starting transfers between devices  13.1 us (37%)
  Pallas kernels  5.26 us (15%)
  between operations  1.34 us (4%)
    ppermute x11, waiting for transfers between devices, exchange(): lax.ppermute(value, axis, list(enumerate(target)))  15.4 us
    ppermute x11, starting transfers between devices, exchange(): lax.ppermute(value, axis, list(enumerate(target)))  13.1 us
    pallas_call x6, Pallas kernels, call(): pl.pallas_call(kernel, out_shape=tuple(outs), in_specs=specs or [vmem() f...  5.26 us
  transfers between devices with their start and end apart: 11, of which 7 were waited for; matrix products, arithmetic and copies ran while one was open for 0% of the time, Pallas kernels for 3%

profile of v2, /device:TPU:0, one launch (start us, length us, event | category | flops | bytes accessed | tf_op | source)
XLA Modules:
  0.0 35.0 jit_solution(17322010712401920402)
XLA Ops:
  0.6 0.0 copy-start
  1.3 0.0 copy-done
  1.3 1.4 %shard_map.95 = (f32[19,64,128]{2,1,0:T(8,128)S(1)}, f32[72,128]{1,0:T(8,128)S(1)}, f32[152,128]{1,0:T(8,128)S(1)}, f32[152,128]{1,0:T(8,128)S(1)}, f32[72,128]{1,0:T(8,128)S(1)}) custom-call(f32[4,64,128]{2,1,0:T(8,128)} %refs_0_.1, f32[4,64,128]{2,1,0:T(8,128)} %refs_1_.1, f32[3,64,128]{2,1,0:T(8,128)} %refs_2_.1, f32[4,64,128]{2,1,0:T(8,128)} %refs_3_.1, ...), custom_call_target="tpu_custom_call" | custom-call | bytes 1738756 | tf_op jit(solution)/shard_map/pallas_call | solution.py:323
  2.8 3.1 %collective-permute-start = (f32[152,128]{1,0:T(8,128)S(1)}, f32[152,128]{1,0:T(8,128)S(1)}, u32[]{:S(2)}, u32[]{:S(2)}) collective-permute-start(f32[152,128]{1,0:T(8,128)S(1)} %get-tuple-element.16), channel_id=1, source_target_pairs={{0,4},{4,0},{8,12},{12,8},{1,5},{5,1},{9,13},{13,9},{2,6},{6,2},{1... | collective-permute-start | bytes 233480 | tf_op jit(solution)/shard_map/ppermute | solution.py:338
  5.9 2.5 %collective-permute-start.1 = (f32[152,128]{1,0:T(8,128)S(1)}, f32[152,128]{1,0:T(8,128)S(1)}, u32[]{:S(2)}, u32[]{:S(2)}) collective-permute-start(f32[152,128]{1,0:T(8,128)S(1)} %get-tuple-element.17), channel_id=1, source_target_pairs={{0,12},{4,8},{8,4},{12,0},{1,13},{5,9},{9,5},{13,1},{2,14},{6,10},... | collective-permute-start | bytes 233480 | tf_op jit(solution)/shard_map/ppermute | solution.py:338
  8.3 0.1 collective-permute-start.2
  8.5 5.5 %collective-permute-done.2.refs_4_ = f32[72,128]{1,0:T(8,128)S(1)} collective-permute-done((f32[72,128]{1,0:T(8,128)S(1)}, f32[72,128]{1,0:T(8,128)S(1)}, u32[]{:S(2)}, u32[]{:S(2)}) %collective-permute-start.2) | collective-permute-done | bytes 36896 | tf_op jit(solution)/shard_map/ppermute | solution.py:338
  14.0 0.0 collective-permute-done.refs_2_
  14.0 0.0 collective-permute-done.1.refs_3_
  14.0 0.3 shard_map.96
  14.2 0.1 collective-permute-start.3
  14.3 1.6 %collective-permute-start.4 = (f32[48,128]{1,0:T(8,128)S(1)}, f32[48,128]{1,0:T(8,128)S(1)}, u32[]{:S(2)}, u32[]{:S(2)}) collective-permute-start(f32[48,128]{1,0:T(8,128)S(1)} %get-tuple-element.22), channel_id=1, source_target_pairs={{0,3},{1,2},{2,1},{3,0},{4,7},{5,6},{6,5},{7,4},{8,11},{9,10},{10,... | collective-permute-start | bytes 73736 | tf_op jit(solution)/shard_map/ppermute | solution.py:338
  15.9 0.0 collective-permute-done.3.refs_3_
  15.9 1.7 %collective-permute-done.4.refs_4_ = f32[48,128]{1,0:T(8,128)S(1)} collective-permute-done((f32[48,128]{1,0:T(8,128)S(1)}, f32[48,128]{1,0:T(8,128)S(1)}, u32[]{:S(2)}, u32[]{:S(2)}) %collective-permute-start.4) | collective-permute-done | bytes 24608 | tf_op jit(solution)/shard_map/ppermute | solution.py:338
  17.6 1.8 %shard_map.97 = (f32[2,64,128]{2,1,0:T(8,128)S(1)}, f32[4,64,128]{2,1,0:T(8,128)S(1)}, f32[136,128]{1,0:T(8,128)S(1)}) custom-call(f32[19,64,128]{2,1,0:T(8,128)S(1)} %get-tuple-element.14.refs_0_, f32[19,8,128]{2,1,0:T(8,128)S(1)} %get-tuple-element.19.refs_1_, f32[72,128]{1,0:T(8,128)S(1)} %get-tuple-element.20.refs_2_, ...), custom_call_target="tpu_custom_call" | custom-call | bytes 1052672 | tf_op jit(solution)/shard_map/pallas_call | solution.py:323
  19.4 0.1 collective-permute-start.5
  19.5 2.6 %collective-permute-start.6 = (f32[136,128]{1,0:T(8,128)S(1)}, f32[136,128]{1,0:T(8,128)S(1)}, u32[]{:S(2)}, u32[]{:S(2)}) collective-permute-start(f32[136,128]{1,0:T(8,128)S(1)} %get-tuple-element.23.refs_1_), channel_id=1, source_target_pairs={{0,12},{4,8},{8,4},{12,0},{1,13},{5,9},{9,5},{13,1},{2,14},{6,10},... | collective-permute-start | bytes 208904 | tf_op jit(solution)/shard_map/ppermute | solution.py:338
  22.1 0.9 %collective-permute-start.7 = (f32[136,128]{1,0:T(8,128)S(1)}, f32[136,128]{1,0:T(8,128)S(1)}, u32[]{:S(2)}, u32[]{:S(2)}) collective-permute-start(f32[136,128]{1,0:T(8,128)S(1)} %get-tuple-element.23.refs_1_), channel_id=1, source_target_pairs={{0,8},{4,12},{8,0},{12,4},{1,9},{5,13},{9,1},{13,5},{2,10},{6,14},... | collective-permute-start | bytes 208904 | tf_op jit(solution)/shard_map/ppermute | solution.py:338
  22.9 1.0 %collective-permute-done.5.refs_2_ = f32[136,128]{1,0:T(8,128)S(1)} collective-permute-done((f32[136,128]{1,0:T(8,128)S(1)}, f32[136,128]{1,0:T(8,128)S(1)}, u32[]{:S(2)}, u32[]{:S(2)}) %collective-permute-start.5) | collective-permute-done | bytes 69664 | tf_op jit(solution)/shard_map/ppermute | solution.py:338
  24.0 2.6 %collective-permute-done.6.refs_3_ = f32[136,128]{1,0:T(8,128)S(1)} collective-permute-done((f32[136,128]{1,0:T(8,128)S(1)}, f32[136,128]{1,0:T(8,128)S(1)}, u32[]{:S(2)}, u32[]{:S(2)}) %collective-permute-start.6) | collective-permute-done | bytes 69664 | tf_op jit(solution)/shard_map/ppermute | solution.py:338
  26.6 3.1 %collective-permute-done.7.refs_4_ = f32[136,128]{1,0:T(8,128)S(1)} collective-permute-done((f32[136,128]{1,0:T(8,128)S(1)}, f32[136,128]{1,0:T(8,128)S(1)}, u32[]{:S(2)}, u32[]{:S(2)}) %collective-permute-start.7) | collective-permute-done | bytes 69664 | tf_op jit(solution)/shard_map/ppermute | solution.py:338
  29.7 1.5 %collective-permute-start.10 = (f32[8,128]{1,0:T(8,128)S(1)}, f32[8,128]{1,0:T(8,128)S(1)}, u32[]{:S(2)}, u32[]{:S(2)}) collective-permute-start(f32[8,128]{1,0:T(8,128)S(1)} %slice_add_fusion.refs_0_), channel_id=1, source_target_pairs={{0,2},{1,3},{2,0},{3,1},{4,6},{5,7},{6,4},{7,5},{8,10},{9,11},{10,... | collective-permute-start | bytes 12296 | tf_op jit(solution)/shard_map/ppermute | solution.py:338
  31.2 0.0 collective-permute-start.8
  31.2 0.6 %collective-permute-start.9 = (f32[8,128]{1,0:T(8,128)S(1)}, f32[8,128]{1,0:T(8,128)S(1)}, u32[]{:S(2)}, u32[]{:S(2)}) collective-permute-start(f32[8,128]{1,0:T(8,128)S(1)} %slice_add_fusion.refs_0_), channel_id=1, source_target_pairs={{0,3},{1,2},{2,1},{3,0},{4,7},{5,6},{6,5},{7,4},{8,11},{9,10},{10,... | collective-permute-start | bytes 12296 | tf_op jit(solution)/shard_map/ppermute | solution.py:338
  31.8 0.4 %shard_map.98.refs_0_ = bf16[512,256]{1,0:T(8,128)(2,1)S(1)} custom-call(s32[1,512]{1,0:T(1,128)S(1)} %bitcast.2, s32[1]{0:T(128)S(6)} %copy.10.refs_7_.block_count, f32[72,128]{1,0:T(8,128)S(1)} %get-tuple-element.15.refs_1_.own), custom_call_target="tpu_custom_call" | custom-call | bytes 301060 | tf_op jit(solution)/shard_map/pallas_call | solution.py:323
  32.2 0.6 %shard_map.99.refs_6_ = f32[512,256]{1,0:T(8,128)S(1)} custom-call(bf16[512,256]{1,0:T(8,128)(2,1)S(1)} %shard_map.98.refs_0_, f32[136,128]{1,0:T(8,128)S(1)} %get-tuple-element.23.refs_1_, f32[136,128]{1,0:T(8,128)S(1)} %collective-permute-done.5.refs_2_, f32[136,128]{1,0:T(8,128)S(1)} %collective-permute-done.6.refs_3_, ...), custom_call_target="tpu_custom_call" | custom-call | bytes 1064960 | tf_op jit(solution)/shard_map/pallas_call | solution.py:323
  32.7 0.5 %collective-permute-done.10.refs_3_ = f32[8,128]{1,0:T(8,128)S(1)} collective-permute-done((f32[8,128]{1,0:T(8,128)S(1)}, f32[8,128]{1,0:T(8,128)S(1)}, u32[]{:S(2)}, u32[]{:S(2)}) %collective-permute-start.10) | collective-permute-done | bytes 4128 | tf_op jit(solution)/shard_map/ppermute | solution.py:338
  33.3 0.0 collective-permute-done.8.refs_1_
  33.3 0.9 %collective-permute-done.9.refs_2_ = f32[8,128]{1,0:T(8,128)S(1)} collective-permute-done((f32[8,128]{1,0:T(8,128)S(1)}, f32[8,128]{1,0:T(8,128)S(1)}, u32[]{:S(2)}, u32[]{:S(2)}) %collective-permute-start.9) | collective-permute-done | bytes 4128 | tf_op jit(solution)/shard_map/ppermute | solution.py:338
  34.2 0.9 %shard_map.100 = (f32[4,64,128]{2,1,0:T(8,128)}, f32[512,128]{1,0:T(8,128)}) custom-call(f32[8,128]{1,0:T(8,128)S(1)} %slice_add_fusion.refs_0_, f32[8,128]{1,0:T(8,128)S(1)} %collective-permute-done.8.refs_1_, f32[8,128]{1,0:T(8,128)S(1)} %collective-permute-done.9.refs_2_, f32[8,128]{1,0:T(8,128)S(1)} %collective-permute-done.10.refs_3_, ...), custom_call_target="tpu_custom_call" | custom-call | bytes 1130496 | tf_op jit(solution)/shard_map/pallas_call | solution.py:323
  (1 shorter events, 0.0 us)
Async XLA Ops:
  0.6 0.7 %copy-start = (s32[512]{0:T(512)S(1)}, s32[512]{0:T(512)}, u32[]{:S(2)}) copy-start(s32[512]{0:T(512)} %param.9) | copy-start | bytes 6148
  2.8 11.2 %collective-permute-start = (f32[152,128]{1,0:T(8,128)S(1)}, f32[152,128]{1,0:T(8,128)S(1)}, u32[]{:S(2)}, u32[]{:S(2)}) collective-permute-start(f32[152,128]{1,0:T(8,128)S(1)} %get-tuple-element.16), channel_id=1, source_target_pairs={{0,4},{4,0},{8,12},{12,8},{1,5},{5,1},{9,13},{13,9},{2,6},{6,2},{1... | collective-permute-start | bytes 233480 | tf_op jit(solution)/shard_map/ppermute | solution.py:338
  5.9 8.1 %collective-permute-start.1 = (f32[152,128]{1,0:T(8,128)S(1)}, f32[152,128]{1,0:T(8,128)S(1)}, u32[]{:S(2)}, u32[]{:S(2)}) collective-permute-start(f32[152,128]{1,0:T(8,128)S(1)} %get-tuple-element.17), channel_id=1, source_target_pairs={{0,12},{4,8},{8,4},{12,0},{1,13},{5,9},{9,5},{13,1},{2,14},{6,10},... | collective-permute-start | bytes 233480 | tf_op jit(solution)/shard_map/ppermute | solution.py:338
  8.3 5.6 %collective-permute-start.2 = (f32[72,128]{1,0:T(8,128)S(1)}, f32[72,128]{1,0:T(8,128)S(1)}, u32[]{:S(2)}, u32[]{:S(2)}) collective-permute-start(f32[72,128]{1,0:T(8,128)S(1)} %get-tuple-element.18), channel_id=1, source_target_pairs={{0,8},{4,12},{8,0},{12,4},{1,9},{5,13},{9,1},{13,5},{2,10},{6,14},... | collective-permute-start | bytes 110600 | tf_op jit(solution)/shard_map/ppermute | solution.py:338
  14.2 1.7 %collective-permute-start.3 = (f32[48,128]{1,0:T(8,128)S(1)}, f32[48,128]{1,0:T(8,128)S(1)}, u32[]{:S(2)}, u32[]{:S(2)}) collective-permute-start(f32[48,128]{1,0:T(8,128)S(1)} %get-tuple-element.21), channel_id=1, source_target_pairs={{0,1},{1,0},{2,3},{3,2},{4,5},{5,4},{6,7},{7,6},{8,9},{9,8},{10,11... | collective-permute-start | bytes 73736 | tf_op jit(solution)/shard_map/ppermute | solution.py:338
  14.3 3.3 %collective-permute-start.4 = (f32[48,128]{1,0:T(8,128)S(1)}, f32[48,128]{1,0:T(8,128)S(1)}, u32[]{:S(2)}, u32[]{:S(2)}) collective-permute-start(f32[48,128]{1,0:T(8,128)S(1)} %get-tuple-element.22), channel_id=1, source_target_pairs={{0,3},{1,2},{2,1},{3,0},{4,7},{5,6},{6,5},{7,4},{8,11},{9,10},{10,... | collective-permute-start | bytes 73736 | tf_op jit(solution)/shard_map/ppermute | solution.py:338
  19.4 4.6 %collective-permute-start.5 = (f32[136,128]{1,0:T(8,128)S(1)}, f32[136,128]{1,0:T(8,128)S(1)}, u32[]{:S(2)}, u32[]{:S(2)}) collective-permute-start(f32[136,128]{1,0:T(8,128)S(1)} %get-tuple-element.23.refs_1_), channel_id=1, source_target_pairs={{0,4},{4,0},{8,12},{12,8},{1,5},{5,1},{9,13},{13,9},{2,6},{6,2},{1... | collective-permute-start | bytes 208904 | tf_op jit(solution)/shard_map/ppermute | solution.py:338
  19.5 7.1 %collective-permute-start.6 = (f32[136,128]{1,0:T(8,128)S(1)}, f32[136,128]{1,0:T(8,128)S(1)}, u32[]{:S(2)}, u32[]{:S(2)}) collective-permute-start(f32[136,128]{1,0:T(8,128)S(1)} %get-tuple-element.23.refs_1_), channel_id=1, source_target_pairs={{0,12},{4,8},{8,4},{12,0},{1,13},{5,9},{9,5},{13,1},{2,14},{6,10},... | collective-permute-start | bytes 208904 | tf_op jit(solution)/shard_map/ppermute | solution.py:338
  22.1 7.6 %collective-permute-start.7 = (f32[136,128]{1,0:T(8,128)S(1)}, f32[136,128]{1,0:T(8,128)S(1)}, u32[]{:S(2)}, u32[]{:S(2)}) collective-permute-start(f32[136,128]{1,0:T(8,128)S(1)} %get-tuple-element.23.refs_1_), channel_id=1, source_target_pairs={{0,8},{4,12},{8,0},{12,4},{1,9},{5,13},{9,1},{13,5},{2,10},{6,14},... | collective-permute-start | bytes 208904 | tf_op jit(solution)/shard_map/ppermute | solution.py:338
  29.7 3.6 %collective-permute-start.10 = (f32[8,128]{1,0:T(8,128)S(1)}, f32[8,128]{1,0:T(8,128)S(1)}, u32[]{:S(2)}, u32[]{:S(2)}) collective-permute-start(f32[8,128]{1,0:T(8,128)S(1)} %slice_add_fusion.refs_0_), channel_id=1, source_target_pairs={{0,2},{1,3},{2,0},{3,1},{4,6},{5,7},{6,4},{7,5},{8,10},{9,11},{10,... | collective-permute-start | bytes 12296 | tf_op jit(solution)/shard_map/ppermute | solution.py:338
  31.2 2.1 %collective-permute-start.8 = (f32[8,128]{1,0:T(8,128)S(1)}, f32[8,128]{1,0:T(8,128)S(1)}, u32[]{:S(2)}, u32[]{:S(2)}) collective-permute-start(f32[8,128]{1,0:T(8,128)S(1)} %slice_add_fusion.refs_0_), channel_id=1, source_target_pairs={{0,1},{1,0},{2,3},{3,2},{4,5},{5,4},{6,7},{7,6},{8,9},{9,8},{10,11... | collective-permute-start | bytes 12296 | tf_op jit(solution)/shard_map/ppermute | solution.py:338
  31.2 3.0 %collective-permute-start.9 = (f32[8,128]{1,0:T(8,128)S(1)}, f32[8,128]{1,0:T(8,128)S(1)}, u32[]{:S(2)}, u32[]{:S(2)}) collective-permute-start(f32[8,128]{1,0:T(8,128)S(1)} %slice_add_fusion.refs_0_), channel_id=1, source_target_pairs={{0,3},{1,2},{2,1},{3,0},{4,7},{5,6},{6,5},{7,4},{8,11},{9,10},{10,... | collective-permute-start | bytes 12296 | tf_op jit(solution)/shard_map/ppermute | solution.py:338

commit v3 on v2

--- a/solution.py
+++ b/solution.py
@@ -13,6 +13,8 @@
 SLOTS = LANES // HALO
 F32 = jnp.float32
 BF16 = jnp.bfloat16
+ROW_TURNS = (1, 0, 2)
+DATA_TURNS = (2, 0, 1)
 
 
 def lanes_of(shape):
@@ -46,6 +48,13 @@
 
 def dot(left, right):
     return jnp.dot(left, right, preferred_element_type=F32)
+
+
+def in_turn(values, turns, back=False):
+    turns = turns + tuple(range(len(turns), len(values)))
+    if back:
+        turns = tuple(turns.index(k) for k in range(len(values)))
+    return [values[k] for k in turns]
 
 
 def rounds(index, count):
@@ -64,11 +73,13 @@
 
 
 def begin(count, shape, refs):
-    fields, cell_in, block_row, block_count = refs[:5], refs[5], refs[6], refs[7]
-    planes, own = refs[8:10]
-    sends = refs[10 : 10 + count - 1]
-    cell, picker, sems = refs[10 + count - 1 :]
+    fields, cell_in, row_in, block_count = refs[:5], refs[5], refs[6], refs[7]
+    planes, own, home = refs[8:11]
+    sends = refs[11 : 11 + count - 1]
+    cell, picker, block_row, sems = refs[11 + count - 1 :]
     rows, ring = shape
+    fetch_row = pltpu.make_async_copy(row_in, block_row, sems.at[6])
+    fetch_row.start()
     fetch_cell = pltpu.make_async_copy(cell_in, cell, sems.at[0])
     fetch_cell.start()
     fetches, at = [], 0
@@ -81,13 +92,15 @@
     me = lax.axis_index("tx")
     even = lax.rem(me, 2) == 0
     blocks = block_row.shape[1]
-    live = lanes_of((1, blocks)) < block_count[0]
-    home = jnp.where(live, block_row[...], -rows)
     line = rows_of((ring, blocks))
     line = jnp.where(line < rows + HALO, line, line - ring)
+    fetch_row.wait()
+    live = lanes_of((1, blocks)) < block_count[0]
+    land = jnp.where(live, block_row[...], -rows)
+    home[...] = land
     targets = [me] + [target for _, target, _ in rounds(me, count)]
     for k, target in enumerate(targets):
-        picker[k * ring : (k + 1) * ring, :] = (line == home - target * rows).astype(F32)
+        picker[k * ring : (k + 1) * ring, :] = (line == land - target * rows).astype(F32)
     hot = picker[...].astype(BF16)
     fetch_cell.wait()
     high, middle, low = three_parts(cell[...])
@@ -110,20 +123,18 @@
         sends[1][at : at + SUB, :] = jnp.where(even, first, last)
 
 
-def order(count, rows, block_row, block_count, own, chooser):
+def order(count, rows, home, chooser):
     me = lax.axis_index("tx")
-    blocks = block_row.shape[1]
-    live = lanes_of((1, blocks)) < block_count[0]
-    home = jnp.where(live, block_row[...], -rows)
+    blocks = home.shape[1]
     line = rows_of((rows, blocks))
-    for k, source in enumerate([me] + [source for _, _, source in rounds(me, count)]):
-        hot = (line == home - source * rows).astype(F32)
+    for k, source in enumerate(in_turn([source for _, _, source in rounds(me, count)], DATA_TURNS) + [me]):
+        hot = (line == home[...] - source * rows).astype(F32)
         chooser[:, k * rows : (k + 1) * rows] = hot.T.astype(BF16)
 
 
 def columns(count, shape, refs):
     planes, own = refs[:2]
-    got = refs[2 : 2 + count - 1]
+    got = in_turn(refs[2 : 2 + count - 1], ROW_TURNS, True)
     base, rims, send_even, send_odd = refs[2 + count - 1 :]
     rows, ring = shape
     tx_even = lax.rem(lax.axis_index("tx"), 2) == 0
@@ -157,46 +168,119 @@
         send_odd[at : at + SUB, :] = jnp.where(ty_even, left, right)
 
 
-def solve(layers, shape, refs):
-    planes, rims, middle, even, odd, zed, you, message, ext, base = refs
+class Grid:
+    def __init__(self, ref, layers, rows):
+        self.layers, self.rows = layers, rows
+        self.ring, self.width = ref.shape[1:]
+        names = ("cx", "cy", "via", "cx_low", "cy_low", "diagonal", "inverse", "weight")
+        at = 0
+        for name in names:
+            depth = layers - 1 if name == "via" else layers
+            setattr(self, name, [ref.at[at + p] for p in range(depth)])
+            at += depth
+        self.planes = at
+
+    def below(self, v):
+        return pltpu.roll(v, self.ring - 1, 0)
+
+    def above(self, v):
+        return pltpu.roll(v, 1, 0)
+
+    def right(self, v):
+        return pltpu.roll(v, self.width - 1, 1)
+
+    def left(self, v):
+        return pltpu.roll(v, 1, 1)
+
+    def couple(self, v, p):
+        total = None
+        if v[p] is not None:
+            total = (
+                self.cx[p][...] * self.below(v[p])
+                + self.cx_low[p][...] * self.above(v[p])
+                + self.cy[p][...] * self.right(v[p])
+                + self.cy_low[p][...] * self.left(v[p])
+            )
+        if p + 1 < self.layers and v[p + 1] is not None:
+            term = self.via[p][...] * v[p + 1]
+            total = term if total is None else total + term
+        if p > 0 and v[p - 1] is not None:
+            term = self.via[p - 1][...] * v[p - 1]
+            total = term if total is None else total + term
+        return total
+
+    def smooth(self, b):
+        scaled = [None if v is None else self.inverse[p][...] * v for p, v in enumerate(b)]
+        result = []
+        for p in range(self.layers):
+            total = self.couple(scaled, p)
+            if total is not None:
+                if b[p] is not None:
+                    total = total + b[p]
+                total = self.inverse[p][...] * total
+            result.append(total)
+        return result
+
+    def apply(self, z):
+        result = []
+        for p in range(self.layers):
+            term = self.couple(z, p)
+            if z[p] is not None:
+                term = self.diagonal[p][...] * z[p] - term
+            elif term is not None:
+                term = -term
+            result.append(term)
+        return result
+
+    def flow(self, u):
+        result = []
+        for p in range(self.layers):
+            term = self.cx[p][...] * self.below(u[p]) + self.cy[p][...] * self.right(u[p])
+            if p + 1 < self.layers:
+                term = term + self.via[p][...] * u[p + 1]
+            result.append(self.diagonal[p][...] * u[p] - 2.0 * term)
+        return result
+
+    def products(self, b, z, q, u):
+        flow = self.flow(u)
+        found = []
+        for one, two in ((b, z), (z, q), (q, u), (u, flow)):
+            total = None
+            for left, right in zip(one, two):
+                if left is None or right is None:
+                    continue
+                term = left[0 : self.rows, 0:LANES] * right[0 : self.rows, 0:LANES]
+                total = term if total is None else total + term
+            found.append(jnp.sum(total, axis=0, keepdims=True))
+        return found
+
+
+def adjoint(layers, shape, refs):
+    planes, rims, middle, even, odd, message, grid, base, fields, ground = refs
     rows, ring = shape
     width = 2 * LANES
     tx, ty = lax.axis_index("tx"), lax.axis_index("ty")
     ty_even = lax.rem(ty, 2) == 0
+    op = Grid(grid, layers, rows)
+    targets = [*op.cx, *op.cy, *op.via, *(ground.at[p] for p in range(layers)), *op.weight]
 
     slot = lanes_of((SUB, LANES)) // HALO
-    for j, (ref, index) in enumerate(tiles_of((planes, rims, middle))):
-        q, s = divmod(j, SLOTS)
-        one, two = even[q * SUB : (q + 1) * SUB, :], odd[q * SUB : (q + 1) * SUB, :]
-        both = jnp.where(
-            slot == s, jnp.where(ty_even, one, two), jnp.where(ty_even, two, one)
-        )
-        both = pltpu.roll(both, LANES - HALO * s, 1) if s else both
-        if ref is middle:
-            base[index[0], 0:LANES] = ref[index]
-            base[index[0], LANES:] = both
-        else:
-            at = slice(rows, ring) if ref is rims else index[1]
-            ext[index[0], at, 0:LANES] = ref[index]
-            ext[index[0], at, LANES:] = both
-
-    def below(v):
-        return pltpu.roll(v, ring - 1, 0)
-
-    def above(v):
-        return pltpu.roll(v, 1, 0)
-
-    def right(v):
-        return pltpu.roll(v, width - 1, 1)
-
-    def left(v):
-        return pltpu.roll(v, 1, 1)
-
-    cx = [ext[p] for p in range(layers)]
-    cy = [ext[layers + p] for p in range(layers)]
-    via = [ext[2 * layers + p] for p in range(layers - 1)]
-    ground = [ext[3 * layers - 1 + p] for p in range(layers)]
-    weight = [ext[4 * layers - 1 + p] for p in range(layers)]
+    tiles = tiles_of((planes, rims, middle))
+    for first in range(0, len(tiles), SLOTS):
+        q = first // SLOTS * SUB
+        one, two = even[q : q + SUB, :], odd[q : q + SUB, :]
+        after, before = jnp.where(ty_even, one, two), jnp.where(ty_even, two, one)
+        for s, (ref, index) in enumerate(tiles[first : first + SLOTS]):
+            both = jnp.where(slot == s, after, before)
+            both = pltpu.roll(both, LANES - HALO * s, 1) if s else both
+            if ref is middle:
+                base[index[0], 0:LANES] = ref[index]
+                base[index[0], LANES:] = both
+            else:
+                at = slice(rows, ring) if ref is rims else index[1]
+                targets[index[0]][at, 0:LANES] = ref[index]
+                targets[index[0]][at, LANES:] = both
+
     row, lane = rows_of((ring, width)), lanes_of((ring, width))
     inside = (
         ((row < rows) | (row >= rows + HALO) | (tx < lax.axis_size("tx") - 1))
@@ -204,82 +288,46 @@
         & ((lane < LANES) | (lane >= width - HALO) | ((lane < LANES + HALO) & (ty < lax.axis_size("ty") - 1)))
         & ((lane < width - HALO) | (ty > 0))
     )
-    cx_low = [jnp.where((row == 0) & (tx == 0), 0.0, above(v)) for v in cx]
-    cy_low = [jnp.where((lane == 0) & (ty == 0), 0.0, left(v)) for v in cy]
-    diagonal, inverse = [], []
     for p in range(layers):
-        total = ground[p] + cx[p] + cx_low[p] + cy[p] + cy_low[p]
+        cx, cy = op.cx[p][...], op.cy[p][...]
+        cx_low = jnp.where((row == 0) & (tx == 0), 0.0, op.above(cx))
+        cy_low = jnp.where((lane == 0) & (ty == 0), 0.0, op.left(cy))
+        total = ground[p] + cx + cx_low + cy + cy_low
         if p + 1 < layers:
-            total = total + via[p]
+            total = total + op.via[p][...]
         if p > 0:
-            total = total + via[p - 1]
-        diagonal.append(total)
-        inverse.append(jnp.where(inside, 1.0 / total, 0.0))
-
-    def couple(v, p):
-        total = None
-        if v[p] is not None:
-            total = (
-                cx[p] * below(v[p])
-                + cx_low[p] * above(v[p])
-                + cy[p] * right(v[p])
-                + cy_low[p] * left(v[p])
-            )
-        if p + 1 < layers and v[p + 1] is not None:
-            term = via[p] * v[p + 1]
-            total = term if total is None else total + term
-        if p > 0 and v[p - 1] is not None:
-            term = via[p - 1] * v[p - 1]
-            total = term if total is None else total + term
-        return total
-
-    def smooth(b):
-        scaled = [None if b[p] is None else inverse[p] * b[p] for p in range(layers)]
-        result = []
+            total = total + op.via[p - 1][...]
+        op.cx_low[p][...] = cx_low
+        op.cy_low[p][...] = cy_low
+        op.diagonal[p][...] = total
+        op.inverse[p][...] = jnp.where(inside, 1.0 / total, 0.0)
+
+    z = op.smooth([ref[...] for ref in op.weight])
+    q = op.apply(z)
+    u = op.smooth(q)
+    message[0:rows, :] = z[0][0:rows, 0:LANES]
+    message[rows : 2 * rows, :] = u[0][0:rows, 0:LANES]
+    for k, field in enumerate((z, q, u)):
         for p in range(layers):
-            total = couple(scaled, p)
-            if total is None:
-                result.append(None)
-                continue
-            if b[p] is not None:
-                total = total + b[p]
-            result.append(inverse[p] * total)
-        return result
-
-    def tile_sum(left_, right_):
-        total = None
-        for p in range(layers):
-            if left_[p] is None or right_[p] is None:
-                continue
-            term = left_[p][0:rows, 0:LANES] * right_[p][0:rows, 0:LANES]
-            total = term if total is None else total + term
-        return jnp.sum(total, axis=0, keepdims=True)
-
-    for which, b in enumerate(([base[...]] + [None] * (layers - 1), weight)):
-        z = smooth(b)
-        q = []
-        for p in range(layers):
-            term = couple(z, p)
-            q.append(None if z[p] is None and term is None else (-term if z[p] is None else diagonal[p] * z[p] - term))
-        u = smooth(q)
-        flow = []
-        for p in range(layers):
-            term = cx[p] * below(u[p]) + cy[p] * right(u[p])
-            if p + 1 < layers:
-                term = term + via[p] * u[p + 1]
-            flow.append(diagonal[p] * u[p] - 2.0 * term)
-        at = 2 * rows + 4 * which
-        message[at : at + 4, :] = jnp.concatenate(
-            [tile_sum(b, z), tile_sum(z, q), tile_sum(q, u), tile_sum(u, flow)], axis=0
-        )
-        if which == 0:
-            for p in range(layers):
-                if z[p] is not None:
-                    zed[p] = z[p][0:rows, 0:LANES]
-                you[p] = u[p][0:rows, 0:LANES]
-        else:
-            message[0:rows, :] = z[0][0:rows, 0:LANES]
-            message[rows : 2 * rows, :] = u[0][0:rows, 0:LANES]
+            fields[k * layers + p] = field[p]
+
+
+def forward(layers, shape, refs):
+    grid, base, fields, zed, you, scalars = refs
+    rows, ring = shape
+    op = Grid(grid, layers, rows)
+    b = [base[...]] + [None] * (layers - 1)
+    z = op.smooth(b)
+    q = op.apply(z)
+    u = op.smooth(q)
+    for p in range(layers):
+        if z[p] is not None:
+            zed[p] = z[p][0:rows, 0:LANES]
+        you[p] = u[p][0:rows, 0:LANES]
+    found = op.products(b, z, q, u)
+    z, q, u = ([fields[k * layers + p] for p in range(layers)] for k in range(3))
+    found += op.products([ref[...] for ref in op.weight], z, q, u)
+    scalars[...] = jnp.concatenate(found, axis=0)
 
 
 def choose(count, rows, refs):
@@ -332,8 +380,7 @@
 
 
 def exchange(values, axis):
-    count = lax.axis_size(axis)
-    plan = rounds(lax.axis_index(axis), count)
+    plan = rounds(lax.axis_index(axis), lax.axis_size(axis))
     return [
         lax.ppermute(value, axis, list(enumerate(target)))
         for value, (target, _, _) in zip(values, plan)
@@ -349,50 +396,64 @@
     fields = (cond_x, cond_y, cond_via, ground, drop_weight)
     planes = sum(f.shape[0] for f in fields)
     block_row = block_row.reshape(1, blocks)
-    smem, hbm = pl.BlockSpec(memory_space=pltpu.SMEM), pl.BlockSpec(memory_space=pltpu.HBM)
+    hbm = pl.BlockSpec(memory_space=pltpu.HBM)
 
     def array(*dims, dtype=F32):
         return jax.ShapeDtypeStruct(dims, dtype)
 
     edges = (planes + 1) // 2 * SUB
     lengths = [ring + (edges if k < 2 else 0) for k in range(count - 1)]
-    held, own, *sends = call(
+    held, own, home, *sends = call(
         lambda *refs: begin(count, shape, refs),
-        [array(planes, rows, LANES), array(ring, LANES)] + [array(n, LANES) for n in lengths],
+        [array(planes, rows, LANES), array(ring, LANES), array(1, blocks, dtype=jnp.int32)]
+        + [array(n, LANES) for n in lengths],
         (
-            *(pltpu.with_memory_space_constraint(f, pltpu.HBM) for f in (*fields, cell_current)),
-            block_row,
+            *(
+                pltpu.with_memory_space_constraint(f, pltpu.HBM)
+                for f in (*fields, cell_current, block_row)
+            ),
             block_count,
         ),
         scratch=[
             pltpu.VMEM((blocks, LANES), F32),
             pltpu.VMEM((count * ring, blocks), F32),
-            pltpu.SemaphoreType.DMA((len(fields) + 1,)),
+            pltpu.VMEM((1, blocks), jnp.int32),
+            pltpu.SemaphoreType.DMA((len(fields) + 2,)),
         ],
-        specs=[hbm] * 6 + [vmem(), smem],
+        specs=[hbm] * 7 + [pl.BlockSpec(memory_space=pltpu.SMEM)],
     )
     got = exchange(sends, "tx")
     (chooser,) = call(
         functools.partial(order, count, rows),
         (array(blocks, count * rows, dtype=BF16),),
-        (block_row, block_count, own),
-        specs=[vmem(), smem, vmem()],
+        (home,),
     )
     packed = array(pl.cdiv(planes * (rows // SUB + 1) + ring // SUB, SLOTS) * SUB, LANES)
     middle, rims, *sends = call(
         lambda *refs: columns(count, shape, refs),
         (array(ring, LANES), array(planes, SUB, LANES), packed, packed),
-        (held, own, *got),
+        (held, own, *in_turn(got, ROW_TURNS)),
     )
     even, odd = exchange(sends, "ty")
-    zed, you, message = call(
-        lambda *refs: solve(layers, shape, refs),
-        (array(min(2, layers), rows, LANES), array(layers, rows, LANES), array(2 * rows + SUB, LANES)),
+    width2 = 2 * LANES
+    message, *state = call(
+        lambda *refs: adjoint(layers, shape, refs),
+        (
+            array(2 * rows, LANES),
+            array(8 * layers - 1, ring, width2),
+            array(ring, width2),
+            array(3 * layers, ring, width2),
+        ),
         (held, rims, middle, even, odd),
-        scratch=[pltpu.VMEM((planes, ring, 2 * LANES), F32), pltpu.VMEM((ring, 2 * LANES), F32)],
-    )
-    messages = [message] + exchange([message] * (count - 1), "tx")
-    total = functools.reduce(jnp.add, [m[2 * rows :] for m in messages])
+        scratch=[pltpu.VMEM((layers, ring, width2), F32)],
+    )
+    messages = in_turn(exchange([message] * (count - 1), "tx"), DATA_TURNS) + [message]
+    zed, you, total = call(
+        lambda *refs: forward(layers, shape, refs),
+        (array(min(2, layers), rows, LANES), array(layers, rows, LANES), array(SUB, LANES)),
+        state,
+    )
+    total = functools.reduce(jnp.add, [total] + exchange([total] * (count - 1), "tx"))
     totals = [total] + exchange([total] * (ways - 1), "ty")
     (chosen,) = call(
         lambda *refs: choose(count, rows, refs),

time: 35.3 us -> 33.3 us (0.943)
  waiting for transfers between devices: 15.4 us -> 7.31 us
  starting transfers between devices: 13.1 us -> 19.2 us
    ppermute x11 -> x14, waiting for transfers between devices: 15.4 us -> 7.31 us  [exchange(): lax.ppermute(value, axis, list(enumerate(target)))]
    ppermute x11 -> x14, starting transfers between devices: 13.1 us -> 19.2 us  [exchange(): lax.ppermute(value, axis, list(enumerate(target)))]
    pallas_call x6 -> x7, Pallas kernels: 5.26 us -> 5.19 us  [call(): pl.pallas_call(kernel, out_shape=tuple(outs), in_specs=specs or [vmem() f...]
  transfers between devices with their start and end apart: 11 -> 14, of which waited for: 7 -> 4; matrix products, arithmetic and copies ran while one was open for 0% -> 0% of each run, Pallas kernels for 3% -> 3%
where the time goes in v3:
time: 33.3 us; the launch traced here: 33.1 us
  starting transfers between devices  19.2 us (58%)
  waiting for transfers between devices  7.31 us (22%)
  Pallas kernels  5.19 us (16%)
  between operations  1.36 us (4%)
    ppermute x14, starting transfers between devices, exchange(): lax.ppermute(value, axis, list(enumerate(target)))  19.2 us
    ppermute x14, waiting for transfers between devices, exchange(): lax.ppermute(value, axis, list(enumerate(target)))  7.31 us
    pallas_call x7, Pallas kernels, call(): pl.pallas_call(kernel, out_shape=tuple(outs), in_specs=specs or [vmem() f...  5.19 us
  transfers between devices with their start and end apart: 14, of which 4 were waited for; matrix products, arithmetic and copies ran while one was open for 0% of the time, Pallas kernels for 3%

profile of v3, /device:TPU:0, one launch (start us, length us, event | category | flops | bytes accessed | tf_op | source)
XLA Modules:
  0.0 33.1 jit_solution(2086903674724273363)
XLA Ops:
  1.3 1.5 %shard_map.95 = (f32[19,64,128]{2,1,0:T(8,128)S(1)}, f32[72,128]{1,0:T(8,128)S(1)}, s32[1,512]{1,0:T(1,128)S(1)}, f32[152,128]{1,0:T(8,128)S(1)}, f32[152,128]{1,0:T(8,128)S(1)}, /*index=5*/f32[72,128]{1,0:T(8,128)S(1)}) custom-call(f32[4,64,128]{2,1,0:T(8,128)} %refs_0_.1, f32[4,64,128]{2,1,0:T(8,128)} %refs_1_.1, f32[3,64,128]{2,1,0:T(8,128)} %refs_2_.1, ...), custom_call_target="tpu_custom_call" | custom-call | bytes 1740804 | tf_op jit(solution)/shard_map/pallas_call | solution.py:371
  2.8 5.1 %collective-permute-start = (f32[152,128]{1,0:T(8,128)S(1)}, f32[152,128]{1,0:T(8,128)S(1)}, u32[]{:S(2)}, u32[]{:S(2)}) collective-permute-start(f32[152,128]{1,0:T(8,128)S(1)} %get-tuple-element.21), channel_id=1, source_target_pairs={{0,12},{4,8},{8,4},{12,0},{1,13},{5,9},{9,5},{13,1},{2,14},{6,10},... | collective-permute-start | bytes 233480 | tf_op jit(solution)/shard_map/ppermute | solution.py:385
  7.9 0.0 collective-permute-start.1
  7.9 0.6 %collective-permute-start.2 = (f32[72,128]{1,0:T(8,128)S(1)}, f32[72,128]{1,0:T(8,128)S(1)}, u32[]{:S(2)}, u32[]{:S(2)}) collective-permute-start(f32[72,128]{1,0:T(8,128)S(1)} %get-tuple-element.23), channel_id=1, source_target_pairs={{0,8},{4,12},{8,0},{12,4},{1,9},{5,13},{9,1},{13,5},{2,10},{6,14},... | collective-permute-start | bytes 110600 | tf_op jit(solution)/shard_map/ppermute | solution.py:385
  8.5 4.5 %collective-permute-done.2.refs_4_ = f32[72,128]{1,0:T(8,128)S(1)} collective-permute-done((f32[72,128]{1,0:T(8,128)S(1)}, f32[72,128]{1,0:T(8,128)S(1)}, u32[]{:S(2)}, u32[]{:S(2)}) %collective-permute-start.2) | collective-permute-done | bytes 36896 | tf_op jit(solution)/shard_map/ppermute | solution.py:385
  13.0 0.0 collective-permute-done.refs_2_
  13.0 0.0 collective-permute-done.1.refs_3_
  13.0 0.3 shard_map.96
  13.2 0.1 collective-permute-start.3
  13.3 1.7 %collective-permute-start.4 = (f32[48,128]{1,0:T(8,128)S(1)}, f32[48,128]{1,0:T(8,128)S(1)}, u32[]{:S(2)}, u32[]{:S(2)}) collective-permute-start(f32[48,128]{1,0:T(8,128)S(1)} %get-tuple-element.27), channel_id=1, source_target_pairs={{0,3},{1,2},{2,1},{3,0},{4,7},{5,6},{6,5},{7,4},{8,11},{9,10},{10,... | collective-permute-start | bytes 73736 | tf_op jit(solution)/shard_map/ppermute | solution.py:385
  15.1 0.0 collective-permute-done.3.refs_3_
  15.1 1.6 %collective-permute-done.4.refs_4_ = f32[48,128]{1,0:T(8,128)S(1)} collective-permute-done((f32[48,128]{1,0:T(8,128)S(1)}, f32[48,128]{1,0:T(8,128)S(1)}, u32[]{:S(2)}, u32[]{:S(2)}) %collective-permute-start.4) | collective-permute-done | bytes 24608 | tf_op jit(solution)/shard_map/ppermute | solution.py:385
  16.6 1.1 %shard_map.97 = (f32[128,128]{1,0:T(8,128)S(1)}, f32[31,72,256]{2,1,0:T(8,128)S(1)}, f32[72,256]{1,0:T(8,128)S(1)}, f32[12,72,256]{2,1,0:T(8,128)S(1)}) custom-call(f32[19,64,128]{2,1,0:T(8,128)S(1)} %get-tuple-element.19.refs_0_, f32[19,8,128]{2,1,0:T(8,128)S(1)} %get-tuple-element.24.refs_1_, f32[72,128]{1,0:T(8,128)S(1)} %get-tuple-element.25.refs_2_, ...), custom_call_target="tpu_custom_call" | custom-call | bytes 4096000 | tf_op jit(solution)/shard_map/pallas_call | solution.py:371
  17.7 0.6 %shard_map.98 = (f32[2,64,128]{2,1,0:T(8,128)S(1)}, f32[4,64,128]{2,1,0:T(8,128)S(1)}, f32[8,128]{1,0:T(8,128)S(1)}) custom-call(f32[31,72,256]{2,1,0:T(8,128)S(1)} %get-tuple-element.28.refs_0_, f32[72,256]{1,0:T(8,128)S(1)} %get-tuple-element.29.refs_1_, f32[12,72,256]{2,1,0:T(8,128)S(1)} %get-tuple-element.30.refs_2_), custom_call_target="tpu_custom_call" | custom-call | bytes 3444736 | tf_op jit(solution)/shard_map/pallas_call | solution.py:371
  18.3 2.4 %collective-permute-start.7 = (f32[8,128]{1,0:T(8,128)S(1)}, f32[8,128]{1,0:T(8,128)S(1)}, u32[]{:S(2)}, u32[]{:S(2)}) collective-permute-start(f32[8,128]{1,0:T(8,128)S(1)} %get-tuple-element.31), channel_id=1, source_target_pairs={{0,8},{4,12},{8,0},{12,4},{1,9},{5,13},{9,1},{13,5},{2,10},{6,14},... | collective-permute-start | bytes 12296 | tf_op jit(solution)/shard_map/ppermute | solution.py:385
  20.7 1.8 %collective-permute-start.6 = (f32[8,128]{1,0:T(8,128)S(1)}, f32[8,128]{1,0:T(8,128)S(1)}, u32[]{:S(2)}, u32[]{:S(2)}) collective-permute-start(f32[8,128]{1,0:T(8,128)S(1)} %get-tuple-element.31), channel_id=1, source_target_pairs={{0,12},{4,8},{8,4},{12,0},{1,13},{5,9},{9,5},{13,1},{2,14},{6,10},... | collective-permute-start | bytes 12296 | tf_op jit(solution)/shard_map/ppermute | solution.py:385
  22.5 0.0 collective-permute-start.5
  22.5 2.6 %collective-permute-start.11 = (f32[128,128]{1,0:T(8,128)S(1)}, f32[128,128]{1,0:T(8,128)S(1)}, u32[]{:S(2)}, u32[]{:S(2)}) collective-permute-start(f32[128,128]{1,0:T(8,128)S(1)} %get-tuple-element.35.refs_4_), channel_id=1, source_target_pairs={{0,8},{4,12},{8,0},{12,4},{1,9},{5,13},{9,1},{13,5},{2,10},{6,14},... | collective-permute-start | bytes 196616 | tf_op jit(solution)/shard_map/ppermute | solution.py:385
  25.1 1.8 %collective-permute-start.13 = (f32[128,128]{1,0:T(8,128)S(1)}, f32[128,128]{1,0:T(8,128)S(1)}, u32[]{:S(2)}, u32[]{:S(2)}) collective-permute-start(f32[128,128]{1,0:T(8,128)S(1)} %get-tuple-element.35.refs_4_), channel_id=1, source_target_pairs={{0,12},{4,8},{8,4},{12,0},{1,13},{5,9},{9,5},{13,1},{2,14},{6,10},... | collective-permute-start | bytes 196616 | tf_op jit(solution)/shard_map/ppermute | solution.py:385
  26.9 0.0 collective-permute-done.6
  26.9 0.0 collective-permute-done.5
  26.9 0.1 collective-permute-start.8
  27.0 1.6 %collective-permute-start.9 = (f32[8,128]{1,0:T(8,128)S(1)}, f32[8,128]{1,0:T(8,128)S(1)}, u32[]{:S(2)}, u32[]{:S(2)}) collective-permute-start(f32[8,128]{1,0:T(8,128)S(1)} %add_add_fusion.refs_0_), channel_id=1, source_target_pairs={{0,3},{1,2},{2,1},{3,0},{4,7},{5,6},{6,5},{7,4},{8,11},{9,10},{10,... | collective-permute-start | bytes 12296 | tf_op jit(solution)/shard_map/ppermute | solution.py:385
  28.6 0.0 collective-permute-done.11.refs_1_
  28.6 1.4 %collective-permute-start.10 = (f32[8,128]{1,0:T(8,128)S(1)}, f32[8,128]{1,0:T(8,128)S(1)}, u32[]{:S(2)}, u32[]{:S(2)}) collective-permute-start(f32[8,128]{1,0:T(8,128)S(1)} %add_add_fusion.refs_0_), channel_id=1, source_target_pairs={{0,2},{1,3},{2,0},{3,1},{4,6},{5,7},{6,4},{7,5},{8,10},{9,11},{10,... | collective-permute-start | bytes 12296 | tf_op jit(solution)/shard_map/ppermute | solution.py:385
  30.1 0.4 %shard_map.99.refs_0_ = bf16[512,256]{1,0:T(8,128)(2,1)S(1)} custom-call(s32[1,512]{1,0:T(1,128)S(1)} %get-tuple-element.34.home), custom_call_target="tpu_custom_call" | custom-call | bytes 264192 | tf_op jit(solution)/shard_map/pallas_call | solution.py:371
  30.4 0.0 collective-permute-done.12.refs_2_
  30.4 1.0 %collective-permute-done.13.refs_3_ = f32[128,128]{1,0:T(8,128)S(1)} collective-permute-done((f32[128,128]{1,0:T(8,128)S(1)}, f32[128,128]{1,0:T(8,128)S(1)}, u32[]{:S(2)}, u32[]{:S(2)}) %collective-permute-start.13) | collective-permute-done | bytes 65568 | tf_op jit(solution)/shard_map/ppermute | solution.py:385
  31.4 0.6 %shard_map.100.refs_6_ = f32[512,256]{1,0:T(8,128)S(1)} custom-call(bf16[512,256]{1,0:T(8,128)(2,1)S(1)} %shard_map.99.refs_0_, f32[128,128]{1,0:T(8,128)S(1)} %collective-permute-done.11.refs_1_, f32[128,128]{1,0:T(8,128)S(1)} %collective-permute-done.12.refs_2_, f32[128,128]{1,0:T(8,128)S(1)} %collective-permute-done.13.refs_3_, ...), custom_call_target="tpu_custom_call" | custom-call | bytes 1048576 | tf_op jit(solution)/shard_map/pallas_call | solution.py:371
  32.0 0.0 collective-permute-done.9.refs_2_
  32.0 0.2 collective-permute-done.10.refs_3_
  32.2 0.9 %shard_map.101 = (f32[4,64,128]{2,1,0:T(8,128)}, f32[512,128]{1,0:T(8,128)}) custom-call(f32[8,128]{1,0:T(8,128)S(1)} %add_add_fusion.refs_0_, f32[8,128]{1,0:T(8,128)S(1)} %collective-permute-done.8.refs_1_, f32[8,128]{1,0:T(8,128)S(1)} %collective-permute-done.9.refs_2_, f32[8,128]{1,0:T(8,128)S(1)} %collective-permute-done.10.refs_3_, ...), custom_call_target="tpu_custom_call" | custom-call | bytes 1130496 | tf_op jit(solution)/shard_map/pallas_call | solution.py:371
  (4 shorter events, 0.0 us)
Async XLA Ops:
  2.8 10.2 %collective-permute-start = (f32[152,128]{1,0:T(8,128)S(1)}, f32[152,128]{1,0:T(8,128)S(1)}, u32[]{:S(2)}, u32[]{:S(2)}) collective-permute-start(f32[152,128]{1,0:T(8,128)S(1)} %get-tuple-element.21), channel_id=1, source_target_pairs={{0,12},{4,8},{8,4},{12,0},{1,13},{5,9},{9,5},{13,1},{2,14},{6,10},... | collective-permute-start | bytes 233480 | tf_op jit(solution)/shard_map/ppermute | solution.py:385
  7.9 5.1 %collective-permute-start.1 = (f32[152,128]{1,0:T(8,128)S(1)}, f32[152,128]{1,0:T(8,128)S(1)}, u32[]{:S(2)}, u32[]{:S(2)}) collective-permute-start(f32[152,128]{1,0:T(8,128)S(1)} %get-tuple-element.22), channel_id=1, source_target_pairs={{0,4},{4,0},{8,12},{12,8},{1,5},{5,1},{9,13},{13,9},{2,6},{6,2},{1... | collective-permute-start | bytes 233480 | tf_op jit(solution)/shard_map/ppermute | solution.py:385
  7.9 5.1 %collective-permute-start.2 = (f32[72,128]{1,0:T(8,128)S(1)}, f32[72,128]{1,0:T(8,128)S(1)}, u32[]{:S(2)}, u32[]{:S(2)}) collective-permute-start(f32[72,128]{1,0:T(8,128)S(1)} %get-tuple-element.23), channel_id=1, source_target_pairs={{0,8},{4,12},{8,0},{12,4},{1,9},{5,13},{9,1},{13,5},{2,10},{6,14},... | collective-permute-start | bytes 110600 | tf_op jit(solution)/shard_map/ppermute | solution.py:385
  13.2 1.8 %collective-permute-start.3 = (f32[48,128]{1,0:T(8,128)S(1)}, f32[48,128]{1,0:T(8,128)S(1)}, u32[]{:S(2)}, u32[]{:S(2)}) collective-permute-start(f32[48,128]{1,0:T(8,128)S(1)} %get-tuple-element.26), channel_id=1, source_target_pairs={{0,1},{1,0},{2,3},{3,2},{4,5},{5,4},{6,7},{7,6},{8,9},{9,8},{10,11... | collective-permute-start | bytes 73736 | tf_op jit(solution)/shard_map/ppermute | solution.py:385
  13.3 3.3 %collective-permute-start.4 = (f32[48,128]{1,0:T(8,128)S(1)}, f32[48,128]{1,0:T(8,128)S(1)}, u32[]{:S(2)}, u32[]{:S(2)}) collective-permute-start(f32[48,128]{1,0:T(8,128)S(1)} %get-tuple-element.27), channel_id=1, source_target_pairs={{0,3},{1,2},{2,1},{3,0},{4,7},{5,6},{6,5},{7,4},{8,11},{9,10},{10,... | collective-permute-start | bytes 73736 | tf_op jit(solution)/shard_map/ppermute | solution.py:385
  18.3 6.8 %collective-permute-start.7 = (f32[8,128]{1,0:T(8,128)S(1)}, f32[8,128]{1,0:T(8,128)S(1)}, u32[]{:S(2)}, u32[]{:S(2)}) collective-permute-start(f32[8,128]{1,0:T(8,128)S(1)} %get-tuple-element.31), channel_id=1, source_target_pairs={{0,8},{4,12},{8,0},{12,4},{1,9},{5,13},{9,1},{13,5},{2,10},{6,14},... | collective-permute-start | bytes 12296 | tf_op jit(solution)/shard_map/ppermute | solution.py:385
  20.7 6.2 %collective-permute-start.6 = (f32[8,128]{1,0:T(8,128)S(1)}, f32[8,128]{1,0:T(8,128)S(1)}, u32[]{:S(2)}, u32[]{:S(2)}) collective-permute-start(f32[8,128]{1,0:T(8,128)S(1)} %get-tuple-element.31), channel_id=1, source_target_pairs={{0,12},{4,8},{8,4},{12,0},{1,13},{5,9},{9,5},{13,1},{2,14},{6,10},... | collective-permute-start | bytes 12296 | tf_op jit(solution)/shard_map/ppermute | solution.py:385
  22.5 4.4 %collective-permute-start.5 = (f32[8,128]{1,0:T(8,128)S(1)}, f32[8,128]{1,0:T(8,128)S(1)}, u32[]{:S(2)}, u32[]{:S(2)}) collective-permute-start(f32[8,128]{1,0:T(8,128)S(1)} %get-tuple-element.31), channel_id=1, source_target_pairs={{0,4},{4,0},{8,12},{12,8},{1,5},{5,1},{9,13},{13,9},{2,6},{6,2},{1... | collective-permute-start | bytes 12296 | tf_op jit(solution)/shard_map/ppermute | solution.py:385
  22.5 6.1 %collective-permute-start.11 = (f32[128,128]{1,0:T(8,128)S(1)}, f32[128,128]{1,0:T(8,128)S(1)}, u32[]{:S(2)}, u32[]{:S(2)}) collective-permute-start(f32[128,128]{1,0:T(8,128)S(1)} %get-tuple-element.35.refs_4_), channel_id=1, source_target_pairs={{0,8},{4,12},{8,0},{12,4},{1,9},{5,13},{9,1},{13,5},{2,10},{6,14},... | collective-permute-start | bytes 196616 | tf_op jit(solution)/shard_map/ppermute | solution.py:385
  25.1 5.3 %collective-permute-start.12 = (f32[128,128]{1,0:T(8,128)S(1)}, f32[128,128]{1,0:T(8,128)S(1)}, u32[]{:S(2)}, u32[]{:S(2)}) collective-permute-start(f32[128,128]{1,0:T(8,128)S(1)} %get-tuple-element.35.refs_4_), channel_id=1, source_target_pairs={{0,4},{4,0},{8,12},{12,8},{1,5},{5,1},{9,13},{13,9},{2,6},{6,2},{1... | collective-permute-start | bytes 196616 | tf_op jit(solution)/shard_map/ppermute | solution.py:385
  25.1 6.3 %collective-permute-start.13 = (f32[128,128]{1,0:T(8,128)S(1)}, f32[128,128]{1,0:T(8,128)S(1)}, u32[]{:S(2)}, u32[]{:S(2)}) collective-permute-start(f32[128,128]{1,0:T(8,128)S(1)} %get-tuple-element.35.refs_4_), channel_id=1, source_target_pairs={{0,12},{4,8},{8,4},{12,0},{1,13},{5,9},{9,5},{13,1},{2,14},{6,10},... | collective-permute-start | bytes 196616 | tf_op jit(solution)/shard_map/ppermute | solution.py:385
  26.9 5.1 %collective-permute-start.8 = (f32[8,128]{1,0:T(8,128)S(1)}, f32[8,128]{1,0:T(8,128)S(1)}, u32[]{:S(2)}, u32[]{:S(2)}) collective-permute-start(f32[8,128]{1,0:T(8,128)S(1)} %add_add_fusion.refs_0_), channel_id=1, source_target_pairs={{0,1},{1,0},{2,3},{3,2},{4,5},{5,4},{6,7},{7,6},{8,9},{9,8},{10,11... | collective-permute-start | bytes 12296 | tf_op jit(solution)/shard_map/ppermute | solution.py:385
  27.0 5.0 %collective-permute-start.9 = (f32[8,128]{1,0:T(8,128)S(1)}, f32[8,128]{1,0:T(8,128)S(1)}, u32[]{:S(2)}, u32[]{:S(2)}) collective-permute-start(f32[8,128]{1,0:T(8,128)S(1)} %add_add_fusion.refs_0_), channel_id=1, source_target_pairs={{0,3},{1,2},{2,1},{3,0},{4,7},{5,6},{6,5},{7,4},{8,11},{9,10},{10,... | collective-permute-start | bytes 12296 | tf_op jit(solution)/shard_map/ppermute | solution.py:385
  28.6 3.6 %collective-permute-start.10 = (f32[8,128]{1,0:T(8,128)S(1)}, f32[8,128]{1,0:T(8,128)S(1)}, u32[]{:S(2)}, u32[]{:S(2)}) collective-permute-start(f32[8,128]{1,0:T(8,128)S(1)} %add_add_fusion.refs_0_), channel_id=1, source_target_pairs={{0,2},{1,3},{2,0},{3,1},{4,6},{5,7},{6,4},{7,5},{8,10},{9,11},{10,... | collective-permute-start | bytes 12296 | tf_op jit(solution)/shard_map/ppermute | solution.py:385

commit v4 on v3

--- a/solution.py
+++ b/solution.py
@@ -14,7 +14,7 @@
 F32 = jnp.float32
 BF16 = jnp.bfloat16
 ROW_TURNS = (1, 0, 2)
-DATA_TURNS = (2, 0, 1)
+DATA_TURNS = (1, 0, 2)
 
 
 def lanes_of(shape):
@@ -255,8 +255,8 @@
         return found
 
 
-def adjoint(layers, shape, refs):
-    planes, rims, middle, even, odd, message, grid, base, fields, ground = refs
+def solve(layers, shape, refs):
+    planes, rims, middle, even, odd, message, zed, you, scalars, grid, base, ground = refs
     rows, ring = shape
     width = 2 * LANES
     tx, ty = lax.axis_index("tx"), lax.axis_index("ty")
@@ -307,16 +307,8 @@
     u = op.smooth(q)
     message[0:rows, :] = z[0][0:rows, 0:LANES]
     message[rows : 2 * rows, :] = u[0][0:rows, 0:LANES]
-    for k, field in enumerate((z, q, u)):
-        for p in range(layers):
-            fields[k * layers + p] = field[p]
-
-
-def forward(layers, shape, refs):
-    grid, base, fields, zed, you, scalars = refs
-    rows, ring = shape
-    op = Grid(grid, layers, rows)
     b = [base[...]] + [None] * (layers - 1)
+    found = op.products([ref[...] for ref in op.weight], z, q, u)
     z = op.smooth(b)
     q = op.apply(z)
     u = op.smooth(q)
@@ -324,10 +316,9 @@
         if z[p] is not None:
             zed[p] = z[p][0:rows, 0:LANES]
         you[p] = u[p][0:rows, 0:LANES]
-    found = op.products(b, z, q, u)
-    z, q, u = ([fields[k * layers + p] for p in range(layers)] for k in range(3))
-    found += op.products([ref[...] for ref in op.weight], z, q, u)
-    scalars[...] = jnp.concatenate(found, axis=0)
+    found = jnp.concatenate(op.products(b, z, q, u) + found, axis=0)
+    scalars[...] = found
+    message[2 * rows :, :] = found
 
 
 def choose(count, rows, refs):
@@ -352,7 +343,8 @@
         bz, zq, qu, uw = (total[4 * which + i : 4 * which + i + 1] for i in range(4))
         ratio = qu / zq
         step = bz / zq
-        second = (zq - ratio * bz) / (uw - ratio * qu)
+        left = uw - ratio * qu
+        second = jnp.where(left > 2e-7 * uw, (zq - ratio * bz) / left, -step)
         first = step - second * ratio
         if which == 0:
             for p in range(you.shape[0]):
@@ -436,24 +428,25 @@
     )
     even, odd = exchange(sends, "ty")
     width2 = 2 * LANES
-    message, *state = call(
-        lambda *refs: adjoint(layers, shape, refs),
+    message, zed, you, total = call(
+        lambda *refs: solve(layers, shape, refs),
         (
-            array(2 * rows, LANES),
-            array(8 * layers - 1, ring, width2),
-            array(ring, width2),
-            array(3 * layers, ring, width2),
+            array(2 * rows + SUB, LANES),
+            array(min(2, layers), rows, LANES),
+            array(layers, rows, LANES),
+            array(SUB, LANES),
         ),
         (held, rims, middle, even, odd),
-        scratch=[pltpu.VMEM((layers, ring, width2), F32)],
-    )
-    messages = in_turn(exchange([message] * (count - 1), "tx"), DATA_TURNS) + [message]
-    zed, you, total = call(
-        lambda *refs: forward(layers, shape, refs),
-        (array(min(2, layers), rows, LANES), array(layers, rows, LANES), array(SUB, LANES)),
-        state,
-    )
-    total = functools.reduce(jnp.add, [total] + exchange([total] * (count - 1), "tx"))
+        scratch=[
+            pltpu.VMEM((8 * layers - 1, ring, width2), F32),
+            pltpu.VMEM((ring, width2), F32),
+            pltpu.VMEM((layers, ring, width2), F32),
+        ],
+    )
+    got = exchange([message] * (count - 1), "tx")
+    ahead = exchange([total] * (count - 1), "tx")[2:]
+    total = functools.reduce(jnp.add, [total] + [m[2 * rows :] for m in got[:2]] + ahead)
+    messages = in_turn(got, DATA_TURNS) + [message]
     totals = [total] + exchange([total] * (ways - 1), "ty")
     (chosen,) = call(
         lambda *refs: choose(count, rows, refs),

time: 33.3 us -> 32.5 us (0.976)
  starting transfers between devices: 19.2 us -> 16.5 us
  waiting for transfers between devices: 7.31 us -> 9.14 us
    ppermute x14 -> x12, starting transfers between devices: 19.2 us -> 16.5 us  [exchange(): lax.ppermute(value, axis, list(enumerate(target)))]
    ppermute x14 -> x12, waiting for transfers between devices: 7.31 us -> 9.14 us  [exchange(): lax.ppermute(value, axis, list(enumerate(target)))]
    pallas_call x7 -> x6, Pallas kernels: 5.19 us -> 5.28 us  [call(): pl.pallas_call(kernel, out_shape=tuple(outs), in_specs=specs or [vmem() f...]
  transfers between devices with their start and end apart: 14 -> 12, of which waited for: 4 -> 6; matrix products, arithmetic and copies ran while one was open for 0% -> 0% of each run, Pallas kernels for 3% -> 3%
where the time goes in v4:
time: 32.5 us; the launch traced here: 32.3 us
  starting transfers between devices  16.5 us (51%)
  waiting for transfers between devices  9.14 us (28%)
  Pallas kernels  5.28 us (16%)
  between operations  1.33 us (4%)
    ppermute x12, starting transfers between devices, exchange(): lax.ppermute(value, axis, list(enumerate(target)))  16.5 us
    ppermute x12, waiting for transfers between devices, exchange(): lax.ppermute(value, axis, list(enumerate(target)))  9.14 us
    pallas_call x6, Pallas kernels, call(): pl.pallas_call(kernel, out_shape=tuple(outs), in_specs=specs or [vmem() f...  5.28 us
  transfers between devices with their start and end apart: 12, of which 6 were waited for; matrix products, arithmetic and copies ran while one was open for 0% of the time, Pallas kernels for 3%

profile of v4, /device:TPU:0, one launch (start us, length us, event | category | flops | bytes accessed | tf_op | source)
XLA Modules:
  0.0 32.3 jit_solution(11873126108456411112)
XLA Ops:
  1.3 1.5 %shard_map.95 = (f32[19,64,128]{2,1,0:T(8,128)S(1)}, f32[72,128]{1,0:T(8,128)S(1)}, s32[1,512]{1,0:T(1,128)S(1)}, f32[152,128]{1,0:T(8,128)S(1)}, f32[152,128]{1,0:T(8,128)S(1)}, /*index=5*/f32[72,128]{1,0:T(8,128)S(1)}) custom-call(f32[4,64,128]{2,1,0:T(8,128)} %refs_0_.1, f32[4,64,128]{2,1,0:T(8,128)} %refs_1_.1, f32[3,64,128]{2,1,0:T(8,128)} %refs_2_.1, ...), custom_call_target="tpu_custom_call" | custom-call | bytes 1740804 | tf_op jit(solution)/shard_map/pallas_call | solution.py:363
  2.8 5.1 %collective-permute-start = (f32[152,128]{1,0:T(8,128)S(1)}, f32[152,128]{1,0:T(8,128)S(1)}, u32[]{:S(2)}, u32[]{:S(2)}) collective-permute-start(f32[152,128]{1,0:T(8,128)S(1)} %get-tuple-element.18), channel_id=1, source_target_pairs={{0,12},{4,8},{8,4},{12,0},{1,13},{5,9},{9,5},{13,1},{2,14},{6,10},... | collective-permute-start | bytes 233480 | tf_op jit(solution)/shard_map/ppermute | solution.py:377
  7.9 0.0 collective-permute-start.1
  7.9 0.6 %collective-permute-start.2 = (f32[72,128]{1,0:T(8,128)S(1)}, f32[72,128]{1,0:T(8,128)S(1)}, u32[]{:S(2)}, u32[]{:S(2)}) collective-permute-start(f32[72,128]{1,0:T(8,128)S(1)} %get-tuple-element.20), channel_id=1, source_target_pairs={{0,8},{4,12},{8,0},{12,4},{1,9},{5,13},{9,1},{13,5},{2,10},{6,14},... | collective-permute-start | bytes 110600 | tf_op jit(solution)/shard_map/ppermute | solution.py:377
  8.5 4.5 %collective-permute-done.2.refs_4_ = f32[72,128]{1,0:T(8,128)S(1)} collective-permute-done((f32[72,128]{1,0:T(8,128)S(1)}, f32[72,128]{1,0:T(8,128)S(1)}, u32[]{:S(2)}, u32[]{:S(2)}) %collective-permute-start.2) | collective-permute-done | bytes 36896 | tf_op jit(solution)/shard_map/ppermute | solution.py:377
  13.0 0.0 collective-permute-done.refs_2_
  13.0 0.0 collective-permute-done.1.refs_3_
  13.0 0.3 shard_map.96
  13.3 0.1 collective-permute-start.3
  13.3 1.7 %collective-permute-start.4 = (f32[48,128]{1,0:T(8,128)S(1)}, f32[48,128]{1,0:T(8,128)S(1)}, u32[]{:S(2)}, u32[]{:S(2)}) collective-permute-start(f32[48,128]{1,0:T(8,128)S(1)} %get-tuple-element.24), channel_id=1, source_target_pairs={{0,3},{1,2},{2,1},{3,0},{4,7},{5,6},{6,5},{7,4},{8,11},{9,10},{10,... | collective-permute-start | bytes 73736 | tf_op jit(solution)/shard_map/ppermute | solution.py:377
  15.1 0.0 collective-permute-done.3.refs_3_
  15.1 1.6 %collective-permute-done.4.refs_4_ = f32[48,128]{1,0:T(8,128)S(1)} collective-permute-done((f32[48,128]{1,0:T(8,128)S(1)}, f32[48,128]{1,0:T(8,128)S(1)}, u32[]{:S(2)}, u32[]{:S(2)}) %collective-permute-start.4) | collective-permute-done | bytes 24608 | tf_op jit(solution)/shard_map/ppermute | solution.py:377
  16.6 1.8 %shard_map.97 = (f32[136,128]{1,0:T(8,128)S(1)}, f32[2,64,128]{2,1,0:T(8,128)S(1)}, f32[4,64,128]{2,1,0:T(8,128)S(1)}, f32[8,128]{1,0:T(8,128)S(1)}) custom-call(f32[19,64,128]{2,1,0:T(8,128)S(1)} %get-tuple-element.16.refs_0_, f32[19,8,128]{2,1,0:T(8,128)S(1)} %get-tuple-element.21.refs_1_, f32[72,128]{1,0:T(8,128)S(1)} %get-tuple-element.22.refs_2_, ...), custom_call_target="tpu_custom_call" | custom-call | bytes 1056768 | tf_op jit(solution)/shard_map/pallas_call | solution.py:363
  18.4 1.8 %collective-permute-start.5 = (f32[136,128]{1,0:T(8,128)S(1)}, f32[136,128]{1,0:T(8,128)S(1)}, u32[]{:S(2)}, u32[]{:S(2)}) collective-permute-start(f32[136,128]{1,0:T(8,128)S(1)} %get-tuple-element.26.refs_4_), channel_id=1, source_target_pairs={{0,4},{4,0},{8,12},{12,8},{1,5},{5,1},{9,13},{13,9},{2,6},{6,2},{1... | collective-permute-start | bytes 208904 | tf_op jit(solution)/shard_map/ppermute | solution.py:377
  20.2 2.0 %collective-permute-start.6 = (f32[136,128]{1,0:T(8,128)S(1)}, f32[136,128]{1,0:T(8,128)S(1)}, u32[]{:S(2)}, u32[]{:S(2)}) collective-permute-start(f32[136,128]{1,0:T(8,128)S(1)} %get-tuple-element.26.refs_4_), channel_id=1, source_target_pairs={{0,12},{4,8},{8,4},{12,0},{1,13},{5,9},{9,5},{13,1},{2,14},{6,10},... | collective-permute-start | bytes 208904 | tf_op jit(solution)/shard_map/ppermute | solution.py:377
  22.3 0.0 collective-permute-start.7
  22.3 2.9 %collective-permute-start.11 = (f32[136,128]{1,0:T(8,128)S(1)}, f32[136,128]{1,0:T(8,128)S(1)}, u32[]{:S(2)}, u32[]{:S(2)}) collective-permute-start(f32[136,128]{1,0:T(8,128)S(1)} %get-tuple-element.26.refs_4_), channel_id=1, source_target_pairs={{0,8},{4,12},{8,0},{12,4},{1,9},{5,13},{9,1},{13,5},{2,10},{6,14},... | collective-permute-start | bytes 208904 | tf_op jit(solution)/shard_map/ppermute | solution.py:377
  25.2 1.6 %collective-permute-done.7 = f32[8,128]{1,0:T(8,128)S(1)} collective-permute-done((f32[8,128]{1,0:T(8,128)S(1)}, f32[8,128]{1,0:T(8,128)S(1)}, u32[]{:S(2)}, u32[]{:S(2)}) %collective-permute-start.7) | collective-permute-done | bytes 4128 | tf_op jit(solution)/shard_map/ppermute | solution.py:377
  26.8 0.0 collective-permute-done.5.refs_2_
  26.8 0.0 collective-permute-done.6.refs_1_
  26.8 1.6 %collective-permute-start.10 = (f32[8,128]{1,0:T(8,128)S(1)}, f32[8,128]{1,0:T(8,128)S(1)}, u32[]{:S(2)}, u32[]{:S(2)}) collective-permute-start(f32[8,128]{1,0:T(8,128)S(1)} %fusion.refs_0_), channel_id=1, source_target_pairs={{0,2},{1,3},{2,0},{3,1},{4,6},{5,7},{6,4},{7,5},{8,10},{9,11},{10,... | collective-permute-start | bytes 12296 | tf_op jit(solution)/shard_map/ppermute | solution.py:377
  28.4 0.0 collective-permute-start.8
  28.4 0.7 %collective-permute-start.9 = (f32[8,128]{1,0:T(8,128)S(1)}, f32[8,128]{1,0:T(8,128)S(1)}, u32[]{:S(2)}, u32[]{:S(2)}) collective-permute-start(f32[8,128]{1,0:T(8,128)S(1)} %fusion.refs_0_), channel_id=1, source_target_pairs={{0,3},{1,2},{2,1},{3,0},{4,7},{5,6},{6,5},{7,4},{8,11},{9,10},{10,... | collective-permute-start | bytes 12296 | tf_op jit(solution)/shard_map/ppermute | solution.py:377
  29.0 0.4 %shard_map.98.refs_0_ = bf16[512,256]{1,0:T(8,128)(2,1)S(1)} custom-call(s32[1,512]{1,0:T(1,128)S(1)} %get-tuple-element.29.home), custom_call_target="tpu_custom_call" | custom-call | bytes 264192 | tf_op jit(solution)/shard_map/pallas_call | solution.py:363
  29.4 0.1 collective-permute-done.11.refs_3_
  29.5 0.6 %shard_map.99.refs_6_ = f32[512,256]{1,0:T(8,128)S(1)} custom-call(bf16[512,256]{1,0:T(8,128)(2,1)S(1)} %shard_map.98.refs_0_, f32[136,128]{1,0:T(8,128)S(1)} %collective-permute-done.6.refs_1_, f32[136,128]{1,0:T(8,128)S(1)} %collective-permute-done.5.refs_2_, f32[136,128]{1,0:T(8,128)S(1)} %collective-permute-done.11.refs_3_, ...), custom_call_target="tpu_custom_call" | custom-call | bytes 1064960 | tf_op jit(solution)/shard_map/pallas_call | solution.py:363
  30.0 0.5 %collective-permute-done.10.refs_3_ = f32[8,128]{1,0:T(8,128)S(1)} collective-permute-done((f32[8,128]{1,0:T(8,128)S(1)}, f32[8,128]{1,0:T(8,128)S(1)}, u32[]{:S(2)}, u32[]{:S(2)}) %collective-permute-start.10) | collective-permute-done | bytes 4128 | tf_op jit(solution)/shard_map/ppermute | solution.py:377
  30.5 0.0 collective-permute-done.8.refs_1_
  30.5 0.9 %collective-permute-done.9.refs_2_ = f32[8,128]{1,0:T(8,128)S(1)} collective-permute-done((f32[8,128]{1,0:T(8,128)S(1)}, f32[8,128]{1,0:T(8,128)S(1)}, u32[]{:S(2)}, u32[]{:S(2)}) %collective-permute-start.9) | collective-permute-done | bytes 4128 | tf_op jit(solution)/shard_map/ppermute | solution.py:377
  31.4 0.9 %shard_map.100 = (f32[4,64,128]{2,1,0:T(8,128)}, f32[512,128]{1,0:T(8,128)}) custom-call(f32[8,128]{1,0:T(8,128)S(1)} %fusion.refs_0_, f32[8,128]{1,0:T(8,128)S(1)} %collective-permute-done.8.refs_1_, f32[8,128]{1,0:T(8,128)S(1)} %collective-permute-done.9.refs_2_, f32[8,128]{1,0:T(8,128)S(1)} %collective-permute-done.10.refs_3_, ...), custom_call_target="tpu_custom_call" | custom-call | bytes 1130496 | tf_op jit(solution)/shard_map/pallas_call | solution.py:363
  (1 shorter events, 0.0 us)
Async XLA Ops:
  2.8 10.2 %collective-permute-start = (f32[152,128]{1,0:T(8,128)S(1)}, f32[152,128]{1,0:T(8,128)S(1)}, u32[]{:S(2)}, u32[]{:S(2)}) collective-permute-start(f32[152,128]{1,0:T(8,128)S(1)} %get-tuple-element.18), channel_id=1, source_target_pairs={{0,12},{4,8},{8,4},{12,0},{1,13},{5,9},{9,5},{13,1},{2,14},{6,10},... | collective-permute-start | bytes 233480 | tf_op jit(solution)/shard_map/ppermute | solution.py:377
  7.9 5.1 %collective-permute-start.1 = (f32[152,128]{1,0:T(8,128)S(1)}, f32[152,128]{1,0:T(8,128)S(1)}, u32[]{:S(2)}, u32[]{:S(2)}) collective-permute-start(f32[152,128]{1,0:T(8,128)S(1)} %get-tuple-element.19), channel_id=1, source_target_pairs={{0,4},{4,0},{8,12},{12,8},{1,5},{5,1},{9,13},{13,9},{2,6},{6,2},{1... | collective-permute-start | bytes 233480 | tf_op jit(solution)/shard_map/ppermute | solution.py:377
  7.9 5.1 %collective-permute-start.2 = (f32[72,128]{1,0:T(8,128)S(1)}, f32[72,128]{1,0:T(8,128)S(1)}, u32[]{:S(2)}, u32[]{:S(2)}) collective-permute-start(f32[72,128]{1,0:T(8,128)S(1)} %get-tuple-element.20), channel_id=1, source_target_pairs={{0,8},{4,12},{8,0},{12,4},{1,9},{5,13},{9,1},{13,5},{2,10},{6,14},... | collective-permute-start | bytes 110600 | tf_op jit(solution)/shard_map/ppermute | solution.py:377
  13.3 1.8 %collective-permute-start.3 = (f32[48,128]{1,0:T(8,128)S(1)}, f32[48,128]{1,0:T(8,128)S(1)}, u32[]{:S(2)}, u32[]{:S(2)}) collective-permute-start(f32[48,128]{1,0:T(8,128)S(1)} %get-tuple-element.23), channel_id=1, source_target_pairs={{0,1},{1,0},{2,3},{3,2},{4,5},{5,4},{6,7},{7,6},{8,9},{9,8},{10,11... | collective-permute-start | bytes 73736 | tf_op jit(solution)/shard_map/ppermute | solution.py:377
  13.3 3.3 %collective-permute-start.4 = (f32[48,128]{1,0:T(8,128)S(1)}, f32[48,128]{1,0:T(8,128)S(1)}, u32[]{:S(2)}, u32[]{:S(2)}) collective-permute-start(f32[48,128]{1,0:T(8,128)S(1)} %get-tuple-element.24), channel_id=1, source_target_pairs={{0,3},{1,2},{2,1},{3,0},{4,7},{5,6},{6,5},{7,4},{8,11},{9,10},{10,... | collective-permute-start | bytes 73736 | tf_op jit(solution)/shard_map/ppermute | solution.py:377
  18.4 8.4 %collective-permute-start.5 = (f32[136,128]{1,0:T(8,128)S(1)}, f32[136,128]{1,0:T(8,128)S(1)}, u32[]{:S(2)}, u32[]{:S(2)}) collective-permute-start(f32[136,128]{1,0:T(8,128)S(1)} %get-tuple-element.26.refs_4_), channel_id=1, source_target_pairs={{0,4},{4,0},{8,12},{12,8},{1,5},{5,1},{9,13},{13,9},{2,6},{6,2},{1... | collective-permute-start | bytes 208904 | tf_op jit(solution)/shard_map/ppermute | solution.py:377
  20.2 6.6 %collective-permute-start.6 = (f32[136,128]{1,0:T(8,128)S(1)}, f32[136,128]{1,0:T(8,128)S(1)}, u32[]{:S(2)}, u32[]{:S(2)}) collective-permute-start(f32[136,128]{1,0:T(8,128)S(1)} %get-tuple-element.26.refs_4_), channel_id=1, source_target_pairs={{0,12},{4,8},{8,4},{12,0},{1,13},{5,9},{9,5},{13,1},{2,14},{6,10},... | collective-permute-start | bytes 208904 | tf_op jit(solution)/shard_map/ppermute | solution.py:377
  22.3 4.5 %collective-permute-start.7 = (f32[8,128]{1,0:T(8,128)S(1)}, f32[8,128]{1,0:T(8,128)S(1)}, u32[]{:S(2)}, u32[]{:S(2)}) collective-permute-start(f32[8,128]{1,0:T(8,128)S(1)} %get-tuple-element.25), channel_id=1, source_target_pairs={{0,8},{4,12},{8,0},{12,4},{1,9},{5,13},{9,1},{13,5},{2,10},{6,14},... | collective-permute-start | bytes 12296 | tf_op jit(solution)/shard_map/ppermute | solution.py:377
  22.3 7.2 %collective-permute-start.11 = (f32[136,128]{1,0:T(8,128)S(1)}, f32[136,128]{1,0:T(8,128)S(1)}, u32[]{:S(2)}, u32[]{:S(2)}) collective-permute-start(f32[136,128]{1,0:T(8,128)S(1)} %get-tuple-element.26.refs_4_), channel_id=1, source_target_pairs={{0,8},{4,12},{8,0},{12,4},{1,9},{5,13},{9,1},{13,5},{2,10},{6,14},... | collective-permute-start | bytes 208904 | tf_op jit(solution)/shard_map/ppermute | solution.py:377
  26.8 3.7 %collective-permute-start.10 = (f32[8,128]{1,0:T(8,128)S(1)}, f32[8,128]{1,0:T(8,128)S(1)}, u32[]{:S(2)}, u32[]{:S(2)}) collective-permute-start(f32[8,128]{1,0:T(8,128)S(1)} %fusion.refs_0_), channel_id=1, source_target_pairs={{0,2},{1,3},{2,0},{3,1},{4,6},{5,7},{6,4},{7,5},{8,10},{9,11},{10,... | collective-permute-start | bytes 12296 | tf_op jit(solution)/shard_map/ppermute | solution.py:377
  28.4 2.1 %collective-permute-start.8 = (f32[8,128]{1,0:T(8,128)S(1)}, f32[8,128]{1,0:T(8,128)S(1)}, u32[]{:S(2)}, u32[]{:S(2)}) collective-permute-start(f32[8,128]{1,0:T(8,128)S(1)} %fusion.refs_0_), channel_id=1, source_target_pairs={{0,1},{1,0},{2,3},{3,2},{4,5},{5,4},{6,7},{7,6},{8,9},{9,8},{10,11... | collective-permute-start | bytes 12296 | tf_op jit(solution)/shard_map/ppermute | solution.py:377
  28.4 3.0 %collective-permute-start.9 = (f32[8,128]{1,0:T(8,128)S(1)}, f32[8,128]{1,0:T(8,128)S(1)}, u32[]{:S(2)}, u32[]{:S(2)}) collective-permute-start(f32[8,128]{1,0:T(8,128)S(1)} %fusion.refs_0_), channel_id=1, source_target_pairs={{0,3},{1,2},{2,1},{3,0},{4,7},{5,6},{6,5},{7,4},{8,11},{9,10},{10,... | collective-permute-start | bytes 12296 | tf_op jit(solution)/shard_map/ppermute | solution.py:377

commit v5 on v4

--- a/solution.py
+++ b/solution.py
@@ -11,6 +11,7 @@
 SUB = 8
 LANES = 128
 SLOTS = LANES // HALO
+WINDOW = 8 * HALO
 F32 = jnp.float32
 BF16 = jnp.bfloat16
 ROW_TURNS = (1, 0, 2)
@@ -241,7 +242,7 @@
             result.append(self.diagonal[p][...] * u[p] - 2.0 * term)
         return result
 
-    def products(self, b, z, q, u):
+    def products(self, b, z, q, u, kept):
         flow = self.flow(u)
         found = []
         for one, two in ((b, z), (z, q), (q, u), (u, flow)):
@@ -251,47 +252,28 @@
                     continue
                 term = left[0 : self.rows, 0:LANES] * right[0 : self.rows, 0:LANES]
                 total = term if total is None else total + term
-            found.append(jnp.sum(total, axis=0, keepdims=True))
+            found.append(jnp.sum(jnp.where(kept, total, 0.0), axis=0, keepdims=True))
         return found
 
 
-def solve(layers, shape, refs):
-    planes, rims, middle, even, odd, message, zed, you, scalars, grid, base, ground = refs
+def inner(layers, shape, refs):
+    planes, rims, middle, front, zed, you, sums, strips, grid, ground = refs
     rows, ring = shape
-    width = 2 * LANES
-    tx, ty = lax.axis_index("tx"), lax.axis_index("ty")
-    ty_even = lax.rem(ty, 2) == 0
+    tx = lax.axis_index("tx")
     op = Grid(grid, layers, rows)
     targets = [*op.cx, *op.cy, *op.via, *(ground.at[p] for p in range(layers)), *op.weight]
-
-    slot = lanes_of((SUB, LANES)) // HALO
-    tiles = tiles_of((planes, rims, middle))
-    for first in range(0, len(tiles), SLOTS):
-        q = first // SLOTS * SUB
-        one, two = even[q : q + SUB, :], odd[q : q + SUB, :]
-        after, before = jnp.where(ty_even, one, two), jnp.where(ty_even, two, one)
-        for s, (ref, index) in enumerate(tiles[first : first + SLOTS]):
-            both = jnp.where(slot == s, after, before)
-            both = pltpu.roll(both, LANES - HALO * s, 1) if s else both
-            if ref is middle:
-                base[index[0], 0:LANES] = ref[index]
-                base[index[0], LANES:] = both
-            else:
-                at = slice(rows, ring) if ref is rims else index[1]
-                targets[index[0]][at, 0:LANES] = ref[index]
-                targets[index[0]][at, LANES:] = both
-
-    row, lane = rows_of((ring, width)), lanes_of((ring, width))
-    inside = (
-        ((row < rows) | (row >= rows + HALO) | (tx < lax.axis_size("tx") - 1))
-        & ((row < rows + HALO) | (tx > 0))
-        & ((lane < LANES) | (lane >= width - HALO) | ((lane < LANES + HALO) & (ty < lax.axis_size("ty") - 1)))
-        & ((lane < width - HALO) | (ty > 0))
+    for p, target in enumerate(targets):
+        target[0:rows, :] = planes[p]
+        target[rows:ring, :] = rims[p]
+
+    row = rows_of((ring, LANES))
+    inside = ((row < rows) | (row >= rows + HALO) | (tx < lax.axis_size("tx") - 1)) & (
+        (row < rows + HALO) | (tx > 0)
     )
     for p in range(layers):
         cx, cy = op.cx[p][...], op.cy[p][...]
         cx_low = jnp.where((row == 0) & (tx == 0), 0.0, op.above(cx))
-        cy_low = jnp.where((lane == 0) & (ty == 0), 0.0, op.left(cy))
+        cy_low = op.left(cy)
         total = ground[p] + cx + cx_low + cy + cy_low
         if p + 1 < layers:
             total = total + op.via[p][...]
@@ -302,21 +284,132 @@
         op.diagonal[p][...] = total
         op.inverse[p][...] = jnp.where(inside, 1.0 / total, 0.0)
 
-    z = op.smooth([ref[...] for ref in op.weight])
+    lane = lanes_of((rows, LANES))
+    kept = (lane >= HALO) & (lane < LANES - HALO)
+    b = [ref[...] for ref in op.weight]
+    z = op.smooth(b)
     q = op.apply(z)
     u = op.smooth(q)
-    message[0:rows, :] = z[0][0:rows, 0:LANES]
-    message[rows : 2 * rows, :] = u[0][0:rows, 0:LANES]
-    b = [base[...]] + [None] * (layers - 1)
-    found = op.products([ref[...] for ref in op.weight], z, q, u)
+    front[0] = z[0][0:rows]
+    front[1] = u[0][0:rows]
+    found = op.products(b, z, q, u, kept)
+    b = [middle[...]] + [None] * (layers - 1)
     z = op.smooth(b)
     q = op.apply(z)
     u = op.smooth(q)
     for p in range(layers):
         if z[p] is not None:
-            zed[p] = z[p][0:rows, 0:LANES]
-        you[p] = u[p][0:rows, 0:LANES]
-    found = jnp.concatenate(op.products(b, z, q, u) + found, axis=0)
+            zed[p] = z[p][0:rows]
+        you[p] = u[p][0:rows]
+    sums[...] = jnp.concatenate(op.products(b, z, q, u, kept) + found, axis=0)
+
+    lane = lanes_of((ring, LANES))
+    grounds = [ground.at[p] for p in range(layers)]
+    for kind, refs_ in enumerate((op.cx, op.cy, op.via, grounds, op.weight, [middle])):
+        packed = jnp.zeros((ring, LANES), F32)
+        for p, ref in enumerate(refs_):
+            at = p * WINDOW
+            first = pltpu.roll(ref[...], at + HALO, 1)
+            last = pltpu.roll(ref[...], (at + WINDOW - HALO) % LANES, 1)
+            packed = jnp.where((lane >= at + HALO) & (lane < at + WINDOW // 2), first, packed)
+            packed = jnp.where((lane >= at + WINDOW // 2) & (lane < at + WINDOW - HALO), last, packed)
+        strips[kind] = packed
+
+
+def outer(layers, shape, refs):
+    strips, even, odd, front, zed_in, you_in, sums, message, zed, you, scalars, held = refs
+    rows, ring = shape
+    tx, ty = lax.axis_index("tx"), lax.axis_index("ty")
+    ty_even = lax.rem(ty, 2) == 0
+
+    depths = (layers, layers, layers - 1, layers, layers)
+    homes = [(kind, p) for kind, depth in enumerate(depths) for p in range(depth)]
+    tiles = [(kind, p, at) for kind, p in homes for at in range(0, rows, SUB)]
+    tiles += [(kind, p, at) for kind, p in homes for at in range(rows, ring, SUB)]
+    tiles += [(len(depths), 0, at) for at in range(0, ring, SUB)]
+    parts = {}
+    lane = lanes_of((SUB, LANES))
+    for j, (kind, p, at) in enumerate(tiles):
+        q, s = divmod(j, SLOTS)
+        one, two = even[q * SUB : (q + 1) * SUB, :], odd[q * SUB : (q + 1) * SUB, :]
+        after, before = jnp.where(ty_even, one, two), jnp.where(ty_even, two, one)
+        start = p * WINDOW
+        part = parts[kind, at] if (kind, at) in parts else strips[kind, at : at + SUB, :]
+        before = pltpu.roll(before, (start + HALO - HALO * s) % LANES, 1)
+        after = pltpu.roll(after, (start + WINDOW - HALO - HALO * s) % LANES, 1)
+        part = jnp.where((lane >= start) & (lane < start + HALO), before, part)
+        part = jnp.where((lane >= start + WINDOW - HALO) & (lane < start + WINDOW), after, part)
+        parts[kind, at] = part
+    for (kind, at), part in parts.items():
+        held[kind, at : at + SUB, :] = part
+    cx, cy, via, ground, weight, source = (held[kind] for kind in range(len(depths) + 1))
+
+    def below(v):
+        return pltpu.roll(v, ring - 1, 0)
+
+    def right(v):
+        return pltpu.roll(v, LANES - 1, 1)
+
+    def upper(v):
+        return pltpu.roll(v, LANES - WINDOW, 1)
+
+    row, lane = rows_of((ring, LANES)), lax.rem(lanes_of((ring, LANES)), WINDOW)
+    inside = (
+        ((row < rows) | (row >= rows + HALO) | (tx < lax.axis_size("tx") - 1))
+        & ((row < rows + HALO) | (tx > 0))
+        & ((lane < WINDOW - HALO) | (ty < lax.axis_size("ty") - 1))
+        & ((lane >= HALO) | (ty > 0))
+    )
+    cx_low = jnp.where((row == 0) & (tx == 0), 0.0, pltpu.roll(cx, 1, 0))
+    cy_low = jnp.where((lane == HALO) & (ty == 0), 0.0, pltpu.roll(cy, 1, 1))
+    via_low = pltpu.roll(via, WINDOW, 1)
+    diagonal = ground + cx + cx_low + cy + cy_low + via + via_low
+    inverse = jnp.where(inside, 1.0 / diagonal, 0.0)
+
+    def couple(v):
+        return (
+            cx * below(v)
+            + cx_low * pltpu.roll(v, 1, 0)
+            + cy * right(v)
+            + cy_low * pltpu.roll(v, 1, 1)
+            + via * upper(v)
+            + via_low * pltpu.roll(v, WINDOW, 1)
+        )
+
+    def smooth(b):
+        return inverse * (b + couple(inverse * b))
+
+    near = lane[0:rows]
+    near = ((near >= HALO) & (near < 2 * HALO)) | (
+        (near >= WINDOW - 2 * HALO) & (near < WINDOW - HALO)
+    )
+    column = lanes_of((rows, LANES))
+
+    def whole(middle_part, side, p):
+        first = pltpu.roll(side[0:rows], (LANES - HALO - p * WINDOW) % LANES, 1)
+        last = pltpu.roll(side[0:rows], (LANES + HALO - (p + 1) * WINDOW) % LANES, 1)
+        return jnp.where(
+            column < HALO, first, jnp.where(column >= LANES - HALO, last, middle_part)
+        )
+
+    found = []
+    for which, b in enumerate((source, weight)):
+        z = smooth(b)
+        q = diagonal * z - couple(z)
+        u = smooth(q)
+        flow = diagonal * u - 2.0 * (cx * below(u) + cy * right(u) + via * upper(u))
+        for one, two in ((b, z), (z, q), (q, u), (u, flow)):
+            term = jnp.where(near, one[0:rows] * two[0:rows], 0.0)
+            found.append(jnp.sum(term, axis=0, keepdims=True))
+        if which == 0:
+            for p in range(layers):
+                if p < zed.shape[0]:
+                    zed[p] = whole(zed_in[p], z, p)
+                you[p] = whole(you_in[p], u, p)
+        else:
+            message[0:rows, :] = whole(front[0], z, 0)
+            message[rows : 2 * rows, :] = whole(front[1], u, 0)
+    found = sums[...] + jnp.concatenate(found, axis=0)
     scalars[...] = found
     message[2 * rows :, :] = found
 
@@ -427,21 +520,21 @@
         (held, own, *in_turn(got, ROW_TURNS)),
     )
     even, odd = exchange(sends, "ty")
-    width2 = 2 * LANES
+    results = (array(min(2, layers), rows, LANES), array(layers, rows, LANES), array(SUB, LANES))
+    front, zed, you, total, strips = call(
+        lambda *refs: inner(layers, shape, refs),
+        (array(2, rows, LANES), *results, array(6, ring, LANES)),
+        (held, rims, middle),
+        scratch=[
+            pltpu.VMEM((8 * layers - 1, ring, LANES), F32),
+            pltpu.VMEM((layers, ring, LANES), F32),
+        ],
+    )
     message, zed, you, total = call(
-        lambda *refs: solve(layers, shape, refs),
-        (
-            array(2 * rows + SUB, LANES),
-            array(min(2, layers), rows, LANES),
-            array(layers, rows, LANES),
-            array(SUB, LANES),
-        ),
-        (held, rims, middle, even, odd),
-        scratch=[
-            pltpu.VMEM((8 * layers - 1, ring, width2), F32),
-            pltpu.VMEM((ring, width2), F32),
-            pltpu.VMEM((layers, ring, width2), F32),
-        ],
+        lambda *refs: outer(layers, shape, refs),
+        (array(2 * rows + SUB, LANES), *results),
+        (strips, even, odd, front, zed, you, total),
+        scratch=[pltpu.VMEM((6, ring, LANES), F32)],
     )
     got = exchange([message] * (count - 1), "tx")
     ahead = exchange([total] * (count - 1), "tx")[2:]

time: 32.5 us -> 31.7 us (0.975)
  waiting for transfers between devices: 9.14 us -> 7.83 us
  Pallas kernels: 5.28 us -> 5.79 us
    ppermute x12, waiting for transfers between devices: 9.14 us -> 7.83 us  [exchange(): lax.ppermute(value, axis, list(enumerate(target)))]
    pallas_call x6 -> x7, Pallas kernels: 5.28 us -> 5.79 us  [call(): pl.pallas_call(kernel, out_shape=tuple(outs), in_specs=specs or [vmem() f...]
  transfers between devices with their start and end apart: 12 -> 12, of which waited for: 6 -> 6; matrix products, arithmetic and copies ran while one was open for 0% -> 0% of each run, Pallas kernels for 3% -> 7%
where the time goes in v5:
time: 31.7 us; the launch traced here: 31.5 us
  starting transfers between devices  16.5 us (52%)
  waiting for transfers between devices  7.83 us (25%)
  Pallas kernels  5.79 us (18%)
  between operations  1.34 us (4%)
    ppermute x12, starting transfers between devices, exchange(): lax.ppermute(value, axis, list(enumerate(target)))  16.5 us
    ppermute x12, waiting for transfers between devices, exchange(): lax.ppermute(value, axis, list(enumerate(target)))  7.83 us
    pallas_call x7, Pallas kernels, call(): pl.pallas_call(kernel, out_shape=tuple(outs), in_specs=specs or [vmem() f...  5.79 us
  transfers between devices with their start and end apart: 12, of which 6 were waited for; matrix products, arithmetic and copies ran while one was open for 0% of the time, Pallas kernels for 7%

profile of v5, /device:TPU:0, one launch (start us, length us, event | category | flops | bytes accessed | tf_op | source)
XLA Modules:
  0.0 31.5 jit_solution(6684950860104020909)
XLA Ops:
  1.3 1.5 %shard_map.95 = (f32[19,64,128]{2,1,0:T(8,128)S(1)}, f32[72,128]{1,0:T(8,128)S(1)}, s32[1,512]{1,0:T(1,128)S(1)}, f32[152,128]{1,0:T(8,128)S(1)}, f32[152,128]{1,0:T(8,128)S(1)}, /*index=5*/f32[72,128]{1,0:T(8,128)S(1)}) custom-call(f32[4,64,128]{2,1,0:T(8,128)} %refs_0_.1, f32[4,64,128]{2,1,0:T(8,128)} %refs_1_.1, f32[3,64,128]{2,1,0:T(8,128)} %refs_2_.1, ...), custom_call_target="tpu_custom_call" | custom-call | bytes 1740804 | tf_op jit(solution)/shard_map/pallas_call | solution.py:456
  2.8 5.1 %collective-permute-start = (f32[152,128]{1,0:T(8,128)S(1)}, f32[152,128]{1,0:T(8,128)S(1)}, u32[]{:S(2)}, u32[]{:S(2)}) collective-permute-start(f32[152,128]{1,0:T(8,128)S(1)} %get-tuple-element.23), channel_id=1, source_target_pairs={{0,12},{4,8},{8,4},{12,0},{1,13},{5,9},{9,5},{13,1},{2,14},{6,10},... | collective-permute-start | bytes 233480 | tf_op jit(solution)/shard_map/ppermute | solution.py:470
  7.9 0.0 collective-permute-start.1
  7.9 0.6 %collective-permute-start.2 = (f32[72,128]{1,0:T(8,128)S(1)}, f32[72,128]{1,0:T(8,128)S(1)}, u32[]{:S(2)}, u32[]{:S(2)}) collective-permute-start(f32[72,128]{1,0:T(8,128)S(1)} %get-tuple-element.25), channel_id=1, source_target_pairs={{0,8},{4,12},{8,0},{12,4},{1,9},{5,13},{9,1},{13,5},{2,10},{6,14},... | collective-permute-start | bytes 110600 | tf_op jit(solution)/shard_map/ppermute | solution.py:470
  8.5 4.5 %collective-permute-done.2.refs_4_ = f32[72,128]{1,0:T(8,128)S(1)} collective-permute-done((f32[72,128]{1,0:T(8,128)S(1)}, f32[72,128]{1,0:T(8,128)S(1)}, u32[]{:S(2)}, u32[]{:S(2)}) %collective-permute-start.2) | collective-permute-done | bytes 36896 | tf_op jit(solution)/shard_map/ppermute | solution.py:470
  13.0 0.0 collective-permute-done.refs_2_
  13.0 0.0 collective-permute-done.1.refs_3_
  13.0 0.3 shard_map.96
  13.2 0.1 collective-permute-start.3
  13.3 1.7 %collective-permute-start.4 = (f32[48,128]{1,0:T(8,128)S(1)}, f32[48,128]{1,0:T(8,128)S(1)}, u32[]{:S(2)}, u32[]{:S(2)}) collective-permute-start(f32[48,128]{1,0:T(8,128)S(1)} %get-tuple-element.30), channel_id=1, source_target_pairs={{0,3},{1,2},{2,1},{3,0},{4,7},{5,6},{6,5},{7,4},{8,11},{9,10},{10,... | collective-permute-start | bytes 73736 | tf_op jit(solution)/shard_map/ppermute | solution.py:470
  15.1 1.3 %shard_map.97 = (f32[2,64,128]{2,1,0:T(8,128)S(1)}, f32[2,64,128]{2,1,0:T(8,128)S(1)}, f32[4,64,128]{2,1,0:T(8,128)S(1)}, f32[8,128]{1,0:T(8,128)S(1)}, f32[6,72,128]{2,1,0:T(8,128)S(1)}) custom-call(f32[19,64,128]{2,1,0:T(8,128)S(1)} %get-tuple-element.21.refs_0_, f32[19,8,128]{2,1,0:T(8,128)S(1)} %get-tuple-element.26.refs_1_, ...), custom_call_target="tpu_custom_call" | custom-call | bytes 1224704 | tf_op jit(solution)/shard_map/pallas_call | solution.py:456
  16.4 0.0 collective-permute-done.3.refs_1_
  16.4 0.3 collective-permute-done.4.refs_2_
  16.6 1.0 %shard_map.98 = (f32[136,128]{1,0:T(8,128)S(1)}, f32[2,64,128]{2,1,0:T(8,128)S(1)}, f32[4,64,128]{2,1,0:T(8,128)S(1)}, f32[8,128]{1,0:T(8,128)S(1)}) custom-call(f32[6,72,128]{2,1,0:T(8,128)S(1)} %get-tuple-element.28.refs_0_, f32[48,128]{1,0:T(8,128)S(1)} %collective-permute-done.3.refs_1_, f32[48,128]{1,0:T(8,128)S(1)} %collective-permute-done.4.refs_2_, ...), custom_call_target="tpu_custom_call" | custom-call | bytes 806912 | tf_op jit(solution)/shard_map/pallas_call | solution.py:456
  17.6 1.8 %collective-permute-start.5 = (f32[136,128]{1,0:T(8,128)S(1)}, f32[136,128]{1,0:T(8,128)S(1)}, u32[]{:S(2)}, u32[]{:S(2)}) collective-permute-start(f32[136,128]{1,0:T(8,128)S(1)} %get-tuple-element.36.refs_4_), channel_id=1, source_target_pairs={{0,4},{4,0},{8,12},{12,8},{1,5},{5,1},{9,13},{13,9},{2,6},{6,2},{1... | collective-permute-start | bytes 208904 | tf_op jit(solution)/shard_map/ppermute | solution.py:470
  19.5 2.0 %collective-permute-start.6 = (f32[136,128]{1,0:T(8,128)S(1)}, f32[136,128]{1,0:T(8,128)S(1)}, u32[]{:S(2)}, u32[]{:S(2)}) collective-permute-start(f32[136,128]{1,0:T(8,128)S(1)} %get-tuple-element.36.refs_4_), channel_id=1, source_target_pairs={{0,12},{4,8},{8,4},{12,0},{1,13},{5,9},{9,5},{13,1},{2,14},{6,10},... | collective-permute-start | bytes 208904 | tf_op jit(solution)/shard_map/ppermute | solution.py:470
  21.5 0.0 collective-permute-start.7
  21.5 2.9 %collective-permute-start.11 = (f32[136,128]{1,0:T(8,128)S(1)}, f32[136,128]{1,0:T(8,128)S(1)}, u32[]{:S(2)}, u32[]{:S(2)}) collective-permute-start(f32[136,128]{1,0:T(8,128)S(1)} %get-tuple-element.36.refs_4_), channel_id=1, source_target_pairs={{0,8},{4,12},{8,0},{12,4},{1,9},{5,13},{9,1},{13,5},{2,10},{6,14},... | collective-permute-start | bytes 208904 | tf_op jit(solution)/shard_map/ppermute | solution.py:470
  24.4 1.6 %collective-permute-done.7 = f32[8,128]{1,0:T(8,128)S(1)} collective-permute-done((f32[8,128]{1,0:T(8,128)S(1)}, f32[8,128]{1,0:T(8,128)S(1)}, u32[]{:S(2)}, u32[]{:S(2)}) %collective-permute-start.7) | collective-permute-done | bytes 4128 | tf_op jit(solution)/shard_map/ppermute | solution.py:470
  26.0 0.0 collective-permute-done.5.refs_2_
  26.0 0.0 collective-permute-done.6.refs_1_
  26.0 1.6 %collective-permute-start.10 = (f32[8,128]{1,0:T(8,128)S(1)}, f32[8,128]{1,0:T(8,128)S(1)}, u32[]{:S(2)}, u32[]{:S(2)}) collective-permute-start(f32[8,128]{1,0:T(8,128)S(1)} %fusion.refs_0_), channel_id=1, source_target_pairs={{0,2},{1,3},{2,0},{3,1},{4,6},{5,7},{6,4},{7,5},{8,10},{9,11},{10,... | collective-permute-start | bytes 12296 | tf_op jit(solution)/shard_map/ppermute | solution.py:470
  27.6 0.0 collective-permute-start.8
  27.6 0.7 %collective-permute-start.9 = (f32[8,128]{1,0:T(8,128)S(1)}, f32[8,128]{1,0:T(8,128)S(1)}, u32[]{:S(2)}, u32[]{:S(2)}) collective-permute-start(f32[8,128]{1,0:T(8,128)S(1)} %fusion.refs_0_), channel_id=1, source_target_pairs={{0,3},{1,2},{2,1},{3,0},{4,7},{5,6},{6,5},{7,4},{8,11},{9,10},{10,... | collective-permute-start | bytes 12296 | tf_op jit(solution)/shard_map/ppermute | solution.py:470
  28.3 0.4 %shard_map.99.refs_0_ = bf16[512,256]{1,0:T(8,128)(2,1)S(1)} custom-call(s32[1,512]{1,0:T(1,128)S(1)} %get-tuple-element.39.home), custom_call_target="tpu_custom_call" | custom-call | bytes 264192 | tf_op jit(solution)/shard_map/pallas_call | solution.py:456
  28.6 0.1 collective-permute-done.11.refs_3_
  28.7 0.6 %shard_map.100.refs_6_ = f32[512,256]{1,0:T(8,128)S(1)} custom-call(bf16[512,256]{1,0:T(8,128)(2,1)S(1)} %shard_map.99.refs_0_, f32[136,128]{1,0:T(8,128)S(1)} %collective-permute-done.6.refs_1_, f32[136,128]{1,0:T(8,128)S(1)} %collective-permute-done.5.refs_2_, f32[136,128]{1,0:T(8,128)S(1)} %collective-permute-done.11.refs_3_, ...), custom_call_target="tpu_custom_call" | custom-call | bytes 1064960 | tf_op jit(solution)/shard_map/pallas_call | solution.py:456
  29.3 0.5 %collective-permute-done.10.refs_3_ = f32[8,128]{1,0:T(8,128)S(1)} collective-permute-done((f32[8,128]{1,0:T(8,128)S(1)}, f32[8,128]{1,0:T(8,128)S(1)}, u32[]{:S(2)}, u32[]{:S(2)}) %collective-permute-start.10) | collective-permute-done | bytes 4128 | tf_op jit(solution)/shard_map/ppermute | solution.py:470
  29.7 0.0 collective-permute-done.8.refs_1_
  29.7 0.9 %collective-permute-done.9.refs_2_ = f32[8,128]{1,0:T(8,128)S(1)} collective-permute-done((f32[8,128]{1,0:T(8,128)S(1)}, f32[8,128]{1,0:T(8,128)S(1)}, u32[]{:S(2)}, u32[]{:S(2)}) %collective-permute-start.9) | collective-permute-done | bytes 4128 | tf_op jit(solution)/shard_map/ppermute | solution.py:470
  30.6 0.9 %shard_map.101 = (f32[4,64,128]{2,1,0:T(8,128)}, f32[512,128]{1,0:T(8,128)}) custom-call(f32[8,128]{1,0:T(8,128)S(1)} %fusion.refs_0_, f32[8,128]{1,0:T(8,128)S(1)} %collective-permute-done.8.refs_1_, f32[8,128]{1,0:T(8,128)S(1)} %collective-permute-done.9.refs_2_, f32[8,128]{1,0:T(8,128)S(1)} %collective-permute-done.10.refs_3_, ...), custom_call_target="tpu_custom_call" | custom-call | bytes 1130496 | tf_op jit(solution)/shard_map/pallas_call | solution.py:456
  (1 shorter events, 0.0 us)
Async XLA Ops:
  2.8 10.2 %collective-permute-start = (f32[152,128]{1,0:T(8,128)S(1)}, f32[152,128]{1,0:T(8,128)S(1)}, u32[]{:S(2)}, u32[]{:S(2)}) collective-permute-start(f32[152,128]{1,0:T(8,128)S(1)} %get-tuple-element.23), channel_id=1, source_target_pairs={{0,12},{4,8},{8,4},{12,0},{1,13},{5,9},{9,5},{13,1},{2,14},{6,10},... | collective-permute-start | bytes 233480 | tf_op jit(solution)/shard_map/ppermute | solution.py:470
  7.9 5.1 %collective-permute-start.1 = (f32[152,128]{1,0:T(8,128)S(1)}, f32[152,128]{1,0:T(8,128)S(1)}, u32[]{:S(2)}, u32[]{:S(2)}) collective-permute-start(f32[152,128]{1,0:T(8,128)S(1)} %get-tuple-element.24), channel_id=1, source_target_pairs={{0,4},{4,0},{8,12},{12,8},{1,5},{5,1},{9,13},{13,9},{2,6},{6,2},{1... | collective-permute-start | bytes 233480 | tf_op jit(solution)/shard_map/ppermute | solution.py:470
  7.9 5.1 %collective-permute-start.2 = (f32[72,128]{1,0:T(8,128)S(1)}, f32[72,128]{1,0:T(8,128)S(1)}, u32[]{:S(2)}, u32[]{:S(2)}) collective-permute-start(f32[72,128]{1,0:T(8,128)S(1)} %get-tuple-element.25), channel_id=1, source_target_pairs={{0,8},{4,12},{8,0},{12,4},{1,9},{5,13},{9,1},{13,5},{2,10},{6,14},... | collective-permute-start | bytes 110600 | tf_op jit(solution)/shard_map/ppermute | solution.py:470
  13.2 3.1 %collective-permute-start.3 = (f32[48,128]{1,0:T(8,128)S(1)}, f32[48,128]{1,0:T(8,128)S(1)}, u32[]{:S(2)}, u32[]{:S(2)}) collective-permute-start(f32[48,128]{1,0:T(8,128)S(1)} %get-tuple-element.29), channel_id=1, source_target_pairs={{0,1},{1,0},{2,3},{3,2},{4,5},{5,4},{6,7},{7,6},{8,9},{9,8},{10,11... | collective-permute-start | bytes 73736 | tf_op jit(solution)/shard_map/ppermute | solution.py:470
  13.3 3.3 %collective-permute-start.4 = (f32[48,128]{1,0:T(8,128)S(1)}, f32[48,128]{1,0:T(8,128)S(1)}, u32[]{:S(2)}, u32[]{:S(2)}) collective-permute-start(f32[48,128]{1,0:T(8,128)S(1)} %get-tuple-element.30), channel_id=1, source_target_pairs={{0,3},{1,2},{2,1},{3,0},{4,7},{5,6},{6,5},{7,4},{8,11},{9,10},{10,... | collective-permute-start | bytes 73736 | tf_op jit(solution)/shard_map/ppermute | solution.py:470
  17.6 8.4 %collective-permute-start.5 = (f32[136,128]{1,0:T(8,128)S(1)}, f32[136,128]{1,0:T(8,128)S(1)}, u32[]{:S(2)}, u32[]{:S(2)}) collective-permute-start(f32[136,128]{1,0:T(8,128)S(1)} %get-tuple-element.36.refs_4_), channel_id=1, source_target_pairs={{0,4},{4,0},{8,12},{12,8},{1,5},{5,1},{9,13},{13,9},{2,6},{6,2},{1... | collective-permute-start | bytes 208904 | tf_op jit(solution)/shard_map/ppermute | solution.py:470
  19.5 6.6 %collective-permute-start.6 = (f32[136,128]{1,0:T(8,128)S(1)}, f32[136,128]{1,0:T(8,128)S(1)}, u32[]{:S(2)}, u32[]{:S(2)}) collective-permute-start(f32[136,128]{1,0:T(8,128)S(1)} %get-tuple-element.36.refs_4_), channel_id=1, source_target_pairs={{0,12},{4,8},{8,4},{12,0},{1,13},{5,9},{9,5},{13,1},{2,14},{6,10},... | collective-permute-start | bytes 208904 | tf_op jit(solution)/shard_map/ppermute | solution.py:470
  21.5 4.5 %collective-permute-start.7 = (f32[8,128]{1,0:T(8,128)S(1)}, f32[8,128]{1,0:T(8,128)S(1)}, u32[]{:S(2)}, u32[]{:S(2)}) collective-permute-start(f32[8,128]{1,0:T(8,128)S(1)} %get-tuple-element.35), channel_id=1, source_target_pairs={{0,8},{4,12},{8,0},{12,4},{1,9},{5,13},{9,1},{13,5},{2,10},{6,14},... | collective-permute-start | bytes 12296 | tf_op jit(solution)/shard_map/ppermute | solution.py:470
  21.5 7.2 %collective-permute-start.11 = (f32[136,128]{1,0:T(8,128)S(1)}, f32[136,128]{1,0:T(8,128)S(1)}, u32[]{:S(2)}, u32[]{:S(2)}) collective-permute-start(f32[136,128]{1,0:T(8,128)S(1)} %get-tuple-element.36.refs_4_), channel_id=1, source_target_pairs={{0,8},{4,12},{8,0},{12,4},{1,9},{5,13},{9,1},{13,5},{2,10},{6,14},... | collective-permute-start | bytes 208904 | tf_op jit(solution)/shard_map/ppermute | solution.py:470
  26.0 3.7 %collective-permute-start.10 = (f32[8,128]{1,0:T(8,128)S(1)}, f32[8,128]{1,0:T(8,128)S(1)}, u32[]{:S(2)}, u32[]{:S(2)}) collective-permute-start(f32[8,128]{1,0:T(8,128)S(1)} %fusion.refs_0_), channel_id=1, source_target_pairs={{0,2},{1,3},{2,0},{3,1},{4,6},{5,7},{6,4},{7,5},{8,10},{9,11},{10,... | collective-permute-start | bytes 12296 | tf_op jit(solution)/shard_map/ppermute | solution.py:470
  27.6 2.1 %collective-permute-start.8 = (f32[8,128]{1,0:T(8,128)S(1)}, f32[8,128]{1,0:T(8,128)S(1)}, u32[]{:S(2)}, u32[]{:S(2)}) collective-permute-start(f32[8,128]{1,0:T(8,128)S(1)} %fusion.refs_0_), channel_id=1, source_target_pairs={{0,1},{1,0},{2,3},{3,2},{4,5},{5,4},{6,7},{7,6},{8,9},{9,8},{10,11... | collective-permute-start | bytes 12296 | tf_op jit(solution)/shard_map/ppermute | solution.py:470
  27.6 3.0 %collective-permute-start.9 = (f32[8,128]{1,0:T(8,128)S(1)}, f32[8,128]{1,0:T(8,128)S(1)}, u32[]{:S(2)}, u32[]{:S(2)}) collective-permute-start(f32[8,128]{1,0:T(8,128)S(1)} %fusion.refs_0_), channel_id=1, source_target_pairs={{0,3},{1,2},{2,1},{3,0},{4,7},{5,6},{6,5},{7,4},{8,11},{9,10},{10,... | collective-permute-start | bytes 12296 | tf_op jit(solution)/shard_map/ppermute | solution.py:470

commit v6 on v5

--- a/solution.py
+++ b/solution.py
@@ -12,6 +12,7 @@
 LANES = 128
 SLOTS = LANES // HALO
 WINDOW = 8 * HALO
+SHARE = WINDOW // HALO
 F32 = jnp.float32
 BF16 = jnp.bfloat16
 ROW_TURNS = (1, 0, 2)
@@ -26,17 +27,14 @@
     return lax.broadcasted_iota(jnp.int32, shape, len(shape) - 2)
 
 
-def tiles_of(refs):
-    found = []
-    for ref in refs:
-        rows = ref.shape[-2]
-        for plane in range(ref.shape[0] if len(ref.shape) == 3 else 1):
-            for at in range(0, rows, SUB):
-                if len(ref.shape) == 3:
-                    found.append((ref, (plane, slice(at, at + SUB), slice(None))))
-                else:
-                    found.append((ref, (slice(at, at + SUB), slice(None))))
-    return found
+def strip_kinds(layers):
+    depths = (layers, layers, layers - 1, layers, layers)
+    return [(sum(depths[:k]), depth) for k, depth in enumerate(depths)] + [(None, 1)]
+
+
+def strip_tiles(layers, ring):
+    groups = [(*kind, at) for kind in strip_kinds(layers) for at in range(0, ring, SUB)]
+    return [(k // SHARE * SUB, groups[k : k + SHARE]) for k in range(0, len(groups), SHARE)]
 
 
 def three_parts(value):
@@ -105,7 +103,8 @@
     hot = picker[...].astype(BF16)
     fetch_cell.wait()
     high, middle, low = three_parts(cell[...])
-    sums = dot(hot, high) + dot(hot, middle) + dot(hot, low)
+    wide = dot(hot, jnp.concatenate([high, middle, low], axis=1))
+    sums = wide[:, 0:LANES] + wide[:, LANES : 2 * LANES] + wide[:, 2 * LANES :]
     own[...] = sums[0:ring]
     for k, send in enumerate(sends):
         send[0:ring, :] = sums[(k + 1) * ring : (k + 2) * ring]
@@ -133,7 +132,7 @@
         chooser[:, k * rows : (k + 1) * rows] = hot.T.astype(BF16)
 
 
-def columns(count, shape, refs):
+def columns(count, layers, shape, refs):
     planes, own = refs[:2]
     got = in_turn(refs[2 : 2 + count - 1], ROW_TURNS, True)
     base, rims, send_even, send_odd = refs[2 + count - 1 :]
@@ -156,17 +155,23 @@
             rims[p + 1] = pltpu.roll(jnp.where(lower, before, after), HALO, 0)
 
     slot = lanes_of((SUB, LANES)) // HALO
-    tiles = tiles_of((planes, rims, base))
-    for first in range(0, len(tiles), SLOTS):
+    for q, members in strip_tiles(layers, ring):
         left = jnp.zeros((SUB, LANES), F32)
         right = left
-        for s, (ref, index) in enumerate(tiles[first : first + SLOTS]):
-            turned = pltpu.roll(ref[index], HALO * s, 1) if s else ref[index]
-            left = jnp.where(slot == s, turned, left)
-            right = jnp.where(slot == (s - 1) % SLOTS, turned, right)
-        at = first // SLOTS * SUB
-        send_even[at : at + SUB, :] = jnp.where(ty_even, right, left)
-        send_odd[at : at + SUB, :] = jnp.where(ty_even, left, right)
+        for k, (first, depth, at) in enumerate(members):
+            for p in range(depth):
+                if first is None:
+                    tile = base[at : at + SUB, :]
+                elif at < rows:
+                    tile = planes[first + p, at : at + SUB, :]
+                else:
+                    tile = rims[first + p]
+                s = p * SHARE + k
+                turned = pltpu.roll(tile, HALO * s, 1) if s else tile
+                left = jnp.where(slot == s, turned, left)
+                right = jnp.where(slot == (s - 1) % SLOTS, turned, right)
+        send_even[q : q + SUB, :] = jnp.where(ty_even, right, left)
+        send_odd[q : q + SUB, :] = jnp.where(ty_even, left, right)
 
 
 class Grid:
@@ -322,27 +327,18 @@
     tx, ty = lax.axis_index("tx"), lax.axis_index("ty")
     ty_even = lax.rem(ty, 2) == 0
 
-    depths = (layers, layers, layers - 1, layers, layers)
-    homes = [(kind, p) for kind, depth in enumerate(depths) for p in range(depth)]
-    tiles = [(kind, p, at) for kind, p in homes for at in range(0, rows, SUB)]
-    tiles += [(kind, p, at) for kind, p in homes for at in range(rows, ring, SUB)]
-    tiles += [(len(depths), 0, at) for at in range(0, ring, SUB)]
-    parts = {}
-    lane = lanes_of((SUB, LANES))
-    for j, (kind, p, at) in enumerate(tiles):
-        q, s = divmod(j, SLOTS)
-        one, two = even[q * SUB : (q + 1) * SUB, :], odd[q * SUB : (q + 1) * SUB, :]
+    kinds = strip_kinds(layers)
+    lane = lax.rem(lanes_of((SUB, LANES)), WINDOW)
+    for q, members in strip_tiles(layers, ring):
+        one, two = even[q : q + SUB, :], odd[q : q + SUB, :]
         after, before = jnp.where(ty_even, one, two), jnp.where(ty_even, two, one)
-        start = p * WINDOW
-        part = parts[kind, at] if (kind, at) in parts else strips[kind, at : at + SUB, :]
-        before = pltpu.roll(before, (start + HALO - HALO * s) % LANES, 1)
-        after = pltpu.roll(after, (start + WINDOW - HALO - HALO * s) % LANES, 1)
-        part = jnp.where((lane >= start) & (lane < start + HALO), before, part)
-        part = jnp.where((lane >= start + WINDOW - HALO) & (lane < start + WINDOW), after, part)
-        parts[kind, at] = part
-    for (kind, at), part in parts.items():
-        held[kind, at : at + SUB, :] = part
-    cx, cy, via, ground, weight, source = (held[kind] for kind in range(len(depths) + 1))
+        for k, (first, depth, at) in enumerate(members):
+            kind = kinds.index((first, depth))
+            part = strips[kind, at : at + SUB, :]
+            part = jnp.where(lane < HALO, pltpu.roll(before, (HALO - HALO * k) % LANES, 1), part)
+            turned = pltpu.roll(after, (WINDOW - HALO - HALO * k) % LANES, 1)
+            held[kind, at : at + SUB, :] = jnp.where(lane >= WINDOW - HALO, turned, part)
+    cx, cy, via, ground, weight, source = (held[kind] for kind in range(len(kinds)))
 
     def below(v):
         return pltpu.roll(v, ring - 1, 0)
@@ -513,9 +509,9 @@
         (array(blocks, count * rows, dtype=BF16),),
         (home,),
     )
-    packed = array(pl.cdiv(planes * (rows // SUB + 1) + ring // SUB, SLOTS) * SUB, LANES)
+    packed = array(strip_tiles(layers, ring)[-1][0] + SUB, LANES)
     middle, rims, *sends = call(
-        lambda *refs: columns(count, shape, refs),
+        lambda *refs: columns(count, layers, shape, refs),
         (array(ring, LANES), array(planes, SUB, LANES), packed, packed),
         (held, own, *in_turn(got, ROW_TURNS)),
     )
@@ -538,7 +534,7 @@
     )
     got = exchange([message] * (count - 1), "tx")
     ahead = exchange([total] * (count - 1), "tx")[2:]
-    total = functools.reduce(jnp.add, [total] + [m[2 * rows :] for m in got[:2]] + ahead)
+    total = functools.reduce(jnp.add, ahead + [m[2 * rows :] for m in got[1::-1]] + [total])
     messages = in_turn(got, DATA_TURNS) + [message]
     totals = [total] + exchange([total] * (ways - 1), "ty")
     (chosen,) = call(

time: 31.7 us -> 31.6 us (level)
  no operation moved by 1% of the time
where the time goes in v6:
time: 31.6 us; the launch traced here: 31.4 us
  starting transfers between devices  16.5 us (52%)
  waiting for transfers between devices  7.89 us (25%)
  Pallas kernels  5.62 us (18%)
  between operations  1.34 us (4%)
    ppermute x12, starting transfers between devices, exchange(): lax.ppermute(value, axis, list(enumerate(target)))  16.5 us
    ppermute x12, waiting for transfers between devices, exchange(): lax.ppermute(value, axis, list(enumerate(target)))  7.89 us
    pallas_call x7, Pallas kernels, call(): pl.pallas_call(kernel, out_shape=tuple(outs), in_specs=specs or [vmem() f...  5.62 us
  transfers between devices with their start and end apart: 12, of which 6 were waited for; matrix products, arithmetic and copies ran while one was open for 0% of the time, Pallas kernels for 7%

profile of v6, /device:TPU:0, one launch (start us, length us, event | category | flops | bytes accessed | tf_op | source)
XLA Modules:
  0.0 31.4 jit_solution(12266003689734902653)
XLA Ops:
  1.3 1.4 %shard_map.95 = (f32[19,64,128]{2,1,0:T(8,128)S(1)}, f32[72,128]{1,0:T(8,128)S(1)}, s32[1,512]{1,0:T(1,128)S(1)}, f32[152,128]{1,0:T(8,128)S(1)}, f32[152,128]{1,0:T(8,128)S(1)}, /*index=5*/f32[72,128]{1,0:T(8,128)S(1)}) custom-call(f32[4,64,128]{2,1,0:T(8,128)} %refs_0_.1, f32[4,64,128]{2,1,0:T(8,128)} %refs_1_.1, f32[3,64,128]{2,1,0:T(8,128)} %refs_2_.1, ...), custom_call_target="tpu_custom_call" | custom-call | bytes 1740804 | tf_op jit(solution)/shard_map/pallas_call | solution.py:452
  2.7 5.1 %collective-permute-start = (f32[152,128]{1,0:T(8,128)S(1)}, f32[152,128]{1,0:T(8,128)S(1)}, u32[]{:S(2)}, u32[]{:S(2)}) collective-permute-start(f32[152,128]{1,0:T(8,128)S(1)} %get-tuple-element.23), channel_id=1, source_target_pairs={{0,12},{4,8},{8,4},{12,0},{1,13},{5,9},{9,5},{13,1},{2,14},{6,10},... | collective-permute-start | bytes 233480 | tf_op jit(solution)/shard_map/ppermute | solution.py:466
  7.8 0.0 collective-permute-start.1
  7.8 0.6 %collective-permute-start.2 = (f32[72,128]{1,0:T(8,128)S(1)}, f32[72,128]{1,0:T(8,128)S(1)}, u32[]{:S(2)}, u32[]{:S(2)}) collective-permute-start(f32[72,128]{1,0:T(8,128)S(1)} %get-tuple-element.25), channel_id=1, source_target_pairs={{0,8},{4,12},{8,0},{12,4},{1,9},{5,13},{9,1},{13,5},{2,10},{6,14},... | collective-permute-start | bytes 110600 | tf_op jit(solution)/shard_map/ppermute | solution.py:466
  8.4 4.5 %collective-permute-done.2.refs_4_ = f32[72,128]{1,0:T(8,128)S(1)} collective-permute-done((f32[72,128]{1,0:T(8,128)S(1)}, f32[72,128]{1,0:T(8,128)S(1)}, u32[]{:S(2)}, u32[]{:S(2)}) %collective-permute-start.2) | collective-permute-done | bytes 36896 | tf_op jit(solution)/shard_map/ppermute | solution.py:466
  12.9 0.0 collective-permute-done.refs_2_
  12.9 0.0 collective-permute-done.1.refs_3_
  12.9 0.3 shard_map.96
  13.2 0.1 collective-permute-start.3
  13.2 1.7 %collective-permute-start.4 = (f32[56,128]{1,0:T(8,128)S(1)}, f32[56,128]{1,0:T(8,128)S(1)}, u32[]{:S(2)}, u32[]{:S(2)}) collective-permute-start(f32[56,128]{1,0:T(8,128)S(1)} %get-tuple-element.30), channel_id=1, source_target_pairs={{0,3},{1,2},{2,1},{3,0},{4,7},{5,6},{6,5},{7,4},{8,11},{9,10},{10,... | collective-permute-start | bytes 86024 | tf_op jit(solution)/shard_map/ppermute | solution.py:466
  15.0 1.3 %shard_map.97 = (f32[2,64,128]{2,1,0:T(8,128)S(1)}, f32[2,64,128]{2,1,0:T(8,128)S(1)}, f32[4,64,128]{2,1,0:T(8,128)S(1)}, f32[8,128]{1,0:T(8,128)S(1)}, f32[6,72,128]{2,1,0:T(8,128)S(1)}) custom-call(f32[19,64,128]{2,1,0:T(8,128)S(1)} %get-tuple-element.21.refs_0_, f32[19,8,128]{2,1,0:T(8,128)S(1)} %get-tuple-element.26.refs_1_, ...), custom_call_target="tpu_custom_call" | custom-call | bytes 1224704 | tf_op jit(solution)/shard_map/pallas_call | solution.py:452
  16.3 0.0 collective-permute-done.3.refs_1_
  16.3 0.3 %collective-permute-done.4.refs_2_ = f32[56,128]{1,0:T(8,128)S(1)} collective-permute-done((f32[56,128]{1,0:T(8,128)S(1)}, f32[56,128]{1,0:T(8,128)S(1)}, u32[]{:S(2)}, u32[]{:S(2)}) %collective-permute-start.4) | collective-permute-done | bytes 28704 | tf_op jit(solution)/shard_map/ppermute | solution.py:466
  16.6 0.9 %shard_map.98 = (f32[136,128]{1,0:T(8,128)S(1)}, f32[2,64,128]{2,1,0:T(8,128)S(1)}, f32[4,64,128]{2,1,0:T(8,128)S(1)}, f32[8,128]{1,0:T(8,128)S(1)}) custom-call(f32[6,72,128]{2,1,0:T(8,128)S(1)} %get-tuple-element.28.refs_0_, f32[56,128]{1,0:T(8,128)S(1)} %collective-permute-done.3.refs_1_, f32[56,128]{1,0:T(8,128)S(1)} %collective-permute-done.4.refs_2_, ...), custom_call_target="tpu_custom_call" | custom-call | bytes 815104 | tf_op jit(solution)/shard_map/pallas_call | solution.py:452
  17.5 1.8 %collective-permute-start.7 = (f32[136,128]{1,0:T(8,128)S(1)}, f32[136,128]{1,0:T(8,128)S(1)}, u32[]{:S(2)}, u32[]{:S(2)}) collective-permute-start(f32[136,128]{1,0:T(8,128)S(1)} %get-tuple-element.36.refs_4_), channel_id=1, source_target_pairs={{0,4},{4,0},{8,12},{12,8},{1,5},{5,1},{9,13},{13,9},{2,6},{6,2},{1... | collective-permute-start | bytes 208904 | tf_op jit(solution)/shard_map/ppermute | solution.py:466
  19.3 2.0 %collective-permute-start.6 = (f32[136,128]{1,0:T(8,128)S(1)}, f32[136,128]{1,0:T(8,128)S(1)}, u32[]{:S(2)}, u32[]{:S(2)}) collective-permute-start(f32[136,128]{1,0:T(8,128)S(1)} %get-tuple-element.36.refs_4_), channel_id=1, source_target_pairs={{0,12},{4,8},{8,4},{12,0},{1,13},{5,9},{9,5},{13,1},{2,14},{6,10},... | collective-permute-start | bytes 208904 | tf_op jit(solution)/shard_map/ppermute | solution.py:466
  21.4 0.0 collective-permute-start.5
  21.4 2.9 %collective-permute-start.11 = (f32[136,128]{1,0:T(8,128)S(1)}, f32[136,128]{1,0:T(8,128)S(1)}, u32[]{:S(2)}, u32[]{:S(2)}) collective-permute-start(f32[136,128]{1,0:T(8,128)S(1)} %get-tuple-element.36.refs_4_), channel_id=1, source_target_pairs={{0,8},{4,12},{8,0},{12,4},{1,9},{5,13},{9,1},{13,5},{2,10},{6,14},... | collective-permute-start | bytes 208904 | tf_op jit(solution)/shard_map/ppermute | solution.py:466
  24.3 1.6 %collective-permute-done.5 = f32[8,128]{1,0:T(8,128)S(1)} collective-permute-done((f32[8,128]{1,0:T(8,128)S(1)}, f32[8,128]{1,0:T(8,128)S(1)}, u32[]{:S(2)}, u32[]{:S(2)}) %collective-permute-start.5) | collective-permute-done | bytes 4128 | tf_op jit(solution)/shard_map/ppermute | solution.py:466
  25.9 0.0 collective-permute-done.7.refs_2_
  25.9 0.0 collective-permute-done.6.refs_1_
  25.9 1.6 %collective-permute-start.10 = (f32[8,128]{1,0:T(8,128)S(1)}, f32[8,128]{1,0:T(8,128)S(1)}, u32[]{:S(2)}, u32[]{:S(2)}) collective-permute-start(f32[8,128]{1,0:T(8,128)S(1)} %fusion.refs_0_), channel_id=1, source_target_pairs={{0,2},{1,3},{2,0},{3,1},{4,6},{5,7},{6,4},{7,5},{8,10},{9,11},{10,... | collective-permute-start | bytes 12296 | tf_op jit(solution)/shard_map/ppermute | solution.py:466
  27.5 0.0 collective-permute-start.9
  27.5 0.6 %collective-permute-start.8 = (f32[8,128]{1,0:T(8,128)S(1)}, f32[8,128]{1,0:T(8,128)S(1)}, u32[]{:S(2)}, u32[]{:S(2)}) collective-permute-start(f32[8,128]{1,0:T(8,128)S(1)} %fusion.refs_0_), channel_id=1, source_target_pairs={{0,1},{1,0},{2,3},{3,2},{4,5},{5,4},{6,7},{7,6},{8,9},{9,8},{10,11... | collective-permute-start | bytes 12296 | tf_op jit(solution)/shard_map/ppermute | solution.py:466
  28.1 0.4 %shard_map.99.refs_0_ = bf16[512,256]{1,0:T(8,128)(2,1)S(1)} custom-call(s32[1,512]{1,0:T(1,128)S(1)} %get-tuple-element.39.home), custom_call_target="tpu_custom_call" | custom-call | bytes 264192 | tf_op jit(solution)/shard_map/pallas_call | solution.py:452
  28.5 0.1 collective-permute-done.11.refs_3_
  28.6 0.6 %shard_map.100.refs_6_ = f32[512,256]{1,0:T(8,128)S(1)} custom-call(bf16[512,256]{1,0:T(8,128)(2,1)S(1)} %shard_map.99.refs_0_, f32[136,128]{1,0:T(8,128)S(1)} %collective-permute-done.6.refs_1_, f32[136,128]{1,0:T(8,128)S(1)} %collective-permute-done.7.refs_2_, f32[136,128]{1,0:T(8,128)S(1)} %collective-permute-done.11.refs_3_, ...), custom_call_target="tpu_custom_call" | custom-call | bytes 1064960 | tf_op jit(solution)/shard_map/pallas_call | solution.py:452
  29.2 0.5 %collective-permute-done.10.refs_3_ = f32[8,128]{1,0:T(8,128)S(1)} collective-permute-done((f32[8,128]{1,0:T(8,128)S(1)}, f32[8,128]{1,0:T(8,128)S(1)}, u32[]{:S(2)}, u32[]{:S(2)}) %collective-permute-start.10) | collective-permute-done | bytes 4128 | tf_op jit(solution)/shard_map/ppermute | solution.py:466
  29.6 0.9 %collective-permute-done.9.refs_2_ = f32[8,128]{1,0:T(8,128)S(1)} collective-permute-done((f32[8,128]{1,0:T(8,128)S(1)}, f32[8,128]{1,0:T(8,128)S(1)}, u32[]{:S(2)}, u32[]{:S(2)}) %collective-permute-start.9) | collective-permute-done | bytes 4128 | tf_op jit(solution)/shard_map/ppermute | solution.py:466
  30.5 0.0 collective-permute-done.8.refs_1_
  30.5 0.9 %shard_map.101 = (f32[4,64,128]{2,1,0:T(8,128)}, f32[512,128]{1,0:T(8,128)}) custom-call(f32[8,128]{1,0:T(8,128)S(1)} %fusion.refs_0_, f32[8,128]{1,0:T(8,128)S(1)} %collective-permute-done.8.refs_1_, f32[8,128]{1,0:T(8,128)S(1)} %collective-permute-done.9.refs_2_, f32[8,128]{1,0:T(8,128)S(1)} %collective-permute-done.10.refs_3_, ...), custom_call_target="tpu_custom_call" | custom-call | bytes 1130496 | tf_op jit(solution)/shard_map/pallas_call | solution.py:452
  (1 shorter events, 0.0 us)
Async XLA Ops:
  2.7 10.2 %collective-permute-start = (f32[152,128]{1,0:T(8,128)S(1)}, f32[152,128]{1,0:T(8,128)S(1)}, u32[]{:S(2)}, u32[]{:S(2)}) collective-permute-start(f32[152,128]{1,0:T(8,128)S(1)} %get-tuple-element.23), channel_id=1, source_target_pairs={{0,12},{4,8},{8,4},{12,0},{1,13},{5,9},{9,5},{13,1},{2,14},{6,10},... | collective-permute-start | bytes 233480 | tf_op jit(solution)/shard_map/ppermute | solution.py:466
  7.8 5.1 %collective-permute-start.1 = (f32[152,128]{1,0:T(8,128)S(1)}, f32[152,128]{1,0:T(8,128)S(1)}, u32[]{:S(2)}, u32[]{:S(2)}) collective-permute-start(f32[152,128]{1,0:T(8,128)S(1)} %get-tuple-element.24), channel_id=1, source_target_pairs={{0,4},{4,0},{8,12},{12,8},{1,5},{5,1},{9,13},{13,9},{2,6},{6,2},{1... | collective-permute-start | bytes 233480 | tf_op jit(solution)/shard_map/ppermute | solution.py:466
  7.8 5.1 %collective-permute-start.2 = (f32[72,128]{1,0:T(8,128)S(1)}, f32[72,128]{1,0:T(8,128)S(1)}, u32[]{:S(2)}, u32[]{:S(2)}) collective-permute-start(f32[72,128]{1,0:T(8,128)S(1)} %get-tuple-element.25), channel_id=1, source_target_pairs={{0,8},{4,12},{8,0},{12,4},{1,9},{5,13},{9,1},{13,5},{2,10},{6,14},... | collective-permute-start | bytes 110600 | tf_op jit(solution)/shard_map/ppermute | solution.py:466
  13.2 3.1 %collective-permute-start.3 = (f32[56,128]{1,0:T(8,128)S(1)}, f32[56,128]{1,0:T(8,128)S(1)}, u32[]{:S(2)}, u32[]{:S(2)}) collective-permute-start(f32[56,128]{1,0:T(8,128)S(1)} %get-tuple-element.29), channel_id=1, source_target_pairs={{0,1},{1,0},{2,3},{3,2},{4,5},{5,4},{6,7},{7,6},{8,9},{9,8},{10,11... | collective-permute-start | bytes 86024 | tf_op jit(solution)/shard_map/ppermute | solution.py:466
  13.2 3.4 %collective-permute-start.4 = (f32[56,128]{1,0:T(8,128)S(1)}, f32[56,128]{1,0:T(8,128)S(1)}, u32[]{:S(2)}, u32[]{:S(2)}) collective-permute-start(f32[56,128]{1,0:T(8,128)S(1)} %get-tuple-element.30), channel_id=1, source_target_pairs={{0,3},{1,2},{2,1},{3,0},{4,7},{5,6},{6,5},{7,4},{8,11},{9,10},{10,... | collective-permute-start | bytes 86024 | tf_op jit(solution)/shard_map/ppermute | solution.py:466
  17.5 8.4 %collective-permute-start.7 = (f32[136,128]{1,0:T(8,128)S(1)}, f32[136,128]{1,0:T(8,128)S(1)}, u32[]{:S(2)}, u32[]{:S(2)}) collective-permute-start(f32[136,128]{1,0:T(8,128)S(1)} %get-tuple-element.36.refs_4_), channel_id=1, source_target_pairs={{0,4},{4,0},{8,12},{12,8},{1,5},{5,1},{9,13},{13,9},{2,6},{6,2},{1... | collective-permute-start | bytes 208904 | tf_op jit(solution)/shard_map/ppermute | solution.py:466
  19.3 6.6 %collective-permute-start.6 = (f32[136,128]{1,0:T(8,128)S(1)}, f32[136,128]{1,0:T(8,128)S(1)}, u32[]{:S(2)}, u32[]{:S(2)}) collective-permute-start(f32[136,128]{1,0:T(8,128)S(1)} %get-tuple-element.36.refs_4_), channel_id=1, source_target_pairs={{0,12},{4,8},{8,4},{12,0},{1,13},{5,9},{9,5},{13,1},{2,14},{6,10},... | collective-permute-start | bytes 208904 | tf_op jit(solution)/shard_map/ppermute | solution.py:466
  21.4 4.5 %collective-permute-start.5 = (f32[8,128]{1,0:T(8,128)S(1)}, f32[8,128]{1,0:T(8,128)S(1)}, u32[]{:S(2)}, u32[]{:S(2)}) collective-permute-start(f32[8,128]{1,0:T(8,128)S(1)} %get-tuple-element.35), channel_id=1, source_target_pairs={{0,8},{4,12},{8,0},{12,4},{1,9},{5,13},{9,1},{13,5},{2,10},{6,14},... | collective-permute-start | bytes 12296 | tf_op jit(solution)/shard_map/ppermute | solution.py:466
  21.4 7.2 %collective-permute-start.11 = (f32[136,128]{1,0:T(8,128)S(1)}, f32[136,128]{1,0:T(8,128)S(1)}, u32[]{:S(2)}, u32[]{:S(2)}) collective-permute-start(f32[136,128]{1,0:T(8,128)S(1)} %get-tuple-element.36.refs_4_), channel_id=1, source_target_pairs={{0,8},{4,12},{8,0},{12,4},{1,9},{5,13},{9,1},{13,5},{2,10},{6,14},... | collective-permute-start | bytes 208904 | tf_op jit(solution)/shard_map/ppermute | solution.py:466
  25.9 3.7 %collective-permute-start.10 = (f32[8,128]{1,0:T(8,128)S(1)}, f32[8,128]{1,0:T(8,128)S(1)}, u32[]{:S(2)}, u32[]{:S(2)}) collective-permute-start(f32[8,128]{1,0:T(8,128)S(1)} %fusion.refs_0_), channel_id=1, source_target_pairs={{0,2},{1,3},{2,0},{3,1},{4,6},{5,7},{6,4},{7,5},{8,10},{9,11},{10,... | collective-permute-start | bytes 12296 | tf_op jit(solution)/shard_map/ppermute | solution.py:466
  27.5 3.0 %collective-permute-start.9 = (f32[8,128]{1,0:T(8,128)S(1)}, f32[8,128]{1,0:T(8,128)S(1)}, u32[]{:S(2)}, u32[]{:S(2)}) collective-permute-start(f32[8,128]{1,0:T(8,128)S(1)} %fusion.refs_0_), channel_id=1, source_target_pairs={{0,3},{1,2},{2,1},{3,0},{4,7},{5,6},{6,5},{7,4},{8,11},{9,10},{10,... | collective-permute-start | bytes 12296 | tf_op jit(solution)/shard_map/ppermute | solution.py:466
  27.5 3.0 %collective-permute-start.8 = (f32[8,128]{1,0:T(8,128)S(1)}, f32[8,128]{1,0:T(8,128)S(1)}, u32[]{:S(2)}, u32[]{:S(2)}) collective-permute-start(f32[8,128]{1,0:T(8,128)S(1)} %fusion.refs_0_), channel_id=1, source_target_pairs={{0,1},{1,0},{2,3},{3,2},{4,5},{5,4},{6,7},{7,6},{8,9},{9,8},{10,11... | collective-permute-start | bytes 12296 | tf_op jit(solution)/shard_map/ppermute | solution.py:466

commit v7 on v6

--- a/solution.py
+++ b/solution.py
@@ -388,23 +388,22 @@
             column < HALO, first, jnp.where(column >= LANES - HALO, last, middle_part)
         )
 
+    bs = (source, weight)
+    zs = [smooth(b) for b in bs]
+    qs = [diagonal * z - couple(z) for z in zs]
+    us = [smooth(q) for q in qs]
+    flows = [diagonal * u - 2.0 * (cx * below(u) + cy * right(u) + via * upper(u)) for u in us]
     found = []
-    for which, b in enumerate((source, weight)):
-        z = smooth(b)
-        q = diagonal * z - couple(z)
-        u = smooth(q)
-        flow = diagonal * u - 2.0 * (cx * below(u) + cy * right(u) + via * upper(u))
+    for b, z, q, u, flow in zip(bs, zs, qs, us, flows):
         for one, two in ((b, z), (z, q), (q, u), (u, flow)):
             term = jnp.where(near, one[0:rows] * two[0:rows], 0.0)
             found.append(jnp.sum(term, axis=0, keepdims=True))
-        if which == 0:
-            for p in range(layers):
-                if p < zed.shape[0]:
-                    zed[p] = whole(zed_in[p], z, p)
-                you[p] = whole(you_in[p], u, p)
-        else:
-            message[0:rows, :] = whole(front[0], z, 0)
-            message[rows : 2 * rows, :] = whole(front[1], u, 0)
+    for p in range(layers):
+        if p < zed.shape[0]:
+            zed[p] = whole(zed_in[p], zs[0], p)
+        you[p] = whole(you_in[p], us[0], p)
+    message[0:rows, :] = whole(front[0], zs[1], 0)
+    message[rows : 2 * rows, :] = whole(front[1], us[1], 0)
     found = sums[...] + jnp.concatenate(found, axis=0)
     scalars[...] = found
     message[2 * rows :, :] = found

time: 31.6 us -> 31.5 us (level)
  no operation moved by 1% of the time
where the time goes in v7:
time: 31.5 us; the launch traced here: 31.3 us
  starting transfers between devices  16.5 us (52%)
  waiting for transfers between devices  7.89 us (25%)
  Pallas kernels  5.52 us (18%)
  between operations  1.35 us (4%)
    ppermute x12, starting transfers between devices, exchange(): lax.ppermute(value, axis, list(enumerate(target)))  16.5 us
    ppermute x12, waiting for transfers between devices, exchange(): lax.ppermute(value, axis, list(enumerate(target)))  7.89 us
    pallas_call x7, Pallas kernels, call(): pl.pallas_call(kernel, out_shape=tuple(outs), in_specs=specs or [vmem() f...  5.52 us
  transfers between devices with their start and end apart: 12, of which 6 were waited for; matrix products, arithmetic and copies ran while one was open for 0% of the time, Pallas kernels for 7%

profile of v7, /device:TPU:0, one launch (start us, length us, event | category | flops | bytes accessed | tf_op | source)
XLA Modules:
  0.0 31.3 jit_solution(5086602571199237809)
XLA Ops:
  1.3 1.4 %shard_map.95 = (f32[19,64,128]{2,1,0:T(8,128)S(1)}, f32[72,128]{1,0:T(8,128)S(1)}, s32[1,512]{1,0:T(1,128)S(1)}, f32[152,128]{1,0:T(8,128)S(1)}, f32[152,128]{1,0:T(8,128)S(1)}, /*index=5*/f32[72,128]{1,0:T(8,128)S(1)}) custom-call(f32[4,64,128]{2,1,0:T(8,128)} %refs_0_.1, f32[4,64,128]{2,1,0:T(8,128)} %refs_1_.1, f32[3,64,128]{2,1,0:T(8,128)} %refs_2_.1, ...), custom_call_target="tpu_custom_call" | custom-call | bytes 1740804 | tf_op jit(solution)/shard_map/pallas_call | solution.py:451
  2.7 5.1 %collective-permute-start = (f32[152,128]{1,0:T(8,128)S(1)}, f32[152,128]{1,0:T(8,128)S(1)}, u32[]{:S(2)}, u32[]{:S(2)}) collective-permute-start(f32[152,128]{1,0:T(8,128)S(1)} %get-tuple-element.23), channel_id=1, source_target_pairs={{0,12},{4,8},{8,4},{12,0},{1,13},{5,9},{9,5},{13,1},{2,14},{6,10},... | collective-permute-start | bytes 233480 | tf_op jit(solution)/shard_map/ppermute | solution.py:465
  7.8 0.0 collective-permute-start.1
  7.8 0.6 %collective-permute-start.2 = (f32[72,128]{1,0:T(8,128)S(1)}, f32[72,128]{1,0:T(8,128)S(1)}, u32[]{:S(2)}, u32[]{:S(2)}) collective-permute-start(f32[72,128]{1,0:T(8,128)S(1)} %get-tuple-element.25), channel_id=1, source_target_pairs={{0,8},{4,12},{8,0},{12,4},{1,9},{5,13},{9,1},{13,5},{2,10},{6,14},... | collective-permute-start | bytes 110600 | tf_op jit(solution)/shard_map/ppermute | solution.py:465
  8.4 4.5 %collective-permute-done.2.refs_4_ = f32[72,128]{1,0:T(8,128)S(1)} collective-permute-done((f32[72,128]{1,0:T(8,128)S(1)}, f32[72,128]{1,0:T(8,128)S(1)}, u32[]{:S(2)}, u32[]{:S(2)}) %collective-permute-start.2) | collective-permute-done | bytes 36896 | tf_op jit(solution)/shard_map/ppermute | solution.py:465
  12.9 0.0 collective-permute-done.refs_2_
  12.9 0.0 collective-permute-done.1.refs_3_
  12.9 0.3 shard_map.96
  13.2 0.1 collective-permute-start.3
  13.2 1.7 %collective-permute-start.4 = (f32[56,128]{1,0:T(8,128)S(1)}, f32[56,128]{1,0:T(8,128)S(1)}, u32[]{:S(2)}, u32[]{:S(2)}) collective-permute-start(f32[56,128]{1,0:T(8,128)S(1)} %get-tuple-element.30), channel_id=1, source_target_pairs={{0,3},{1,2},{2,1},{3,0},{4,7},{5,6},{6,5},{7,4},{8,11},{9,10},{10,... | collective-permute-start | bytes 86024 | tf_op jit(solution)/shard_map/ppermute | solution.py:465
  15.0 1.3 %shard_map.97 = (f32[2,64,128]{2,1,0:T(8,128)S(1)}, f32[2,64,128]{2,1,0:T(8,128)S(1)}, f32[4,64,128]{2,1,0:T(8,128)S(1)}, f32[8,128]{1,0:T(8,128)S(1)}, f32[6,72,128]{2,1,0:T(8,128)S(1)}) custom-call(f32[19,64,128]{2,1,0:T(8,128)S(1)} %get-tuple-element.21.refs_0_, f32[19,8,128]{2,1,0:T(8,128)S(1)} %get-tuple-element.26.refs_1_, ...), custom_call_target="tpu_custom_call" | custom-call | bytes 1224704 | tf_op jit(solution)/shard_map/pallas_call | solution.py:451
  16.3 0.0 collective-permute-done.3.refs_1_
  16.3 0.3 %collective-permute-done.4.refs_2_ = f32[56,128]{1,0:T(8,128)S(1)} collective-permute-done((f32[56,128]{1,0:T(8,128)S(1)}, f32[56,128]{1,0:T(8,128)S(1)}, u32[]{:S(2)}, u32[]{:S(2)}) %collective-permute-start.4) | collective-permute-done | bytes 28704 | tf_op jit(solution)/shard_map/ppermute | solution.py:465
  16.6 0.8 %shard_map.98 = (f32[136,128]{1,0:T(8,128)S(1)}, f32[2,64,128]{2,1,0:T(8,128)S(1)}, f32[4,64,128]{2,1,0:T(8,128)S(1)}, f32[8,128]{1,0:T(8,128)S(1)}) custom-call(f32[6,72,128]{2,1,0:T(8,128)S(1)} %get-tuple-element.28.refs_0_, f32[56,128]{1,0:T(8,128)S(1)} %collective-permute-done.3.refs_1_, f32[56,128]{1,0:T(8,128)S(1)} %collective-permute-done.4.refs_2_, ...), custom_call_target="tpu_custom_call" | custom-call | bytes 815104 | tf_op jit(solution)/shard_map/pallas_call | solution.py:451
  17.4 1.8 %collective-permute-start.7 = (f32[136,128]{1,0:T(8,128)S(1)}, f32[136,128]{1,0:T(8,128)S(1)}, u32[]{:S(2)}, u32[]{:S(2)}) collective-permute-start(f32[136,128]{1,0:T(8,128)S(1)} %get-tuple-element.36.refs_4_), channel_id=1, source_target_pairs={{0,4},{4,0},{8,12},{12,8},{1,5},{5,1},{9,13},{13,9},{2,6},{6,2},{1... | collective-permute-start | bytes 208904 | tf_op jit(solution)/shard_map/ppermute | solution.py:465
  19.2 2.0 %collective-permute-start.6 = (f32[136,128]{1,0:T(8,128)S(1)}, f32[136,128]{1,0:T(8,128)S(1)}, u32[]{:S(2)}, u32[]{:S(2)}) collective-permute-start(f32[136,128]{1,0:T(8,128)S(1)} %get-tuple-element.36.refs_4_), channel_id=1, source_target_pairs={{0,12},{4,8},{8,4},{12,0},{1,13},{5,9},{9,5},{13,1},{2,14},{6,10},... | collective-permute-start | bytes 208904 | tf_op jit(solution)/shard_map/ppermute | solution.py:465
  21.3 0.0 collective-permute-start.5
  21.3 2.9 %collective-permute-start.11 = (f32[136,128]{1,0:T(8,128)S(1)}, f32[136,128]{1,0:T(8,128)S(1)}, u32[]{:S(2)}, u32[]{:S(2)}) collective-permute-start(f32[136,128]{1,0:T(8,128)S(1)} %get-tuple-element.36.refs_4_), channel_id=1, source_target_pairs={{0,8},{4,12},{8,0},{12,4},{1,9},{5,13},{9,1},{13,5},{2,10},{6,14},... | collective-permute-start | bytes 208904 | tf_op jit(solution)/shard_map/ppermute | solution.py:465
  24.2 1.6 %collective-permute-done.5 = f32[8,128]{1,0:T(8,128)S(1)} collective-permute-done((f32[8,128]{1,0:T(8,128)S(1)}, f32[8,128]{1,0:T(8,128)S(1)}, u32[]{:S(2)}, u32[]{:S(2)}) %collective-permute-start.5) | collective-permute-done | bytes 4128 | tf_op jit(solution)/shard_map/ppermute | solution.py:465
  25.8 0.0 collective-permute-done.7.refs_2_
  25.8 0.0 collective-permute-done.6.refs_1_
  25.8 1.6 %collective-permute-start.10 = (f32[8,128]{1,0:T(8,128)S(1)}, f32[8,128]{1,0:T(8,128)S(1)}, u32[]{:S(2)}, u32[]{:S(2)}) collective-permute-start(f32[8,128]{1,0:T(8,128)S(1)} %fusion.refs_0_), channel_id=1, source_target_pairs={{0,2},{1,3},{2,0},{3,1},{4,6},{5,7},{6,4},{7,5},{8,10},{9,11},{10,... | collective-permute-start | bytes 12296 | tf_op jit(solution)/shard_map/ppermute | solution.py:465
  27.4 0.0 collective-permute-start.9
  27.4 0.6 %collective-permute-start.8 = (f32[8,128]{1,0:T(8,128)S(1)}, f32[8,128]{1,0:T(8,128)S(1)}, u32[]{:S(2)}, u32[]{:S(2)}) collective-permute-start(f32[8,128]{1,0:T(8,128)S(1)} %fusion.refs_0_), channel_id=1, source_target_pairs={{0,1},{1,0},{2,3},{3,2},{4,5},{5,4},{6,7},{7,6},{8,9},{9,8},{10,11... | collective-permute-start | bytes 12296 | tf_op jit(solution)/shard_map/ppermute | solution.py:465
  28.0 0.4 %shard_map.99.refs_0_ = bf16[512,256]{1,0:T(8,128)(2,1)S(1)} custom-call(s32[1,512]{1,0:T(1,128)S(1)} %get-tuple-element.39.home), custom_call_target="tpu_custom_call" | custom-call | bytes 264192 | tf_op jit(solution)/shard_map/pallas_call | solution.py:451
  28.4 0.1 collective-permute-done.11.refs_3_
  28.5 0.6 %shard_map.100.refs_6_ = f32[512,256]{1,0:T(8,128)S(1)} custom-call(bf16[512,256]{1,0:T(8,128)(2,1)S(1)} %shard_map.99.refs_0_, f32[136,128]{1,0:T(8,128)S(1)} %collective-permute-done.6.refs_1_, f32[136,128]{1,0:T(8,128)S(1)} %collective-permute-done.7.refs_2_, f32[136,128]{1,0:T(8,128)S(1)} %collective-permute-done.11.refs_3_, ...), custom_call_target="tpu_custom_call" | custom-call | bytes 1064960 | tf_op jit(solution)/shard_map/pallas_call | solution.py:451
  29.1 0.5 %collective-permute-done.10.refs_3_ = f32[8,128]{1,0:T(8,128)S(1)} collective-permute-done((f32[8,128]{1,0:T(8,128)S(1)}, f32[8,128]{1,0:T(8,128)S(1)}, u32[]{:S(2)}, u32[]{:S(2)}) %collective-permute-start.10) | collective-permute-done | bytes 4128 | tf_op jit(solution)/shard_map/ppermute | solution.py:465
  29.5 0.9 %collective-permute-done.9.refs_2_ = f32[8,128]{1,0:T(8,128)S(1)} collective-permute-done((f32[8,128]{1,0:T(8,128)S(1)}, f32[8,128]{1,0:T(8,128)S(1)}, u32[]{:S(2)}, u32[]{:S(2)}) %collective-permute-start.9) | collective-permute-done | bytes 4128 | tf_op jit(solution)/shard_map/ppermute | solution.py:465
  30.4 0.0 collective-permute-done.8.refs_1_
  30.4 0.9 %shard_map.101 = (f32[4,64,128]{2,1,0:T(8,128)}, f32[512,128]{1,0:T(8,128)}) custom-call(f32[8,128]{1,0:T(8,128)S(1)} %fusion.refs_0_, f32[8,128]{1,0:T(8,128)S(1)} %collective-permute-done.8.refs_1_, f32[8,128]{1,0:T(8,128)S(1)} %collective-permute-done.9.refs_2_, f32[8,128]{1,0:T(8,128)S(1)} %collective-permute-done.10.refs_3_, ...), custom_call_target="tpu_custom_call" | custom-call | bytes 1130496 | tf_op jit(solution)/shard_map/pallas_call | solution.py:451
  (1 shorter events, 0.0 us)
Async XLA Ops:
  2.7 10.2 %collective-permute-start = (f32[152,128]{1,0:T(8,128)S(1)}, f32[152,128]{1,0:T(8,128)S(1)}, u32[]{:S(2)}, u32[]{:S(2)}) collective-permute-start(f32[152,128]{1,0:T(8,128)S(1)} %get-tuple-element.23), channel_id=1, source_target_pairs={{0,12},{4,8},{8,4},{12,0},{1,13},{5,9},{9,5},{13,1},{2,14},{6,10},... | collective-permute-start | bytes 233480 | tf_op jit(solution)/shard_map/ppermute | solution.py:465
  7.8 5.1 %collective-permute-start.1 = (f32[152,128]{1,0:T(8,128)S(1)}, f32[152,128]{1,0:T(8,128)S(1)}, u32[]{:S(2)}, u32[]{:S(2)}) collective-permute-start(f32[152,128]{1,0:T(8,128)S(1)} %get-tuple-element.24), channel_id=1, source_target_pairs={{0,4},{4,0},{8,12},{12,8},{1,5},{5,1},{9,13},{13,9},{2,6},{6,2},{1... | collective-permute-start | bytes 233480 | tf_op jit(solution)/shard_map/ppermute | solution.py:465
  7.8 5.1 %collective-permute-start.2 = (f32[72,128]{1,0:T(8,128)S(1)}, f32[72,128]{1,0:T(8,128)S(1)}, u32[]{:S(2)}, u32[]{:S(2)}) collective-permute-start(f32[72,128]{1,0:T(8,128)S(1)} %get-tuple-element.25), channel_id=1, source_target_pairs={{0,8},{4,12},{8,0},{12,4},{1,9},{5,13},{9,1},{13,5},{2,10},{6,14},... | collective-permute-start | bytes 110600 | tf_op jit(solution)/shard_map/ppermute | solution.py:465
  13.2 3.1 %collective-permute-start.3 = (f32[56,128]{1,0:T(8,128)S(1)}, f32[56,128]{1,0:T(8,128)S(1)}, u32[]{:S(2)}, u32[]{:S(2)}) collective-permute-start(f32[56,128]{1,0:T(8,128)S(1)} %get-tuple-element.29), channel_id=1, source_target_pairs={{0,1},{1,0},{2,3},{3,2},{4,5},{5,4},{6,7},{7,6},{8,9},{9,8},{10,11... | collective-permute-start | bytes 86024 | tf_op jit(solution)/shard_map/ppermute | solution.py:465
  13.2 3.4 %collective-permute-start.4 = (f32[56,128]{1,0:T(8,128)S(1)}, f32[56,128]{1,0:T(8,128)S(1)}, u32[]{:S(2)}, u32[]{:S(2)}) collective-permute-start(f32[56,128]{1,0:T(8,128)S(1)} %get-tuple-element.30), channel_id=1, source_target_pairs={{0,3},{1,2},{2,1},{3,0},{4,7},{5,6},{6,5},{7,4},{8,11},{9,10},{10,... | collective-permute-start | bytes 86024 | tf_op jit(solution)/shard_map/ppermute | solution.py:465
  17.4 8.4 %collective-permute-start.7 = (f32[136,128]{1,0:T(8,128)S(1)}, f32[136,128]{1,0:T(8,128)S(1)}, u32[]{:S(2)}, u32[]{:S(2)}) collective-permute-start(f32[136,128]{1,0:T(8,128)S(1)} %get-tuple-element.36.refs_4_), channel_id=1, source_target_pairs={{0,4},{4,0},{8,12},{12,8},{1,5},{5,1},{9,13},{13,9},{2,6},{6,2},{1... | collective-permute-start | bytes 208904 | tf_op jit(solution)/shard_map/ppermute | solution.py:465
  19.2 6.6 %collective-permute-start.6 = (f32[136,128]{1,0:T(8,128)S(1)}, f32[136,128]{1,0:T(8,128)S(1)}, u32[]{:S(2)}, u32[]{:S(2)}) collective-permute-start(f32[136,128]{1,0:T(8,128)S(1)} %get-tuple-element.36.refs_4_), channel_id=1, source_target_pairs={{0,12},{4,8},{8,4},{12,0},{1,13},{5,9},{9,5},{13,1},{2,14},{6,10},... | collective-permute-start | bytes 208904 | tf_op jit(solution)/shard_map/ppermute | solution.py:465
  21.3 4.5 %collective-permute-start.5 = (f32[8,128]{1,0:T(8,128)S(1)}, f32[8,128]{1,0:T(8,128)S(1)}, u32[]{:S(2)}, u32[]{:S(2)}) collective-permute-start(f32[8,128]{1,0:T(8,128)S(1)} %get-tuple-element.35), channel_id=1, source_target_pairs={{0,8},{4,12},{8,0},{12,4},{1,9},{5,13},{9,1},{13,5},{2,10},{6,14},... | collective-permute-start | bytes 12296 | tf_op jit(solution)/shard_map/ppermute | solution.py:465
  21.3 7.2 %collective-permute-start.11 = (f32[136,128]{1,0:T(8,128)S(1)}, f32[136,128]{1,0:T(8,128)S(1)}, u32[]{:S(2)}, u32[]{:S(2)}) collective-permute-start(f32[136,128]{1,0:T(8,128)S(1)} %get-tuple-element.36.refs_4_), channel_id=1, source_target_pairs={{0,8},{4,12},{8,0},{12,4},{1,9},{5,13},{9,1},{13,5},{2,10},{6,14},... | collective-permute-start | bytes 208904 | tf_op jit(solution)/shard_map/ppermute | solution.py:465
  25.8 3.7 %collective-permute-start.10 = (f32[8,128]{1,0:T(8,128)S(1)}, f32[8,128]{1,0:T(8,128)S(1)}, u32[]{:S(2)}, u32[]{:S(2)}) collective-permute-start(f32[8,128]{1,0:T(8,128)S(1)} %fusion.refs_0_), channel_id=1, source_target_pairs={{0,2},{1,3},{2,0},{3,1},{4,6},{5,7},{6,4},{7,5},{8,10},{9,11},{10,... | collective-permute-start | bytes 12296 | tf_op jit(solution)/shard_map/ppermute | solution.py:465
  27.4 3.0 %collective-permute-start.9 = (f32[8,128]{1,0:T(8,128)S(1)}, f32[8,128]{1,0:T(8,128)S(1)}, u32[]{:S(2)}, u32[]{:S(2)}) collective-permute-start(f32[8,128]{1,0:T(8,128)S(1)} %fusion.refs_0_), channel_id=1, source_target_pairs={{0,3},{1,2},{2,1},{3,0},{4,7},{5,6},{6,5},{7,4},{8,11},{9,10},{10,... | collective-permute-start | bytes 12296 | tf_op jit(solution)/shard_map/ppermute | solution.py:465
  27.4 3.0 %collective-permute-start.8 = (f32[8,128]{1,0:T(8,128)S(1)}, f32[8,128]{1,0:T(8,128)S(1)}, u32[]{:S(2)}, u32[]{:S(2)}) collective-permute-start(f32[8,128]{1,0:T(8,128)S(1)} %fusion.refs_0_), channel_id=1, source_target_pairs={{0,1},{1,0},{2,3},{3,2},{4,5},{5,4},{6,7},{7,6},{8,9},{9,8},{10,11... | collective-permute-start | bytes 12296 | tf_op jit(solution)/shard_map/ppermute | solution.py:465
